TPU v7x, 32 devices: a whole 2x2x4 slice. The times are simulated.
32 devices in a mesh: hidden: 4 (over z), width: 2 (over x), replica: 4 (over y, core).
Axes of the slice: x: 2, y: 2, z: 4, core: 2. Of those that a mesh axis runs over, the one named last changes fastest.
Arguments:
- saved_input: bfloat16 [1024, 12288], P(('replica', 'hidden'), 'width'), may hold values from -0.19921875 to 0.19921875
- grad_out: bfloat16 [1024, 24576], P(('replica', 'width'), 'hidden'), may hold values from -6 to 6
- weight: bfloat16 [12288, 24576], P('width', 'hidden'), may hold values from -0.0546875 to 0.0546875
- samples: int32 [64], replicated, may hold values from 8 to 16
- correct: int32 [64], replicated, may hold values from 0 to 8
- prompt_ids: int32 [1024], P('replica'), may hold values from 0 to 63
Outputs:
- grad_input: bfloat16 [1024, 12288], P(('replica', 'hidden'), 'width')
- grad_weight: float32 [12288, 24576], P(('width', 'replica'), 'hidden')
Inputs may be any that keep to these rules, and one draw needn't show every extreme that they name: correct[i] <= samples[i] for every prompt.
All inputs are finite; a program needn't handle non-finite values.
Results may differ from a plain program's by a relative error of at most 0.012.
Values may be sent and summed in bfloat16 or wider, within the bound.
No kernel may reach another device: no remote copies, remote signals or barrier semaphores. Data moves between devices by JAX's collectives and lax.ppermute only.
A program may use at most 320 MiB of HBM per device.

v0:
```python
import jax
import jax.numpy as jnp
from jax import lax
from jax.sharding import PartitionSpec as P

K = 4


def pass_weights(samples, correct):
    total = samples.astype(jnp.float32)
    good = correct.astype(jnp.float32)
    missing = jnp.ones_like(total)
    for factor_index in range(K):
        missing = missing * jnp.maximum(total - good - factor_index, 0.0) / (total - factor_index)
    return 1.0 - missing


def token_weights(prompt_ids, samples, correct):
    pass_at_k = pass_weights(samples, correct)
    prompt_range = jnp.arange(samples.shape[0], dtype=jnp.int32)
    matches = prompt_ids[:, None] == prompt_range[None, :]
    picked = jnp.sum(jnp.where(matches, pass_at_k[None, :], 0.0), axis=1)
    rounded = lax.optimization_barrier(picked.astype(jnp.bfloat16))
    return rounded.astype(jnp.float32)


def body(saved_input, grad_out, weight, samples, correct, prompt_ids):
    weights_all = token_weights(prompt_ids, samples, correct)
    gathered_x = lax.all_gather(saved_input, "hidden", axis=0, tiled=True)
    gathered_g = lax.all_gather(grad_out, "width", axis=0, tiled=True)
    scaled = (gathered_g.astype(jnp.float32) * weights_all[:, None]).astype(jnp.bfloat16)
    picked = scaled
    grad_input = lax.psum_scatter(
        lax.dot_general(
            picked, weight, (((1,), (1,)), ((), ())), preferred_element_type=jnp.float32
        ),
        "hidden",
        scatter_dimension=0,
        tiled=True,
    )
    picked = gathered_x
    grad_weight = lax.psum_scatter(
        lax.dot_general(
            picked, scaled, (((0,), (0,)), ((), ())), preferred_element_type=jnp.float32
        ).astype(jnp.bfloat16),
        "replica",
        scatter_dimension=0,
        tiled=True,
    ).astype(jnp.float32)
    return (grad_input.astype(jnp.bfloat16), grad_weight)


def solution(mesh):
    in_specs = (
        P(("replica", "hidden"), "width"),
        P(("replica", "width"), "hidden"),
        P("width", "hidden"),
        P(),
        P(),
        P("replica"),
    )
    out_specs = (P(("replica", "hidden"), "width"), P(("width", "replica"), "hidden"))
    return jax.shard_map(body, mesh=mesh, in_specs=in_specs, out_specs=out_specs, check_vma=False)
```

profile of v0, /device:TPU:0, one launch (start us, length us, event | category | flops | bytes accessed | tf_op | source)
XLA Modules:
  0.0 775.9 jit_solution(17203025529690645143)
XLA Ops:
  7.2 0.0 all-gather.3.cloned.1.call-start
  7.2 0.7 all-gather.3.cloned.1.call-update
  7.9 0.0 all-gather.5.cloned.1.call-start
  7.9 0.7 all-gather.5.cloned.1.call-update
  8.6 0.0 reduce-scatter.3.cloned.1.call-start
  8.7 0.7 fusion.1
  9.4 0.8 select_reduce_fusion
  10.2 47.0 %all-gather.3.cloned.1.call-done = bf16[256,6144]{1,0:T(8,128)(2,1)} async-done(((bf16[128,6144]{1,0:T(8,128)(2,1)}), bf16[256,6144]{1,0:T(8,128)(2,1)}) %all-gather.3.cloned.1.call-update) | async-done | bytes 3145744 | tf_op jit(solution)/shard_map/all_gather | solution.py:30
  57.2 31.8 %fusion = f32[256,6144]{1,0:T(8,128)} fusion(bf16[6144,6144]{1,0:T(8,128)(2,1)} %param.8, bf16[256,6144]{1,0:T(8,128)(2,1)} %all-gather.3.cloned.1.call-done, f32[256]{0:T(256)S(1)} %convert_element_type.34), kind=kOutput, calls=%fused_computation.2 | convolution fusion | flops 19332071424 | bytes 84935680 | tf_op jit(solution)/shard_map/dot_general | solution.py:34
  89.0 0.0 copy-start
  89.0 0.0 reduce-scatter.3.cloned.1.call-update
  89.1 0.0 reduce-scatter.5.cloned.1.call-start
  89.1 33.2 %all-gather.5.cloned.1.call-done = bf16[256,6144]{1,0:T(8,128)(2,1)} async-done(((bf16[64,6144]{1,0:T(8,128)(2,1)}), bf16[256,6144]{1,0:T(8,128)(2,1)}) %all-gather.5.cloned.1.call-update) | async-done | bytes 3145744 | tf_op jit(solution)/shard_map/all_gather | solution.py:29
  122.3 0.0 copy-done
  122.3 30.7 %convert_bitcast_fusion = bf16[6144,6144]{0,1:T(8,128)(2,1)} fusion(bf16[256,6144]{1,0:T(8,128)(2,1)} %all-gather.5.cloned.1.call-done, bf16[256,6144]{1,0:T(8,128)(2,1)S(1)} %copy-done, f32[256]{0:T(256)S(1)} %convert_element_type.34), kind=kOutput, calls=%fused_computation | convolution fusion | flops 19369820160 | bytes 81789952 | tf_op jit(solution)/shard_map/dot_general | solution.py:43
  153.1 0.0 reduce-scatter.5.cloned.1.call-update
  153.1 81.6 %reduce-scatter.3.cloned.1.call-done = f32[64,6144]{1,0:T(8,128)} async-done(((f32[256,6144]{1,0:T(8,128)}), f32[64,6144]{1,0:T(8,128)}) %reduce-scatter.3.cloned.1.call-update) | async-done | bytes 1572880 | tf_op jit(solution)/shard_map/reduce_scatter | solution.py:33
  234.6 2.4 convert_element_type.36
  237.0 506.2 %reduce-scatter.5.cloned.1.call-done = bf16[1536,6144]{0,1:T(8,128)(2,1)} async-done(((bf16[6144,6144]{0,1:T(8,128)(2,1)}), bf16[1536,6144]{0,1:T(8,128)(2,1)}) %reduce-scatter.5.cloned.1.call-update) | async-done | bytes 18874384 | tf_op jit(solution)/shard_map/reduce_scatter | solution.py:42
  743.2 26.2 %copy.9 = f32[1536,6144]{1,0:T(8,128)} copy(bf16[1536,6144]{0,1:T(8,128)(2,1)} %reduce-scatter.5.cloned.1.call-done) | data formatting | bytes 56623104
  (1 shorter events, 0.0 us)
Async XLA Ops:
  7.2 50.0 %all-gather.3.cloned.1.call-start = ((), (), s32[]{:S(2)}) async-start(), calls=%async_computation.2 | async-start | bytes 4718592 | tf_op jit(solution)/shard_map/all_gather | solution.py:30
  7.9 114.4 %all-gather.5.cloned.1.call-start = ((), (), s32[]{:S(2)}) async-start(), calls=%async_computation.4 | async-start | bytes 3932160 | tf_op jit(solution)/shard_map/all_gather | solution.py:29
  8.6 226.0 %reduce-scatter.3.cloned.1.call-start = ((), (), s32[]{:S(2)}) async-start(), calls=%async_computation.3 | async-start | bytes 7864320 | tf_op jit(solution)/shard_map/reduce_scatter | solution.py:33
  89.0 33.3 %copy-start = (bf16[256,6144]{1,0:T(8,128)(2,1)S(1)}, bf16[256,6144]{1,0:T(8,128)(2,1)}, u32[]{:S(2)}) copy-start(bf16[256,6144]{1,0:T(8,128)(2,1)} %all-gather.3.cloned.1.call-done) | copy-start | bytes 9437188
  89.1 654.1 %reduce-scatter.5.cloned.1.call-start = ((), (), s32[]{:S(2)}) async-start(), calls=%async_computation.5 | async-start | bytes 94371840 | tf_op jit(solution)/shard_map/reduce_scatter | solution.py:42
Sparse Core Ops, SparseCore 0:
  9.5 47.6 all-gather.2
  58.8 63.5 all-gather.4
  125.2 109.3 reduce-scatter.2
  237.1 506.0 reduce-scatter.4
where the time goes:
time: 777 us; the launch traced here: 776 us
  waiting for transfers between devices  669 us (86%)
  matrix products  62.6 us (8%)
  local copies, waits for them, and re-layouts  26.2 us (3%)
  between operations  13.8 us (2%)
    reduce_scatter x1, waiting for transfers between devices, body(): lax.psum_scatter(lax.dot_general(picked, scaled, (((0,), (0,)), ((), ()))...  506 us
    reduce_scatter x1, waiting for transfers between devices, body(): lax.psum_scatter(lax.dot_general(picked, weight, (((1,), (1,)), ((), ()))...  81.6 us
    all_gather x1, waiting for transfers between devices, body(): gathered_g = lax.all_gather(grad_out, 'width', axis=0, tiled=True)  47 us
    all_gather x1, waiting for transfers between devices, body(): gathered_x = lax.all_gather(saved_input, 'hidden', axis=0, tiled=True)  33.2 us
    dot_general x1, matrix products, body(): lax.dot_general(picked, weight, (((1,), (1,)), ((), ())), preferred_eleme...  31.8 us
    dot_general x1, matrix products, body(): lax.dot_general(picked, scaled, (((0,), (0,)), ((), ())), preferred_eleme...  30.7 us
    unnamed x3, local copies, waits for them, and re-layouts  26.2 us
  transfers between devices with their start and end apart: 4, of which 4 were waited for; matrix products, arithmetic and copies ran while one was open for 9% of the time, Pallas kernels for 0%

commit v1 on v0

v1 whole, which is shorter than its diff:
```python
import functools

import jax
import jax.numpy as jnp
from jax import lax
from jax.experimental import pallas as pl
from jax.experimental.pallas import tpu as pltpu
from jax.sharding import PartitionSpec as P

K = 4


def pass_weights(samples, correct):
    total = samples.astype(jnp.float32)
    good = correct.astype(jnp.float32)
    missing = jnp.ones_like(total)
    for factor_index in range(K):
        missing = missing * jnp.maximum(total - good - factor_index, 0.0) / (total - factor_index)
    return 1.0 - missing


def token_weights(prompt_ids, samples, correct):
    pass_at_k = pass_weights(samples, correct)
    prompt_range = jnp.arange(samples.shape[0], dtype=jnp.int32)
    matches = prompt_ids[:, None] == prompt_range[None, :]
    picked = jnp.sum(jnp.where(matches, pass_at_k[None, :], 0.0), axis=1, keepdims=True)
    rounded = lax.optimization_barrier(picked.astype(jnp.bfloat16))
    return rounded.astype(jnp.float32)


def after(value, *others):
    return lax.optimization_barrier((value,) + others)[0]


def weight_grad_kernel(place_ref, *refs, n_x, n_s, n_h):
    x_refs, s_refs, out_ref, x_all, s_all = refs[:n_x], refs[n_x:n_x + n_s], refs[-3], refs[-2], refs[-1]
    rows = s_refs[0].shape[0]
    groups = x_refs[0].shape[0] // rows

    @pl.when(pl.program_id(0) == 0)
    def _():
        for k in range(n_x):
            @pl.when(place_ref[k] >= 0)
            def _(k=k):
                for g in range(groups):
                    start = pl.multiple_of((g * n_h + place_ref[k]) * rows, rows)
                    x_all[pl.ds(start, rows), :] = x_refs[k][g * rows:(g + 1) * rows, :]

    for k in range(n_s):
        s_all[k * rows:(k + 1) * rows, :] = s_refs[k][...]
    out_ref[...] = lax.dot_general(
        x_all[...], s_all[...], (((0,), (0,)), ((), ())), preferred_element_type=jnp.float32
    )


def weight_grad(places, x_pieces, s_pieces, n_h):
    x_rows, m = x_pieces[0].shape
    rows, f = s_pieces[0].shape
    tokens = rows * len(s_pieces)
    block = 512 if f % 512 == 0 else f
    body = functools.partial(weight_grad_kernel, n_x=len(x_pieces), n_s=len(s_pieces), n_h=n_h)
    return pl.pallas_call(
        body,
        grid_spec=pltpu.PrefetchScalarGridSpec(
            num_scalar_prefetch=1,
            grid=(f // block,),
            in_specs=[pl.BlockSpec((x_rows, m), lambda j, p: (0, 0))] * len(x_pieces)
            + [pl.BlockSpec((rows, block), lambda j, p: (0, j))] * len(s_pieces),
            out_specs=pl.BlockSpec((m, block), lambda j, p: (0, j)),
            scratch_shapes=[pltpu.VMEM((tokens, m), jnp.bfloat16), pltpu.VMEM((tokens, block), jnp.bfloat16)],
        ),
        out_shape=jax.ShapeDtypeStruct((m, f), jnp.float32),
        compiler_params=pltpu.CompilerParams(vmem_limit_bytes=56 << 20),
        cost_estimate=pl.CostEstimate(
            flops=2 * m * f * tokens, bytes_accessed=2 * tokens * (m + f) + 4 * m * f, transcendentals=0
        ),
    )(places, *x_pieces, *s_pieces)


def make_body(n_h, n_w, n_r):
    n_c = 2 if n_r % 2 == 0 else 1
    n_y = n_r // n_c
    per_w = n_h // n_w

    def slot(w_index, group):
        return group if w_index < n_w // 2 else per_w - 1 - group

    def slot_of(w_index, group):
        return jnp.where(w_index < n_w // 2, group, per_w - 1 - group)

    def replica_perm(dy, dc):
        return [
            (y * n_c + c, (y + dy) % n_y * n_c + (c + dc) % n_c) for y in range(n_y) for c in range(n_c)
        ]

    def over_replica(value, dy, dc):
        return lax.ppermute(value, "replica", replica_perm(dy, dc))

    def over_width(value, dx):
        return lax.ppermute(value, "width", [(w, (w + dx) % n_w) for w in range(n_w)])

    def body(saved_input, grad_out, weight, samples, correct, prompt_ids):
        h, w, r = lax.axis_index("hidden"), lax.axis_index("width"), lax.axis_index("replica")
        y, c = r // n_c, r % n_c
        x_rows, d_half = saved_input.shape
        s_rows, f = grad_out.shape
        rows = s_rows // per_w
        d_core = d_half // n_c
        d_own = d_half // n_r

        parts = []
        for dy in range(n_y):
            for dc in range(n_c):
                target = (y + dy) % n_y * n_c + (c + dc) % n_c
                part = lax.dynamic_slice_in_dim(saved_input, target * d_own, d_own, 1)
                parts.append(part if dy == dc == 0 else over_replica(part, dy, dc))
        x_own = jnp.concatenate(parts, axis=0)

        all_weights = token_weights(prompt_ids, samples, correct)
        s = {}
        for q in range(per_w):
            start = slot_of(w, q) * rows
            g = lax.dynamic_slice_in_dim(grad_out, start, rows, 0).astype(jnp.float32)
            scale = lax.dynamic_slice_in_dim(all_weights, w * s_rows + start, rows, 0)
            s[0, 0, 0, q] = (g * scale).astype(jnp.bfloat16)

        def spread_cores(dy, dx, q):
            for dc in range(1, n_c):
                s[dy, dc, dx, q] = over_replica(s[dy, 0, dx, q], 0, dc)

        for q in range(per_w):
            spread_cores(0, 0, q)
        last = ()
        for q in range(per_w):
            own = after(s[0, 0, 0, q], *last) if last else s[0, 0, 0, q]
            last = ()
            for dx in range(1, n_w):
                s[0, 0, dx, q] = over_width(own, dx)
                last += (s[0, 0, dx, q],)
            for dy in range(1, n_y):
                s[dy, 0, 0, q] = over_replica(own, dy, 0)
            for dx in range(1, n_w):
                spread_cores(0, dx, q)
            for dy in range(1, n_y):
                spread_cores(dy, 0, q)
        for dy in range(1, n_y):
            for dx in range(1, n_w):
                for q in range(per_w):
                    if q % 2 == 0:
                        s[dy, 0, dx, q] = over_width(after(s[dy, 0, 0, q], *last), dx)
                    else:
                        s[dy, 0, dx, q] = over_replica(s[0, 0, dx, q], dy, 0)
                    spread_cores(dy, dx, q)

        right, left = [x_own], [x_own]
        for k in range(1, n_h):
            right.append(lax.ppermute(right[-1], "hidden", [(j, j + 1) for j in range(k - 1, n_h - 1)]))
            left.append(lax.ppermute(left[-1], "hidden", [(j, j - 1) for j in range(1, n_h - k + 1)]))

        own_weight = lax.dynamic_slice_in_dim(weight, c * d_core, d_core, 0)
        shares = []
        for q in range(per_w):
            tokens = jnp.concatenate([s[0, dc, dx, q] for dc in range(n_c) for dx in range(n_w)], axis=0)
            share = lax.dot_general(
                tokens, own_weight, (((1,), (1,)), ((), ())), preferred_element_type=jnp.float32
            )
            shares.append(share.reshape(n_c, n_w, rows, d_core))

        def share_of(target, choices):
            target = jnp.clip(target, 0, n_h - 1)
            owner, group = target // per_w, target % per_w
            dx, q = (w - owner) % n_w, slot_of(owner, group)
            picked = None
            for choice in choices:
                value = lax.dynamic_index_in_dim(shares[choice], dx, 1, keepdims=False)
                picked = value if picked is None else jnp.where(q == choice, value, picked)
            return picked

        def passes(targets):
            return sorted({slot(t // per_w, t % per_w) for t in targets})

        from_left = from_right = None
        for step in range(1, n_h):
            apart = n_h - step
            choices = passes([j + apart for j in range(step)] + [j - apart for j in range(apart, n_h)])
            to_right, to_left = share_of(h + apart, choices), share_of(h - apart, choices)
            if step > 1:
                to_right = to_right + from_left.astype(jnp.float32)
                to_left = to_left + from_right.astype(jnp.float32)
            from_left = lax.ppermute(
                to_right.astype(jnp.bfloat16), "hidden", [(j, j + 1) for j in range(step)]
            )
            from_right = lax.ppermute(
                to_left.astype(jnp.bfloat16), "hidden", [(j, j - 1) for j in range(apart, n_h)]
            )
        total = share_of(h, range(per_w)) + from_left.astype(jnp.float32) + from_right.astype(jnp.float32)
        total = total.astype(jnp.bfloat16)
        held = [total[0]] + [over_replica(total[dc], 0, n_c - dc) for dc in range(1, n_c)]
        held = jnp.stack(held)
        grad_input = jnp.concatenate(
            [lax.dynamic_index_in_dim(held, (p - c) % n_c, 0, keepdims=False) for p in range(n_c)], axis=1
        )

        places, pieces = [], []
        for k in range(n_h):
            for plane, piece, there in (
                (h - k, right[k], h >= k),
                (h + k, left[k], (h + k < n_h) & (k > 0)),
            ):
                if k == 0 and piece is left[0] and len(pieces) == 1:
                    continue
                owner, group = plane // per_w, plane % per_w
                place = (w - owner) % n_w * per_w + slot_of(owner, group)
                places.append(jnp.where(there, place, -1).astype(jnp.int32))
                pieces.append(piece)
        s_pieces = [
            s[dy, dc, dx, q] for dy in range(n_y) for dc in range(n_c) for dx in range(n_w) for q in range(per_w)
        ]
        grad_weight = weight_grad(jnp.stack(places), pieces, s_pieces, n_h)
        return grad_input, grad_weight

    return body


def solution(mesh):
    in_specs = (
        P(("replica", "hidden"), "width"),
        P(("replica", "width"), "hidden"),
        P("width", "hidden"),
        P(),
        P(),
        P("replica"),
    )
    out_specs = (P(("replica", "hidden"), "width"), P(("width", "replica"), "hidden"))
    body = make_body(mesh.shape["hidden"], mesh.shape["width"], mesh.shape["replica"])
    return jax.shard_map(body, mesh=mesh, in_specs=in_specs, out_specs=out_specs, check_vma=False)
```

time: 777 us -> 203 us (0.26)
  waiting for transfers between devices: 669 us -> 63.1 us
  starting transfers between devices: 0.16 us -> 51.6 us
  Pallas kernels: 0 us -> 30 us
  matrix products: 62.6 us -> 35 us
  local copies, waits for them, and re-layouts: 26.2 us -> 4.2 us
  other arithmetic: 3.83 us -> 17.4 us
  between operations: 13.8 us -> 0.88 us
    reduce_scatter x2 -> x0, waiting for transfers between devices: 588 us -> none  [the longest x1 506 us: body(): lax.psum_scatter(lax.dot_general(picked, scaled, (((0,), (0,)), ((), ()))...]
    all_gather x2 -> x0, waiting for transfers between devices: 80.2 us -> none  [the longest x1 47 us: body(): gathered_g = lax.all_gather(grad_out, 'width', axis=0, tiled=True)]
    ppermute x0 -> x30, waiting for transfers between devices: none -> 63.1 us  [the longest x3 17.7 us: over_width(): lax.ppermute(value, 'width', [(w, (w + dx) % n_w) for w in range(n_w)])]
    ppermute x0 -> x30, starting transfers between devices: none -> 51.6 us  [the longest x3 21.5 us: body(): lax.ppermute(to_right.astype(jnp.bfloat16), 'hidden', [(j, j + 1) for j i...]
    pallas_call x0 -> x1, Pallas kernels: none -> 30 us  [weight_grad(): pl.pallas_call(body, grid_spec=pltpu.PrefetchScalarGridSpec(num_scalar_pr...]
    dot_general x2, matrix products: 62.6 us -> 35 us  [body(): lax.dot_general(tokens, own_weight, (((1,), (1,)), ((), ())), preferred_e...]
    unnamed x3 -> x14, local copies, waits for them, and re-layouts: 26.2 us -> 2 us
    convert_element_type x1 -> x4, other arithmetic: 2.36 us -> 13.7 us  [the longest x2 8.53 us: body(): to_right.astype(jnp.bfloat16)]
  transfers between devices with their start and end apart: 4 -> 30, of which waited for: 4 -> 8; matrix products, arithmetic and copies ran while one was open for 9% -> 24% of each run, Pallas kernels for 0% -> 15%
where the time goes in v1:
time: 203 us; the launch traced here: 202 us
  waiting for transfers between devices  63.1 us (31%)
  starting transfers between devices  51.6 us (25%)
  matrix products  35 us (17%)
  Pallas kernels  30 us (15%)
  other arithmetic  17.4 us (9%)
  local copies, waits for them, and re-layouts  4.2 us (2%)
    dot_general x2, matrix products, body(): lax.dot_general(tokens, own_weight, (((1,), (1,)), ((), ())), preferred_e...  35 us
    pallas_call x1, Pallas kernels, weight_grad(): pl.pallas_call(body, grid_spec=pltpu.PrefetchScalarGridSpec(num_scalar_pr...  30 us
    ppermute x3, starting transfers between devices, body(): lax.ppermute(to_right.astype(jnp.bfloat16), 'hidden', [(j, j + 1) for j i...  21.5 us
    ppermute x3, waiting for transfers between devices, over_width(): lax.ppermute(value, 'width', [(w, (w + dx) % n_w) for w in range(n_w)])  17.7 us
    ppermute x3, waiting for transfers between devices, body(): lax.ppermute(to_left.astype(jnp.bfloat16), 'hidden', [(j, j - 1) for j in...  12.7 us
    ppermute x3, waiting for transfers between devices, body(): lax.ppermute(to_right.astype(jnp.bfloat16), 'hidden', [(j, j + 1) for j i...  12.5 us
    ppermute x3, waiting for transfers between devices, body(): lax.ppermute(left[-1], 'hidden', [(j, j - 1) for j in range(1, n_h - k +...  12.3 us
    ppermute x15, starting transfers between devices, over_replica(): return lax.ppermute(value, 'replica', replica_perm(dy, dc))  9.76 us
  transfers between devices with their start and end apart: 30, of which 8 were waited for; matrix products, arithmetic and copies ran while one was open for 24% of the time, Pallas kernels for 15%

profile of v1, /device:TPU:0, one launch (start us, length us, event | category | flops | bytes accessed | tf_op | source)
XLA Modules:
  0.0 202.2 jit_solution(13359064374208419245)
XLA Ops:
  2.3 2.9 %multiply_convert_fusion.1 = (bf16[64,6144]{1,0:T(8,128)(2,1)}, bf16[64,6144]{1,0:T(8,128)(2,1)}) fusion(f32[64]{0:T(128)S(1)} %get-tuple-element.22, bf16[128,6144]{1,0:T(8,128)(2,1)} %param.7, s32[]{:T(128)S(6)} %select_n.371, f32[64]{0:T(128)S(1)} %get-tuple-element.23, s32[]{:T(128)S(6)} %select_n.375), kind=kLoop, calls=%fused_computation.40 | loop fusion | flops 2359296 | bytes 3146248 | tf_op jit(solution)/shard_map/convert_element_type | solution.py:125
  5.2 2.9 %collective-permute-start = (bf16[64,6144]{1,0:T(8,128)(2,1)}, bf16[64,6144]{1,0:T(8,128)(2,1)S(1)}, u32[]{:S(2)}, u32[]{:S(2)}) collective-permute-start(bf16[64,6144]{1,0:T(8,128)(2,1)} %get-tuple-element.13.refs_7_), channel_id=1, source_target_pairs={{0,4},{4,0},{1,5},{5,1},{2,6},{6,2},{3,7},{7,3},{8,12},{12,8},{9,1... | collective-permute-start | bytes 2359304 | tf_op jit(solution)/shard_map/ppermute | solution.py:100
  8.1 17.7 %collective-permute-done.refs_9_ = bf16[64,6144]{1,0:T(8,128)(2,1)S(1)} collective-permute-done((bf16[64,6144]{1,0:T(8,128)(2,1)}, bf16[64,6144]{1,0:T(8,128)(2,1)S(1)}, u32[]{:S(2)}, u32[]{:S(2)}) %collective-permute-start) | collective-permute-done | bytes 786464 | tf_op jit(solution)/shard_map/ppermute | solution.py:100
  25.9 1.7 collective-permute-start.1
  28.2 1.5 collective-permute-start.14
  30.2 1.3 collective-permute-start.15
  31.4 4.6 %collective-permute-done.14 = bf16[64,1536]{1,0:T(8,128)(2,1)S(1)} collective-permute-done((bf16[64,1536]{1,0:T(8,128)(2,1)S(1)}, bf16[64,1536]{1,0:T(8,128)(2,1)S(1)}, u32[]{:S(2)}, u32[]{:S(2)}) %collective-permute-start.14) | collective-permute-done | bytes 196640 | tf_op jit(solution)/shard_map/ppermute | solution.py:97
  36.0 1.5 collective-permute-start.22
  37.5 1.7 collective-permute-done.15
  41.4 4.4 %collective-permute-start.16 = (bf16[256,1536]{1,0:T(8,128)(2,1)}, bf16[256,1536]{1,0:T(8,128)(2,1)}, u32[]{:S(2)}, u32[]{:S(2)}) collective-permute-start(bf16[256,1536]{1,0:T(8,128)(2,1)} %pad_maximum_fusion.1.refs_0_), channel_id=1, source_target_pairs={{0,8},{8,16},{16,24},{1,9},{9,17},{17,25},{2,10},{10,18},{18,26},{... | collective-permute-start | bytes 2359304 | tf_op jit(solution)/shard_map/ppermute | solution.py:157
  45.7 1.3 collective-permute-start.17
  47.1 16.5 %fusion = f32[256,3072]{1,0:T(8,128)S(1)} fusion(bf16[6144,6144]{1,0:T(8,128)(2,1)} %param.8, s32[]{:T(128)S(6)} %select_n.378, bf16[64,6144]{1,0:T(8,128)(2,1)} %collective-permute-done.5.refs_13_, bf16[64,6144]{1,0:T(8,128)(2,1)} %collective-permute-done.4.refs_11_, bf16[64,6144]{1,0:T(8,128)(2,1)} %copy-done.1, bf16[64,6144]{1,0:T(8,128)(2,1)} %get-tuple-element.13.refs_7_), kind=kOutput, calls=%fused_computation | convolution fusion | flops 9676259328 | bytes 44040196 | tf_op jit(solution)/shard_map/dot_general | solution.py:164
  63.7 1.3 fusion.32
  65.0 5.4 %collective-permute-start.6 = (bf16[2,64,3072]{2,1,0:T(8,128)(2,1)}, bf16[2,64,3072]{2,1,0:T(8,128)(2,1)}, u32[]{:S(2)}, u32[]{:S(2)}) collective-permute-start(bf16[2,64,3072]{2,1,0:T(8,128)(2,1)} %get-tuple-element.10), channel_id=1, source_target_pairs={{0,8},{1,9},{2,10},{3,11},{4,12},{5,13},{6,14},{7,15}} | collective-permute-start | bytes 2359304 | tf_op jit(solution)/shard_map/ppermute | solution.py:190
  70.4 1.6 collective-permute-start.9
  72.0 18.5 %fusion.2 = f32[256,3072]{1,0:T(8,128)} fusion(bf16[6144,6144]{1,0:T(8,128)(2,1)} %param.8, s32[]{:T(128)S(6)} %select_n.378, bf16[64,6144]{1,0:T(8,128)(2,1)} %collective-permute-done.3.refs_14_, bf16[64,6144]{1,0:T(8,128)(2,1)} %collective-permute-done.2.refs_12_, bf16[64,6144]{1,0:T(8,128)(2,1)} %collective-permute-done.1.refs_10_, ...), kind=kOutput, calls=%fused_computation.2 | convolution fusion | flops 9676259328 | bytes 44040196 | tf_op jit(solution)/shard_map/dot_general | solution.py:164
  90.5 4.3 %fusion.23 = (bf16[2,64,3072]{2,1,0:T(8,128)(2,1)}, bf16[2,64,3072]{2,1,0:T(8,128)(2,1)}) fusion(bf16[2,64,3072]{2,1,0:T(8,128)(2,1)} %collective-permute-done.6, f32[2,2,64,3072]{3,2,1,0:T(8,128)S(1)} %bitcast.105, s32[]{:T(128)S(6)} %select_n.396, f32[2,2,64,3072]{3,2,1,0:T(8,128)} %bitcast.108, pred[]{:T(512)S(6)} %eq.71, ...), kind=kLoop, calls=%fused_computation.27 | loop fusion | flops 3145728 | bytes 9437194 | tf_op jit(solution)/shard_map/convert_element_type | solution.py:191
  94.8 1.6 collective-permute-start.10
  96.3 2.2 %collective-permute-start.7 = (bf16[2,64,3072]{2,1,0:T(8,128)(2,1)}, bf16[2,64,3072]{2,1,0:T(8,128)(2,1)}, u32[]{:S(2)}, u32[]{:S(2)}) collective-permute-start(bf16[2,64,3072]{2,1,0:T(8,128)(2,1)} %get-tuple-element.8), channel_id=1, source_target_pairs={{0,8},{8,16},{1,9},{9,17},{2,10},{10,18},{3,11},{11,19},{4,12},{12... | collective-permute-start | bytes 2359304 | tf_op jit(solution)/shard_map/ppermute | solution.py:190
  98.5 1.5 collective-permute-start.23
  100.1 1.6 collective-permute-start.18
  101.6 1.3 collective-permute-start.19
  102.9 12.5 %collective-permute-done.7 = bf16[2,64,3072]{2,1,0:T(8,128)(2,1)} collective-permute-done((bf16[2,64,3072]{2,1,0:T(8,128)(2,1)}, bf16[2,64,3072]{2,1,0:T(8,128)(2,1)}, u32[]{:S(2)}, u32[]{:S(2)}) %collective-permute-start.7) | collective-permute-done | bytes 786464 | tf_op jit(solution)/shard_map/ppermute | solution.py:190
  116.0 4.2 %fusion.26 = (bf16[2,64,3072]{2,1,0:T(8,128)(2,1)}, bf16[2,64,3072]{2,1,0:T(8,128)(2,1)}) fusion(bf16[2,64,3072]{2,1,0:T(8,128)(2,1)} %collective-permute-done.7, f32[2,2,64,3072]{3,2,1,0:T(8,128)S(1)} %bitcast.106, s32[]{:T(128)S(6)} %select_n.388, f32[2,2,64,3072]{3,2,1,0:T(8,128)} %bitcast.109, pred[]{:T(512)S(6)} %eq.70, ...), kind=kLoop, calls=%fused_computation.31 | loop fusion | flops 3145728 | bytes 9437194 | tf_op jit(solution)/shard_map/convert_element_type | solution.py:191
  120.2 1.5 collective-permute-start.25
  121.8 1.3 collective-permute-start.11
  123.1 13.9 %collective-permute-start.8 = (bf16[2,64,3072]{2,1,0:T(8,128)(2,1)}, bf16[2,64,3072]{2,1,0:T(8,128)(2,1)}, u32[]{:S(2)}, u32[]{:S(2)}) collective-permute-start(bf16[2,64,3072]{2,1,0:T(8,128)(2,1)} %get-tuple-element.6), channel_id=1, source_target_pairs={{0,8},{8,16},{16,24},{1,9},{9,17},{17,25},{2,10},{10,18},{18,26},{... | collective-permute-start | bytes 2359304 | tf_op jit(solution)/shard_map/ppermute | solution.py:190
  139.4 1.5 collective-permute-start.21
  140.9 12.7 %collective-permute-done.11 = bf16[2,64,3072]{2,1,0:T(8,128)(2,1)} collective-permute-done((bf16[2,64,3072]{2,1,0:T(8,128)(2,1)}, bf16[2,64,3072]{2,1,0:T(8,128)(2,1)}, u32[]{:S(2)}, u32[]{:S(2)}) %collective-permute-start.11) | collective-permute-done | bytes 786464 | tf_op jit(solution)/shard_map/ppermute | solution.py:193
  154.1 2.3 %fusion.30 = bf16[2,64,3072]{2,1,0:T(8,128)(2,1)S(1)} fusion(bf16[2,64,3072]{2,1,0:T(8,128)(2,1)} %collective-permute-done.11, bf16[2,64,3072]{2,1,0:T(8,128)(2,1)} %collective-permute-done.8, f32[2,2,64,3072]{3,2,1,0:T(8,128)S(1)} %bitcast.107, s32[]{:T(128)S(6)} %select_n.380, f32[2,2,64,3072]{3,2,1,0:T(8,128)} %bitcast.110, pred[]{:T(512)S(6)} %eq.66), kind=kLoop, calls=%fused_computation.36 | loop fusion | flops 2359296 | bytes 5505029 | tf_op jit(solution)/shard_map/convert_element_type | solution.py:197
  156.6 12.3 %collective-permute-done.21.refs_6_ = bf16[256,1536]{1,0:T(8,128)(2,1)S(1)} collective-permute-done((bf16[256,1536]{1,0:T(8,128)(2,1)}, bf16[256,1536]{1,0:T(8,128)(2,1)S(1)}, u32[]{:S(2)}, u32[]{:S(2)}) %collective-permute-start.21) | collective-permute-done | bytes 786464 | tf_op jit(solution)/shard_map/ppermute | solution.py:158
  170.9 30.0 %shard_map.77 = f32[1536,6144]{1,0:T(8,128)} custom-call(s32[7]{0:T(128)} %stack.39.place_ref, bf16[256,1536]{1,0:T(8,128)(2,1)} %pad_maximum_fusion.1.refs_0_, bf16[256,1536]{1,0:T(8,128)(2,1)} %collective-permute-done.16.refs_1_, bf16[256,1536]{1,0:T(8,128)(2,1)} %collective-permute-done.17.refs_2_, bf16[256,1536]{1,0:T(8,128)(2,1)} %collective-permute-done.18.refs_3_, ...), custom_call_target="tpu_custom_call" | custom-call | flops 19327352832 | bytes 53477376 | tf_op jit(solution)/shard_map/pallas_call | solution.py:62
  (61 shorter events, 11.8 us)
Async XLA Ops:
  0.6 27.0 %copy-start = (bf16[64,6144]{1,0:T(8,128)(2,1)S(1)}, bf16[64,6144]{1,0:T(8,128)(2,1)}, u32[]{:S(2)}) copy-start(bf16[64,6144]{1,0:T(8,128)(2,1)} %param.6) | copy-start | bytes 2359300
  5.2 20.7 %collective-permute-start = (bf16[64,6144]{1,0:T(8,128)(2,1)}, bf16[64,6144]{1,0:T(8,128)(2,1)S(1)}, u32[]{:S(2)}, u32[]{:S(2)}) collective-permute-start(bf16[64,6144]{1,0:T(8,128)(2,1)} %get-tuple-element.13.refs_7_), channel_id=1, source_target_pairs={{0,4},{4,0},{1,5},{5,1},{2,6},{6,2},{3,7},{7,3},{8,12},{12,8},{9,1... | collective-permute-start | bytes 2359304 | tf_op jit(solution)/shard_map/ppermute | solution.py:100
  8.1 33.3 %collective-permute-start.4 = (bf16[64,6144]{1,0:T(8,128)(2,1)}, bf16[64,6144]{1,0:T(8,128)(2,1)}, u32[]{:S(2)}, u32[]{:S(2)}) collective-permute-start(bf16[64,6144]{1,0:T(8,128)(2,1)} %get-tuple-element.13.refs_7_), channel_id=1, source_target_pairs={{0,1},{1,0},{2,3},{3,2},{4,5},{5,4},{6,7},{7,6},{8,9},{9,8},{10,11... | collective-permute-start | bytes 2359304 | tf_op jit(solution)/shard_map/ppermute | solution.py:97
  25.9 21.2 %copy-start.1 = (bf16[64,6144]{1,0:T(8,128)(2,1)}, bf16[64,6144]{1,0:T(8,128)(2,1)S(1)}, u32[]{:S(2)}) copy-start(bf16[64,6144]{1,0:T(8,128)(2,1)S(1)} %collective-permute-done.refs_9_) | copy-start | bytes 2359300
  25.9 19.9 %collective-permute-start.1 = (bf16[64,6144]{1,0:T(8,128)(2,1)}, bf16[64,6144]{1,0:T(8,128)(2,1)}, u32[]{:S(2)}, u32[]{:S(2)}) collective-permute-start(bf16[64,6144]{1,0:T(8,128)(2,1)} %get-tuple-element.4.refs_8_), channel_id=1, source_target_pairs={{0,4},{4,0},{1,5},{5,1},{2,6},{6,2},{3,7},{7,3},{8,12},{12,8},{9,1... | collective-permute-start | bytes 2359304 | tf_op jit(solution)/shard_map/ppermute | solution.py:100
  27.6 19.4 %collective-permute-start.5 = (bf16[64,6144]{1,0:T(8,128)(2,1)S(1)}, bf16[64,6144]{1,0:T(8,128)(2,1)}, u32[]{:S(2)}, u32[]{:S(2)}) collective-permute-start(bf16[64,6144]{1,0:T(8,128)(2,1)S(1)} %collective-permute-done.refs_9_), channel_id=1, source_target_pairs={{0,1},{1,0},{2,3},{3,2},{4,5},{5,4},{6,7},{7,6},{8,9},{9,8},{10,11... | collective-permute-start | bytes 2359304 | tf_op jit(solution)/shard_map/ppermute | solution.py:97
  27.7 2.5 %collective-permute-start.13 = (bf16[64,1536]{1,0:T(8,128)(2,1)S(1)}, bf16[64,1536]{1,0:T(8,128)(2,1)S(1)}, u32[]{:S(2)}, u32[]{:S(2)}) collective-permute-start(bf16[64,1536]{1,0:T(8,128)(2,1)S(1)} %get-tuple-element.15), channel_id=1, source_target_pairs={{0,1},{1,0},{2,3},{3,2},{4,5},{5,4},{6,7},{7,6},{8,9},{9,8},{10,11... | collective-permute-start | bytes 589832 | tf_op jit(solution)/shard_map/ppermute | solution.py:97
  28.2 7.8 %collective-permute-start.14 = (bf16[64,1536]{1,0:T(8,128)(2,1)S(1)}, bf16[64,1536]{1,0:T(8,128)(2,1)S(1)}, u32[]{:S(2)}, u32[]{:S(2)}) collective-permute-start(bf16[64,1536]{1,0:T(8,128)(2,1)S(1)} %get-tuple-element.17), channel_id=1, source_target_pairs={{0,2},{1,3},{2,0},{3,1},{4,6},{5,7},{6,4},{7,5},{8,10},{9,11},{10,... | collective-permute-start | bytes 589832 | tf_op jit(solution)/shard_map/ppermute | solution.py:97
  30.2 9.1 %collective-permute-start.15 = (bf16[64,1536]{1,0:T(8,128)(2,1)S(1)}, bf16[64,1536]{1,0:T(8,128)(2,1)S(1)}, u32[]{:S(2)}, u32[]{:S(2)}) collective-permute-start(bf16[64,1536]{1,0:T(8,128)(2,1)S(1)} %get-tuple-element.16), channel_id=1, source_target_pairs={{0,3},{1,2},{2,1},{3,0},{4,7},{5,6},{6,5},{7,4},{8,11},{9,10},{10,... | collective-permute-start | bytes 589832 | tf_op jit(solution)/shard_map/ppermute | solution.py:97
  36.0 62.5 %collective-permute-start.22 = (bf16[64,6144]{1,0:T(8,128)(2,1)}, bf16[64,6144]{1,0:T(8,128)(2,1)}, u32[]{:S(2)}, u32[]{:S(2)}) collective-permute-start(bf16[64,6144]{1,0:T(8,128)(2,1)} %get-tuple-element.13.refs_7_), channel_id=1, source_target_pairs={{0,2},{1,3},{2,0},{3,1},{4,6},{5,7},{6,4},{7,5},{8,10},{9,11},{10,... | collective-permute-start | bytes 2359304 | tf_op jit(solution)/shard_map/ppermute | solution.py:97
  39.3 25.8 %collective-permute-start.2 = (bf16[64,6144]{1,0:T(8,128)(2,1)}, bf16[64,6144]{1,0:T(8,128)(2,1)}, u32[]{:S(2)}, u32[]{:S(2)}) collective-permute-start(bf16[64,6144]{1,0:T(8,128)(2,1)} %get-tuple-element.4.refs_8_), channel_id=1, source_target_pairs={{0,1},{1,0},{2,3},{3,2},{4,5},{5,4},{6,7},{7,6},{8,9},{9,8},{10,11... | collective-permute-start | bytes 2359304 | tf_op jit(solution)/shard_map/ppermute | solution.py:97
  41.4 58.7 %collective-permute-start.16 = (bf16[256,1536]{1,0:T(8,128)(2,1)}, bf16[256,1536]{1,0:T(8,128)(2,1)}, u32[]{:S(2)}, u32[]{:S(2)}) collective-permute-start(bf16[256,1536]{1,0:T(8,128)(2,1)} %pad_maximum_fusion.1.refs_0_), channel_id=1, source_target_pairs={{0,8},{8,16},{16,24},{1,9},{9,17},{17,25},{2,10},{10,18},{18,26},{... | collective-permute-start | bytes 2359304 | tf_op jit(solution)/shard_map/ppermute | solution.py:157
  45.7 54.3 %collective-permute-start.17 = (bf16[256,1536]{1,0:T(8,128)(2,1)}, bf16[256,1536]{1,0:T(8,128)(2,1)}, u32[]{:S(2)}, u32[]{:S(2)}) collective-permute-start(bf16[256,1536]{1,0:T(8,128)(2,1)} %pad_maximum_fusion.1.refs_0_), channel_id=1, source_target_pairs={{8,0},{16,8},{24,16},{9,1},{17,9},{25,17},{10,2},{18,10},{26,18},{... | collective-permute-start | bytes 2359304 | tf_op jit(solution)/shard_map/ppermute | solution.py:158
  47.1 23.4 %collective-permute-start.3 = (bf16[64,6144]{1,0:T(8,128)(2,1)}, bf16[64,6144]{1,0:T(8,128)(2,1)}, u32[]{:S(2)}, u32[]{:S(2)}) collective-permute-start(bf16[64,6144]{1,0:T(8,128)(2,1)} %collective-permute-done.1.refs_10_), channel_id=1, source_target_pairs={{0,1},{1,0},{2,3},{3,2},{4,5},{5,4},{6,7},{7,6},{8,9},{9,8},{10,11... | collective-permute-start | bytes 2359304 | tf_op jit(solution)/shard_map/ppermute | solution.py:97
  65.0 25.5 %collective-permute-start.6 = (bf16[2,64,3072]{2,1,0:T(8,128)(2,1)}, bf16[2,64,3072]{2,1,0:T(8,128)(2,1)}, u32[]{:S(2)}, u32[]{:S(2)}) collective-permute-start(bf16[2,64,3072]{2,1,0:T(8,128)(2,1)} %get-tuple-element.10), channel_id=1, source_target_pairs={{0,8},{1,9},{2,10},{3,11},{4,12},{5,13},{6,14},{7,15}} | collective-permute-start | bytes 2359304 | tf_op jit(solution)/shard_map/ppermute | solution.py:190
  70.4 20.0 %collective-permute-start.9 = (bf16[2,64,3072]{2,1,0:T(8,128)(2,1)}, bf16[2,64,3072]{2,1,0:T(8,128)(2,1)}, u32[]{:S(2)}, u32[]{:S(2)}) collective-permute-start(bf16[2,64,3072]{2,1,0:T(8,128)(2,1)} %get-tuple-element.11), channel_id=1, source_target_pairs={{24,16},{25,17},{26,18},{27,19},{28,20},{29,21},{30,22},{31,23}} | collective-permute-start | bytes 2359304 | tf_op jit(solution)/shard_map/ppermute | solution.py:193
  94.8 6.9 %collective-permute-start.10 = (bf16[2,64,3072]{2,1,0:T(8,128)(2,1)}, bf16[2,64,3072]{2,1,0:T(8,128)(2,1)}, u32[]{:S(2)}, u32[]{:S(2)}) collective-permute-start(bf16[2,64,3072]{2,1,0:T(8,128)(2,1)} %get-tuple-element.9), channel_id=1, source_target_pairs={{16,8},{24,16},{17,9},{25,17},{18,10},{26,18},{19,11},{27,19},{20,... | collective-permute-start | bytes 2359304 | tf_op jit(solution)/shard_map/ppermute | solution.py:193
  96.3 19.0 %collective-permute-start.7 = (bf16[2,64,3072]{2,1,0:T(8,128)(2,1)}, bf16[2,64,3072]{2,1,0:T(8,128)(2,1)}, u32[]{:S(2)}, u32[]{:S(2)}) collective-permute-start(bf16[2,64,3072]{2,1,0:T(8,128)(2,1)} %get-tuple-element.8), channel_id=1, source_target_pairs={{0,8},{8,16},{1,9},{9,17},{2,10},{10,18},{3,11},{11,19},{4,12},{12... | collective-permute-start | bytes 2359304 | tf_op jit(solution)/shard_map/ppermute | solution.py:190
  98.5 21.7 %collective-permute-start.23 = (bf16[64,6144]{1,0:T(8,128)(2,1)}, bf16[64,6144]{1,0:T(8,128)(2,1)}, u32[]{:S(2)}, u32[]{:S(2)}) collective-permute-start(bf16[64,6144]{1,0:T(8,128)(2,1)} %get-tuple-element.4.refs_8_), channel_id=1, source_target_pairs={{0,2},{1,3},{2,0},{3,1},{4,6},{5,7},{6,4},{7,5},{8,10},{9,11},{10,... | collective-permute-start | bytes 2359304 | tf_op jit(solution)/shard_map/ppermute | solution.py:97
  100.1 21.7 %collective-permute-start.26 = (bf16[64,6144]{1,0:T(8,128)(2,1)}, bf16[64,6144]{1,0:T(8,128)(2,1)}, u32[]{:S(2)}, u32[]{:S(2)}) collective-permute-start(bf16[64,6144]{1,0:T(8,128)(2,1)} %collective-permute-done.22.refs_15_), channel_id=1, source_target_pairs={{0,1},{1,0},{2,3},{3,2},{4,5},{5,4},{6,7},{7,6},{8,9},{9,8},{10,11... | collective-permute-start | bytes 2359304 | tf_op jit(solution)/shard_map/ppermute | solution.py:97
  100.1 23.0 %collective-permute-start.18 = (bf16[256,1536]{1,0:T(8,128)(2,1)}, bf16[256,1536]{1,0:T(8,128)(2,1)}, u32[]{:S(2)}, u32[]{:S(2)}) collective-permute-start(bf16[256,1536]{1,0:T(8,128)(2,1)} %collective-permute-done.16.refs_1_), channel_id=1, source_target_pairs={{8,16},{16,24},{9,17},{17,25},{10,18},{18,26},{11,19},{19,27},{12,... | collective-permute-start | bytes 2359304 | tf_op jit(solution)/shard_map/ppermute | solution.py:157
  101.6 36.0 %collective-permute-start.19 = (bf16[256,1536]{1,0:T(8,128)(2,1)}, bf16[256,1536]{1,0:T(8,128)(2,1)}, u32[]{:S(2)}, u32[]{:S(2)}) collective-permute-start(bf16[256,1536]{1,0:T(8,128)(2,1)} %collective-permute-done.17.refs_2_), channel_id=1, source_target_pairs={{8,0},{16,8},{9,1},{17,9},{10,2},{18,10},{11,3},{19,11},{12,4},{20... | collective-permute-start | bytes 2359304 | tf_op jit(solution)/shard_map/ppermute | solution.py:158
  115.4 22.2 %collective-permute-start.24 = (bf16[64,6144]{1,0:T(8,128)(2,1)}, bf16[64,6144]{1,0:T(8,128)(2,1)}, u32[]{:S(2)}, u32[]{:S(2)}) collective-permute-start(bf16[64,6144]{1,0:T(8,128)(2,1)} %collective-permute-done.22.refs_15_), channel_id=1, source_target_pairs={{0,4},{4,0},{1,5},{5,1},{2,6},{6,2},{3,7},{7,3},{8,12},{12,8},{9,1... | collective-permute-start | bytes 2359304 | tf_op jit(solution)/shard_map/ppermute | solution.py:100
  120.2 19.2 %collective-permute-start.25 = (bf16[64,6144]{1,0:T(8,128)(2,1)}, bf16[64,6144]{1,0:T(8,128)(2,1)}, u32[]{:S(2)}, u32[]{:S(2)}) collective-permute-start(bf16[64,6144]{1,0:T(8,128)(2,1)} %collective-permute-done.1.refs_10_), channel_id=1, source_target_pairs={{0,2},{1,3},{2,0},{3,1},{4,6},{5,7},{6,4},{7,5},{8,10},{9,11},{10,... | collective-permute-start | bytes 2359304 | tf_op jit(solution)/shard_map/ppermute | solution.py:97
  121.8 31.9 %collective-permute-start.11 = (bf16[2,64,3072]{2,1,0:T(8,128)(2,1)}, bf16[2,64,3072]{2,1,0:T(8,128)(2,1)}, u32[]{:S(2)}, u32[]{:S(2)}) collective-permute-start(bf16[2,64,3072]{2,1,0:T(8,128)(2,1)} %get-tuple-element.7), channel_id=1, source_target_pairs={{8,0},{16,8},{24,16},{9,1},{17,9},{25,17},{10,2},{18,10},{26,18},{... | collective-permute-start | bytes 2359304 | tf_op jit(solution)/shard_map/ppermute | solution.py:193
  123.1 30.6 %collective-permute-start.8 = (bf16[2,64,3072]{2,1,0:T(8,128)(2,1)}, bf16[2,64,3072]{2,1,0:T(8,128)(2,1)}, u32[]{:S(2)}, u32[]{:S(2)}) collective-permute-start(bf16[2,64,3072]{2,1,0:T(8,128)(2,1)} %get-tuple-element.6), channel_id=1, source_target_pairs={{0,8},{8,16},{16,24},{1,9},{9,17},{17,25},{2,10},{10,18},{18,26},{... | collective-permute-start | bytes 2359304 | tf_op jit(solution)/shard_map/ppermute | solution.py:190
  137.6 18.9 %collective-permute-start.27 = (bf16[64,6144]{1,0:T(8,128)(2,1)}, bf16[64,6144]{1,0:T(8,128)(2,1)S(1)}, u32[]{:S(2)}, u32[]{:S(2)}) collective-permute-start(bf16[64,6144]{1,0:T(8,128)(2,1)} %collective-permute-done.23.refs_16_), channel_id=1, source_target_pairs={{0,1},{1,0},{2,3},{3,2},{4,5},{5,4},{6,7},{7,6},{8,9},{9,8},{10,11... | collective-permute-start | bytes 2359304 | tf_op jit(solution)/shard_map/ppermute | solution.py:97
  137.6 19.0 %collective-permute-start.20 = (bf16[256,1536]{1,0:T(8,128)(2,1)}, bf16[256,1536]{1,0:T(8,128)(2,1)S(1)}, u32[]{:S(2)}, u32[]{:S(2)}) collective-permute-start(bf16[256,1536]{1,0:T(8,128)(2,1)} %collective-permute-done.18.refs_3_), channel_id=1, source_target_pairs={{16,24},{17,25},{18,26},{19,27},{20,28},{21,29},{22,30},{23,31}} | collective-permute-start | bytes 2359304 | tf_op jit(solution)/shard_map/ppermute | solution.py:157
  139.4 29.4 %collective-permute-start.21 = (bf16[256,1536]{1,0:T(8,128)(2,1)}, bf16[256,1536]{1,0:T(8,128)(2,1)S(1)}, u32[]{:S(2)}, u32[]{:S(2)}) collective-permute-start(bf16[256,1536]{1,0:T(8,128)(2,1)} %collective-permute-done.19.refs_4_), channel_id=1, source_target_pairs={{8,0},{9,1},{10,2},{11,3},{12,4},{13,5},{14,6},{15,7}} | collective-permute-start | bytes 2359304 | tf_op jit(solution)/shard_map/ppermute | solution.py:158
  153.6 15.2 %collective-permute-start.28 = (bf16[64,6144]{1,0:T(8,128)(2,1)}, bf16[64,6144]{1,0:T(8,128)(2,1)S(1)}, u32[]{:S(2)}, u32[]{:S(2)}) collective-permute-start(bf16[64,6144]{1,0:T(8,128)(2,1)} %collective-permute-done.24.refs_17_), channel_id=1, source_target_pairs={{0,1},{1,0},{2,3},{3,2},{4,5},{5,4},{6,7},{7,6},{8,9},{9,8},{10,11... | collective-permute-start | bytes 2359304 | tf_op jit(solution)/shard_map/ppermute | solution.py:97
  153.6 15.2 %collective-permute-start.29 = (bf16[64,6144]{1,0:T(8,128)(2,1)}, bf16[64,6144]{1,0:T(8,128)(2,1)S(1)}, u32[]{:S(2)}, u32[]{:S(2)}) collective-permute-start(bf16[64,6144]{1,0:T(8,128)(2,1)} %collective-permute-done.25.refs_18_), channel_id=1, source_target_pairs={{0,1},{1,0},{2,3},{3,2},{4,5},{5,4},{6,7},{7,6},{8,9},{9,8},{10,11... | collective-permute-start | bytes 2359304 | tf_op jit(solution)/shard_map/ppermute | solution.py:97
  156.5 44.4 %collective-permute-start.12 = (bf16[64,3072]{1,0:T(8,128)(2,1)S(1)}, bf16[64,3072]{1,0:T(8,128)(2,1)S(1)}, u32[]{:S(2)}, u32[]{:S(2)}) collective-permute-start(bf16[64,3072]{1,0:T(8,128)(2,1)S(1)} %get-tuple-element.20), channel_id=1, source_target_pairs={{0,1},{1,0},{2,3},{3,2},{4,5},{5,4},{6,7},{7,6},{8,9},{9,8},{10,11... | collective-permute-start | bytes 1179656 | tf_op jit(solution)/shard_map/ppermute | solution.py:97
  (5 other events, 27.6 us)

commit v2 on v1

v2 whole, which is shorter than its diff:
```python
import functools

import jax
import jax.numpy as jnp
from jax import lax
from jax.experimental import pallas as pl
from jax.experimental.pallas import tpu as pltpu
from jax.sharding import PartitionSpec as P

K = 4
CDW = 2
CDX = 0
VMEM = 60 << 20


def pass_weights(samples, correct):
    total = samples.astype(jnp.float32)
    good = correct.astype(jnp.float32)
    missing = jnp.ones_like(total)
    for factor_index in range(K):
        missing = missing * jnp.maximum(total - good - factor_index, 0.0) / (total - factor_index)
    return 1.0 - missing


def token_weights(prompt_ids, samples, correct):
    pass_at_k = pass_weights(samples, correct)
    prompt_range = jnp.arange(samples.shape[0], dtype=jnp.int32)
    matches = prompt_ids[:, None] == prompt_range[None, :]
    picked = jnp.sum(jnp.where(matches, pass_at_k[None, :], 0.0), axis=1, keepdims=True)
    rounded = lax.optimization_barrier(picked.astype(jnp.bfloat16))
    return rounded.astype(jnp.float32)


def COST_DW(m, f, tokens):
    return pl.CostEstimate(flops=CDW * m * f * tokens, bytes_accessed=CDW * (tokens * (m + f) + 2 * m * f), transcendentals=0)


def COST_DX(n, f, width):
    return pl.CostEstimate(flops=CDX * n * f * width, bytes_accessed=CDX * f * (width + n), transcendentals=0)


def after(value, *others):
    return lax.optimization_barrier((value,) + others)[0]


def weight_grad_kernel(place_ref, *refs, n_x, n_s, n_h, rows):
    x_refs, s_refs, out_ref, x_all, s_all = refs[:n_x], refs[n_x:n_x + n_s], refs[-3], refs[-2], refs[-1]
    groups = x_refs[0].shape[0] // rows

    @pl.when(pl.program_id(0) == 0)
    def _():
        for k in range(n_x):
            @pl.when(place_ref[k * groups] >= 0)
            def _(k=k):
                for g in range(groups):
                    start = pl.multiple_of((g * n_h + place_ref[k * groups + g]) * rows, rows)
                    x_all[pl.ds(start, rows), :] = x_refs[k][g * rows:(g + 1) * rows, :]

    start = 0
    for s_ref in s_refs:
        s_all[start:start + s_ref.shape[0], :] = s_ref[...]
        start += s_ref.shape[0]
    out_ref[...] = lax.dot_general(
        x_all[...], s_all[...], (((0,), (0,)), ((), ())), preferred_element_type=jnp.float32
    )


def column_block(f):
    return next((b for b in (1024, 512, 256, 128) if f % b == 0 and f // b > 2), f)


def weight_grad(places, x_pieces, s_pieces, n_h, rows, due):
    x_rows, m = x_pieces[0].shape
    f = s_pieces[0].shape[1]
    tokens = x_rows * n_h
    block = column_block(f)
    body = functools.partial(weight_grad_kernel, n_x=len(x_pieces), n_s=len(s_pieces), n_h=n_h, rows=rows)
    return pl.pallas_call(
        body,
        grid_spec=pltpu.PrefetchScalarGridSpec(
            num_scalar_prefetch=1,
            grid=(f // block,),
            in_specs=[pl.BlockSpec((x_rows, m), lambda j, p: (0, 0))] * len(x_pieces)
            + [pl.BlockSpec((piece.shape[0], block), lambda j, p: (0, j)) for piece in s_pieces],
            out_specs=pl.BlockSpec((m, block), lambda j, p: (0, j)),
            scratch_shapes=[pltpu.VMEM((tokens, m), jnp.bfloat16), pltpu.VMEM((tokens, block), jnp.bfloat16)],
        ),
        out_shape=jax.ShapeDtypeStruct((m, f), jnp.float32),
        compiler_params=pltpu.CompilerParams(vmem_limit_bytes=VMEM),
        cost_estimate=COST_DW(m, f, tokens),
    )(after(places, *due) if due else places, *x_pieces, *s_pieces)


def input_grad_kernel(first_ref, *refs):
    piece_refs, weight_ref, out_ref, tokens = refs[:-3], refs[-3], refs[-2], refs[-1]
    rows = piece_refs[0].shape[0]

    @pl.when(pl.program_id(0) == 0)
    def _():
        for k, piece_ref in enumerate(piece_refs):
            tokens[k * rows:(k + 1) * rows, :] = piece_ref[...]

    share = lax.dot_general(
        tokens[...], weight_ref[...], (((1,), (1,)), ((), ())), preferred_element_type=jnp.float32
    ).astype(out_ref.dtype)
    per_owner = out_ref.shape[2]
    for k in range(out_ref.shape[0]):
        out_ref[k, 0] = share[k * per_owner:(k + 1) * per_owner]


def input_grad(core, n_c, rows, pieces, weight, owners, parts, due):
    d, f = weight.shape
    width = d // n_c
    n = rows * len(pieces)
    part = width // parts
    block = next(b for b in (512, 256, 128, part) if part % b == 0)
    per_part = part // block
    steps = width // block
    first = jnp.stack([core * steps] + [index for _, index in pieces]).astype(jnp.int32)
    return pl.pallas_call(
        input_grad_kernel,
        grid_spec=pltpu.PrefetchScalarGridSpec(
            num_scalar_prefetch=1,
            grid=(steps,),
            in_specs=[pl.BlockSpec((rows, f), lambda j, c, k=k: (c[k + 1], 0)) for k in range(len(pieces))]
            + [pl.BlockSpec((block, f), lambda j, c: (c[0] + j, 0))],
            out_specs=pl.BlockSpec(
                (owners, 1, n // owners, block), lambda j, c: (0, j // per_part, 0, j % per_part)
            ),
            scratch_shapes=[pltpu.VMEM((n, f), jnp.bfloat16)],
        ),
        out_shape=jax.ShapeDtypeStruct((owners, parts, n // owners, part), jnp.bfloat16),
        compiler_params=pltpu.CompilerParams(vmem_limit_bytes=VMEM),
        cost_estimate=COST_DX(n, f, width),
    )(after(first, *due) if due else first, *[piece for piece, _ in pieces], weight)


def make_body(n_h, n_w, n_r):
    n_c = 2 if n_r % 2 == 0 else 1
    n_y = n_r // n_c
    per_w = n_h // n_w

    def slot(w_index, group):
        return group if w_index < n_w // 2 else per_w - 1 - group

    def slot_of(w_index, group):
        return jnp.where(w_index < n_w // 2, group, per_w - 1 - group)

    def replica_perm(dy, dc):
        return [
            (y * n_c + c, (y + dy) % n_y * n_c + (c + dc) % n_c) for y in range(n_y) for c in range(n_c)
        ]

    def over_replica(value, dy, dc):
        return lax.ppermute(value, "replica", replica_perm(dy, dc))

    def over_width(value, dx):
        return lax.ppermute(value, "width", [(w, (w + dx) % n_w) for w in range(n_w)])

    def body(saved_input, grad_out, weight, samples, correct, prompt_ids):
        h, w, r = lax.axis_index("hidden"), lax.axis_index("width"), lax.axis_index("replica")
        y, c = r // n_c, r % n_c
        x_rows, d_half = saved_input.shape
        s_rows, f = grad_out.shape
        rows = s_rows // per_w
        d_core = d_half // n_c
        d_own = d_half // n_r

        parts = []
        for dy in range(n_y):
            for dc in range(n_c):
                target = (y + dy) % n_y * n_c + (c + dc) % n_c
                part = lax.dynamic_slice_in_dim(saved_input, target * d_own, d_own, 1)
                parts.append(part if dy == dc == 0 else over_replica(part, dy, dc))
        x_own = jnp.concatenate(parts, axis=0)

        all_weights = token_weights(prompt_ids, samples, correct)
        scale = lax.dynamic_slice_in_dim(all_weights, w * s_rows, s_rows, 0)
        scaled = (grad_out.astype(jnp.float32) * scale).astype(jnp.bfloat16)

        own_group = [lax.dynamic_slice_in_dim(scaled, slot_of(w, q) * rows, rows, 0) for q in range(per_w)]

        def spread(value, *late):
            value = after(value, *late) if late else value
            return [value] + [over_replica(value, 0, dc) for dc in range(1, n_c)]

        whole = spread(scaled, *parts[1:n_c])
        x_own = after(x_own, *whole[1:])
        piece, cores = {}, {}

        def send_x(q, *late):
            own = after(own_group[q], *late) if late else own_group[q]
            for dx in range(1, n_w):
                piece[0, dx, q] = over_width(own, dx)

        def send_y(q, *late):
            own = after(own_group[q], *late)
            for dy in range(1, n_y):
                piece[dy, 0, q] = over_replica(own, dy, 0)

        def send_on(q, *late):
            for dy in range(1, n_y):
                for dx in range(1, n_w):
                    if q % 2 == 0:
                        piece[dy, dx, q] = over_width(after(piece[dy, 0, q], *late), dx)
                    else:
                        piece[dy, dx, q] = over_replica(after(piece[0, dx, q], *late), dy, 0)

        def over_x(q):
            return tuple(piece[0, dx, q] for dx in range(1, n_w))

        def over_y(q):
            return tuple(piece[dy, 0, q] for dy in range(1, n_y))

        shares = []

        def share_of(target, choices, come=()):
            target = jnp.clip(target, 0, n_h - 1)
            owner, group = target // per_w, target % per_w
            dx, q = (w - owner) % n_w, slot_of(owner, group)
            picked = None
            for choice in choices:
                share = after(shares[choice], *come) if come else shares[choice]
                value = lax.dynamic_index_in_dim(share, dx, 0, keepdims=False)
                picked = value if picked is None else jnp.where(q == choice, value, picked)
            return picked.reshape(x_own.shape)

        def passes(targets):
            return sorted({slot(t // per_w, t % per_w) for t in targets})

        right, left, sums = [x_own], [x_own], [None, None]

        def step_planes(m, *late):
            step, apart = m - 1, n_h - m + 1
            to_right, to_left = (right[-1], left[-1]) if m < n_h else (None, None)
            if step:
                choices = passes([j + apart for j in range(step)] + [j - apart for j in range(apart, n_h)])
                come = tuple(sums)
                up, down = share_of(h + apart, choices, come), share_of(h - apart, choices, come)
                if step > 1:
                    up = (up.astype(jnp.float32) + sums[0].astype(jnp.float32)).astype(jnp.bfloat16)
                    down = (down.astype(jnp.float32) + sums[1].astype(jnp.float32)).astype(jnp.bfloat16)
                to_right = up if to_right is None else jnp.where(h >= step, to_right, up)
                to_left = down if to_left is None else jnp.where(h < apart, to_left, down)
            if late:
                to_right, to_left = after(to_right, *late), after(to_left, *late)
            come_right = lax.ppermute(to_right, "hidden", [(j, j + 1) for j in range(n_h - 1)])
            come_left = lax.ppermute(to_left, "hidden", [(j, j - 1) for j in range(1, n_h)])
            if m < n_h:
                right.append(come_right)
                left.append(come_left)
            sums[:] = [come_right, come_left]

        send_x(0)
        step_planes(1)
        send_y(0, *parts, *whole[1:])
        for dx in range(1, n_w):
            cores[0, dx, 0] = spread(piece[0, dx, 0])
        for q in range(per_w):
            late = tuple(shares[-1:])
            tokens = []
            for dx in range(n_w):
                for dc in range(n_c):
                    tokens.append((cores[0, dx, q][dc], w * 0) if dx else (whole[dc], slot_of(w, q)))
            due = late + tuple(parts)
            if q:
                due = late + (right[q], left[q]) + tuple(cores[dy, 0, q - 1][-1] for dy in range(1, n_y))
            if q + 1 < per_w:
                send_x(q + 1, *over_x(q), *whole[1:])
            share = input_grad(c, n_c, rows, tokens, weight, n_w, n_y, due)
            shares.append(share)
            for dy in range(1, n_y):
                cores[dy, 0, q] = spread(piece[dy, 0, q], share)
            if q + 1 < per_w:
                for dx in range(1, n_w):
                    cores[0, dx, q + 1] = spread(piece[0, dx, q + 1], share)
                step_planes(q + 2, *(cores[0, dx, q + 1][-1] for dx in range(1, n_w)))
                send_y(q + 1, share, *over_y(q))
                send_on(q, *over_x(q + 1))
        for q in range(per_w - 1, per_w):
            send_on(q, *over_y(q), *over_x(q), *shares[-1:])
        for dy in range(1, n_y):
            for dx in range(1, n_w):
                for q in range(per_w):
                    cores[dy, dx, q] = spread(piece[dy, dx, q])
        for m in range(per_w + 1, n_h):
            step_planes(m)
        due = tuple(sums)
        step_planes(n_h)

        places, pieces = [], []
        for k in range(n_h):
            if right[k] is left[k]:
                sides = [(jnp.where(h >= k, h - k, h + k), right[k], (h >= k) | (h + k < n_h))]
            else:
                sides = [(h - k, right[k], h >= k), (h + k, left[k], h + k < n_h)]
            for plane, planes_x, there in sides:
                owner, group = plane // per_w, plane % per_w
                dx = (w - owner) % n_w
                for dy in range(n_y):
                    sent_order = slot_of(owner, group) if dy else jnp.where(dx == 0, group, slot_of(owner, group))
                    place = jnp.where(there, dx * per_w + sent_order, -1).astype(jnp.int32)
                    places += [place] * n_c
                pieces.append(planes_x)
        s_pieces = []
        for dy in range(n_y):
            for dc in range(n_c):
                for dx in range(n_w):
                    if dy == dx == 0:
                        s_pieces.append(whole[dc])
                    else:
                        s_pieces += [cores[dy, dx, q][dc] for q in range(per_w)]
        places = jnp.stack(places)
        grad_weight = weight_grad(places, pieces, s_pieces, n_h, rows, due)
        from_left, from_right = after(sums[0], grad_weight), sums[1]
        total = share_of(h, range(per_w)).astype(jnp.float32)
        total = total + from_left.astype(jnp.float32) + from_right.astype(jnp.float32)
        total = total.astype(jnp.bfloat16).reshape(n_y, n_c, rows, d_own)
        held = [total[:, 0]] + [over_replica(total[:, dc], 0, n_c - dc) for dc in range(1, n_c)]
        held = jnp.stack(held)
        by_core = [lax.dynamic_index_in_dim(held, (p - c) % n_c, 0, keepdims=False) for p in range(n_c)]
        grad_input = jnp.concatenate([value[k] for value in by_core for k in range(n_y)], axis=1)
        return grad_input, grad_weight

    return body


def solution(mesh):
    in_specs = (
        P(("replica", "hidden"), "width"),
        P(("replica", "width"), "hidden"),
        P("width", "hidden"),
        P(),
        P(),
        P("replica"),
    )
    out_specs = (P(("replica", "hidden"), "width"), P(("width", "replica"), "hidden"))
    body = make_body(mesh.shape["hidden"], mesh.shape["width"], mesh.shape["replica"])
    return jax.shard_map(body, mesh=mesh, in_specs=in_specs, out_specs=out_specs, check_vma=False)
```

time: 203 us -> 161 us (0.79)
  Pallas kernels: 30 us -> 66 us
  matrix products: 35 us -> 0 us
  waiting for transfers between devices: 63.1 us -> 30.2 us
  starting transfers between devices: 51.6 us -> 38.9 us
  local copies, waits for them, and re-layouts: 4.2 us -> 7.5 us
    pallas_call x0 -> x2, Pallas kernels: none -> 37.8 us  [input_grad(): pl.pallas_call(input_grad_kernel, grid_spec=pltpu.PrefetchScalarGridSpec(...]
    dot_general x2 -> x0, matrix products: 35 us -> none  [body(): lax.dot_general(tokens, own_weight, (((1,), (1,)), ((), ())), preferred_e...]
    ppermute x12 -> x8, waiting for transfers between devices: 37.5 us -> 11.7 us  [the longest x4 7.85 us: step_planes(): lax.ppermute(to_left, 'hidden', [(j, j - 1) for j in range(1, n_h)])]
    ppermute x3, waiting for transfers between devices: 17.7 us -> 5.11 us  [over_width(): lax.ppermute(value, 'width', [(w, (w + dx) % n_w) for w in range(n_w)])]
    convert_element_type x5 -> x4, other arithmetic: 13.7 us -> 3.33 us  [the longest x1 1.32 us: step_planes(): (down.astype(jnp.float32) + sums[1].astype(jnp.float32)).astype(jnp.bfloa...]
    ppermute x12 -> x8, starting transfers between devices: 36.6 us -> 26.7 us  [the longest x4 21.6 us: step_planes(): lax.ppermute(to_right, 'hidden', [(j, j + 1) for j in range(n_h - 1)])]
    select_n x0 -> x6, other arithmetic: none -> 9.31 us  [the longest x2 3.98 us: step_planes(): to_left = down if to_left is None else jnp.where(h < apart, to_left, down)]
    ppermute x15 -> x14, waiting for transfers between devices: 7.82 us -> 13.4 us  [over_replica(): return lax.ppermute(value, 'replica', replica_perm(dy, dc))]
  transfers between devices with their start and end apart: 30 -> 25, of which waited for: 8 -> 8; matrix products, arithmetic and copies ran while one was open for 24% -> 11% of each run, Pallas kernels for 15% -> 41%
where the time goes in v2:
time: 161 us; the launch traced here: 160 us
  Pallas kernels  66 us (41%)
  starting transfers between devices  38.9 us (24%)
  waiting for transfers between devices  30.2 us (19%)
  other arithmetic  16.5 us (10%)
  local copies, waits for them, and re-layouts  7.5 us (5%)
    pallas_call x2, Pallas kernels, input_grad(): pl.pallas_call(input_grad_kernel, grid_spec=pltpu.PrefetchScalarGridSpec(...  37.8 us
    pallas_call x1, Pallas kernels, weight_grad(): pl.pallas_call(body, grid_spec=pltpu.PrefetchScalarGridSpec(num_scalar_pr...  28.1 us
    ppermute x4, starting transfers between devices, step_planes(): lax.ppermute(to_right, 'hidden', [(j, j + 1) for j in range(n_h - 1)])  21.6 us
    ppermute x14, waiting for transfers between devices, over_replica(): return lax.ppermute(value, 'replica', replica_perm(dy, dc))  13.4 us
    ppermute x4, waiting for transfers between devices, step_planes(): lax.ppermute(to_left, 'hidden', [(j, j - 1) for j in range(1, n_h)])  7.85 us
    ppermute x14, starting transfers between devices, over_replica(): return lax.ppermute(value, 'replica', replica_perm(dy, dc))  7.5 us
    ppermute x4, starting transfers between devices, step_planes(): lax.ppermute(to_left, 'hidden', [(j, j - 1) for j in range(1, n_h)])  5.13 us
    ppermute x3, waiting for transfers between devices, over_width(): lax.ppermute(value, 'width', [(w, (w + dx) % n_w) for w in range(n_w)])  5.11 us
  transfers between devices with their start and end apart: 25, of which 8 were waited for; matrix products, arithmetic and copies ran while one was open for 11% of the time, Pallas kernels for 41%

profile of v2, /device:TPU:0, one launch (start us, length us, event | category | flops | bytes accessed | tf_op | source)
XLA Modules:
  0.0 160.3 jit_solution(13377787081177644372)
XLA Ops:
  0.8 2.1 %constant_dynamic-slice_fusion.8 = (bf16[64,1536]{1,0:T(8,128)(2,1)S(1)}, bf16[64,1536]{1,0:T(8,128)(2,1)}, bf16[64,1536]{1,0:T(8,128)(2,1)}, bf16[64,1536]{1,0:T(8,128)(2,1)S(1)}) fusion(bf16[64,6144]{1,0:T(8,128)(2,1)} %param.6, s32[]{:T(128)S(6)} %select_n.445, s32[]{:T(128)S(6)} %select_n.447, s32[]{:T(128)S(6)} %select_n.450, s32[]{:T(128)S(6)} %select_n.449), kind=kLoop, calls=%fused_computation.45 | loop fusion | bytes 1572880 | tf_op jit(solution)/shard_map/dynamic_slice | solution.py:173
  5.1 1.2 constant_dynamic-slice_fusion.2
  6.4 2.6 %collective-permute-start.4 = (bf16[64,6144]{1,0:T(8,128)(2,1)}, bf16[64,6144]{1,0:T(8,128)(2,1)}, u32[]{:S(2)}, u32[]{:S(2)}) collective-permute-start(bf16[64,6144]{1,0:T(8,128)(2,1)} %get-tuple-element.26), channel_id=1, source_target_pairs={{0,4},{4,0},{1,5},{5,1},{2,6},{6,2},{3,7},{7,3},{8,12},{12,8},{9,1... | collective-permute-start | bytes 2359304 | tf_op jit(solution)/shard_map/ppermute | solution.py:158
  9.0 1.2 collective-permute-start.2
  10.7 5.2 %collective-permute-done.2 = bf16[64,1536]{1,0:T(8,128)(2,1)S(1)} collective-permute-done((bf16[64,1536]{1,0:T(8,128)(2,1)S(1)}, bf16[64,1536]{1,0:T(8,128)(2,1)S(1)}, u32[]{:S(2)}, u32[]{:S(2)}) %collective-permute-start.2) | collective-permute-done | bytes 196640 | tf_op jit(solution)/shard_map/ppermute | solution.py:155
  16.0 4.5 %collective-permute-done.1 = bf16[64,1536]{1,0:T(8,128)(2,1)S(1)} collective-permute-done((bf16[64,1536]{1,0:T(8,128)(2,1)S(1)}, bf16[64,1536]{1,0:T(8,128)(2,1)S(1)}, u32[]{:S(2)}, u32[]{:S(2)}) %collective-permute-start.1) | collective-permute-done | bytes 196640 | tf_op jit(solution)/shard_map/ppermute | solution.py:155
  20.4 1.9 %pad_maximum_fusion.refs_0_ = bf16[256,1536]{1,0:T(8,128)(2,1)} fusion(bf16[64,1536]{1,0:T(8,128)(2,1)S(1)} %collective-permute-done.2, bf16[64,1536]{1,0:T(8,128)(2,1)S(1)} %collective-permute-done.1, bf16[64,1536]{1,0:T(8,128)(2,1)} %collective-permute-done, bf16[64,1536]{1,0:T(8,128)(2,1)S(1)} %get-tuple-element.56), kind=kLoop, calls=%fused_computation.18 | loop fusion | flops 3145728 | bytes 1572864 | tf_op jit(solution)/shard_map/concatenate | solution.py:175
  22.3 5.1 %collective-permute-done.4.refs_2_.refs_8_ = bf16[64,6144]{1,0:T(8,128)(2,1)} collective-permute-done((bf16[64,6144]{1,0:T(8,128)(2,1)}, bf16[64,6144]{1,0:T(8,128)(2,1)}, u32[]{:S(2)}, u32[]{:S(2)}) %collective-permute-start.4) | collective-permute-done | bytes 786464 | tf_op jit(solution)/shard_map/ppermute | solution.py:158
  27.4 1.8 %collective-permute-start.8 = (bf16[64,6144]{1,0:T(8,128)(2,1)}, bf16[64,6144]{1,0:T(8,128)(2,1)}, u32[]{:S(2)}, u32[]{:S(2)}) collective-permute-start(bf16[64,6144]{1,0:T(8,128)(2,1)} %get-tuple-element.26), channel_id=1, source_target_pairs={{0,2},{1,3},{2,0},{3,1},{4,6},{5,7},{6,4},{7,5},{8,10},{9,11},{10,... | collective-permute-start | bytes 2359304 | tf_op jit(solution)/shard_map/ppermute | solution.py:155
  29.2 1.3 collective-permute-start.7
  30.5 5.4 %collective-permute-start.6 = (bf16[256,1536]{1,0:T(8,128)(2,1)}, bf16[256,1536]{1,0:T(8,128)(2,1)}, u32[]{:S(2)}, u32[]{:S(2)}) collective-permute-start(bf16[256,1536]{1,0:T(8,128)(2,1)} %pad_maximum_fusion.refs_0_), channel_id=1, source_target_pairs={{0,8},{8,16},{16,24},{1,9},{9,17},{17,25},{2,10},{10,18},{18,26},{... | collective-permute-start | bytes 2359304 | tf_op jit(solution)/shard_map/ppermute | solution.py:247
  36.0 1.5 collective-permute-start.10
  38.1 18.9 %shard_map.77 = bf16[2,2,128,1536]{3,2,1,0:T(8,128)(2,1)} custom-call(s32[5]{0:T(128)} %get-tuple-element.23.first_ref, bf16[128,6144]{1,0:T(8,128)(2,1)} %copy-done.1, bf16[128,6144]{1,0:T(8,128)(2,1)} %copy-done.3, bf16[64,6144]{1,0:T(8,128)(2,1)} %collective-permute-done.4.refs_2_.refs_8_, bf16[64,6144]{1,0:T(8,128)(2,1)} %collective-permute-done.5.refs_3_.refs_11_, ...), custom_call_target="tpu_custom_call" | custom-call | tf_op jit(solution)/shard_map/pallas_call | solution.py:120
  59.0 1.5 constant_dynamic-slice_fusion.1
  60.5 1.4 bitcast_select_fusion
  61.9 4.7 %collective-permute-start.12 = (bf16[256,1536]{1,0:T(8,128)(2,1)}, bf16[256,1536]{1,0:T(8,128)(2,1)}, u32[]{:S(2)}, u32[]{:S(2)}) collective-permute-start(bf16[256,1536]{1,0:T(8,128)(2,1)} %get-tuple-element.32), channel_id=1, source_target_pairs={{0,8},{8,16},{16,24},{1,9},{9,17},{17,25},{2,10},{10,18},{18,26},{... | collective-permute-start | bytes 2359304 | tf_op jit(solution)/shard_map/ppermute | solution.py:247
  66.6 1.3 collective-permute-start.13
  69.4 19.0 %shard_map.78 = bf16[2,2,128,1536]{3,2,1,0:T(8,128)(2,1)} custom-call(s32[5]{0:T(128)} %get-tuple-element.28.first_ref, bf16[128,6144]{1,0:T(8,128)(2,1)} %copy-done.1, bf16[128,6144]{1,0:T(8,128)(2,1)} %copy-done.3, bf16[64,6144]{1,0:T(8,128)(2,1)} %copy-done.6, bf16[64,6144]{1,0:T(8,128)(2,1)} %copy-done.7, bf16[6144,6144]{1,0:T(8,128)(2,1)} %refs_4_.3), custom_call_target="tpu_custom_call" | custom-call | tf_op jit(solution)/shard_map/pallas_call | solution.py:120
  88.4 1.5 collective-permute-start.19
  89.9 1.5 dynamic-slice_select_fusion.3
  91.5 2.6 %fusion.7 = bf16[256,1536]{1,0:T(8,128)(2,1)} fusion(bf16[256,1536]{1,0:T(8,128)(2,1)} %collective-permute-done.13.refs_4_, bf16[1,2,128,1536]{3,2,1,0:T(8,128)(2,1)S(1)} %get-tuple-element.47, pred[]{:T(512)S(6)} %lt.294), kind=kLoop, calls=%fused_computation.13 | loop fusion | flops 1966080 | bytes 2359297 | tf_op jit(solution)/shard_map/jit(_where)/select_n | solution.py:244
  94.1 1.3 collective-permute-start.15
  95.3 2.7 %fusion.6 = bf16[256,1536]{1,0:T(8,128)(2,1)} fusion(bf16[256,1536]{1,0:T(8,128)(2,1)} %collective-permute-done.12.refs_3_, bf16[1,2,128,1536]{3,2,1,0:T(8,128)(2,1)S(1)} %get-tuple-element.46, pred[]{:T(512)S(6)} %ge.15), kind=kLoop, calls=%fused_computation.12 | loop fusion | flops 1966080 | bytes 2359297 | tf_op jit(solution)/shard_map/jit(_where)/select_n | solution.py:243
  98.0 6.1 %collective-permute-start.14 = (bf16[256,1536]{1,0:T(8,128)(2,1)}, bf16[256,1536]{1,0:T(8,128)(2,1)}, u32[]{:S(2)}, u32[]{:S(2)}) collective-permute-start(bf16[256,1536]{1,0:T(8,128)(2,1)} %fusion.6), channel_id=1, source_target_pairs={{0,8},{8,16},{16,24},{1,9},{9,17},{17,25},{2,10},{10,18},{18,26},{... | collective-permute-start | bytes 2359304 | tf_op jit(solution)/shard_map/ppermute | solution.py:247
  107.4 7.8 %collective-permute-done.15.refs_6_ = bf16[256,1536]{1,0:T(8,128)(2,1)} collective-permute-done((bf16[256,1536]{1,0:T(8,128)(2,1)}, bf16[256,1536]{1,0:T(8,128)(2,1)}, u32[]{:S(2)}, u32[]{:S(2)}) %collective-permute-start.15) | collective-permute-done | bytes 786464 | tf_op jit(solution)/shard_map/ppermute | solution.py:248
  115.2 3.9 %collective-permute-done.14.refs_5_ = bf16[256,1536]{1,0:T(8,128)(2,1)} collective-permute-done((bf16[256,1536]{1,0:T(8,128)(2,1)}, bf16[256,1536]{1,0:T(8,128)(2,1)}, u32[]{:S(2)}, u32[]{:S(2)}) %collective-permute-start.14) | collective-permute-done | bytes 786464 | tf_op jit(solution)/shard_map/ppermute | solution.py:247
  119.2 1.3 fusion
  120.6 1.3 collective-permute-start.23
  121.9 1.3 fusion.1
  123.2 5.4 %collective-permute-start.16 = (bf16[256,1536]{1,0:T(8,128)(2,1)S(1)}, bf16[256,1536]{1,0:T(8,128)(2,1)S(1)}, u32[]{:S(2)}, u32[]{:S(2)}) collective-permute-start(bf16[256,1536]{1,0:T(8,128)(2,1)S(1)} %fusion.1), channel_id=1, source_target_pairs={{0,8},{8,16},{16,24},{1,9},{9,17},{17,25},{2,10},{10,18},{18,26},{... | collective-permute-start | bytes 2359304 | tf_op jit(solution)/shard_map/ppermute | solution.py:247
  128.6 28.1 %shard_map.79 = f32[1536,6144]{1,0:T(8,128)} custom-call(s32[28]{0:T(128)} %stack.102.place_ref, bf16[256,1536]{1,0:T(8,128)(2,1)} %pad_maximum_fusion.refs_0_, bf16[256,1536]{1,0:T(8,128)(2,1)} %collective-permute-done.6.refs_1_, bf16[256,1536]{1,0:T(8,128)(2,1)} %copy-done.8, bf16[256,1536]{1,0:T(8,128)(2,1)} %collective-permute-done.12.refs_3_, ...), custom_call_target="tpu_custom_call" | custom-call | flops 19327352832 | bytes 53477376 | tf_op jit(solution)/shard_map/pallas_call | solution.py:78
  157.3 1.7 %collective-permute-done.24 = bf16[2,64,1536]{2,1,0:T(8,128)(2,1)S(1)} collective-permute-done((bf16[2,64,1536]{2,1,0:T(8,128)(2,1)S(1)}, bf16[2,64,1536]{2,1,0:T(8,128)(2,1)S(1)}, u32[]{:S(2)}, u32[]{:S(2)}) %collective-permute-start.24) | collective-permute-done | bytes 393248 | tf_op jit(solution)/shard_map/ppermute | solution.py:155
  (77 shorter events, 12.1 us)
Async XLA Ops:
  2.9 1.9 %collective-permute-start = (bf16[64,1536]{1,0:T(8,128)(2,1)}, bf16[64,1536]{1,0:T(8,128)(2,1)}, u32[]{:S(2)}, u32[]{:S(2)}) collective-permute-start(bf16[64,1536]{1,0:T(8,128)(2,1)} %get-tuple-element.57), channel_id=1, source_target_pairs={{0,1},{1,0},{2,3},{3,2},{4,5},{5,4},{6,7},{7,6},{8,9},{9,8},{10,11... | collective-permute-start | bytes 589832 | tf_op jit(solution)/shard_map/ppermute | solution.py:155
  4.7 22.6 %collective-permute-start.3 = (bf16[128,6144]{1,0:T(8,128)(2,1)S(1)}, bf16[128,6144]{1,0:T(8,128)(2,1)S(1)}, u32[]{:S(2)}, u32[]{:S(2)}) collective-permute-start(bf16[128,6144]{1,0:T(8,128)(2,1)S(1)} %multiply_convert_fusion.refs_0_.refs_7_), channel_id=1, source_target_pairs={{0,1},{1,0},{2,3},{3,2},{4,5},{5,4},{6,7},{7,6},{8,9},{9,8},{10,11... | collective-permute-start | bytes 4718600 | tf_op jit(solution)/shard_map/ppermute | solution.py:155
  5.1 3.9 %copy-start.10 = (bf16[64,1536]{1,0:T(8,128)(2,1)S(1)}, bf16[64,1536]{1,0:T(8,128)(2,1)}, u32[]{:S(2)}) copy-start(bf16[64,1536]{1,0:T(8,128)(2,1)} %get-tuple-element.58) | copy-start | bytes 589828
  6.4 21.0 %collective-permute-start.4 = (bf16[64,6144]{1,0:T(8,128)(2,1)}, bf16[64,6144]{1,0:T(8,128)(2,1)}, u32[]{:S(2)}, u32[]{:S(2)}) collective-permute-start(bf16[64,6144]{1,0:T(8,128)(2,1)} %get-tuple-element.26), channel_id=1, source_target_pairs={{0,4},{4,0},{1,5},{5,1},{2,6},{6,2},{3,7},{7,3},{8,12},{12,8},{9,1... | collective-permute-start | bytes 2359304 | tf_op jit(solution)/shard_map/ppermute | solution.py:158
  9.0 6.9 %collective-permute-start.2 = (bf16[64,1536]{1,0:T(8,128)(2,1)S(1)}, bf16[64,1536]{1,0:T(8,128)(2,1)S(1)}, u32[]{:S(2)}, u32[]{:S(2)}) collective-permute-start(bf16[64,1536]{1,0:T(8,128)(2,1)S(1)} %copy-done.10), channel_id=1, source_target_pairs={{0,3},{1,2},{2,1},{3,0},{4,7},{5,6},{6,5},{7,4},{8,11},{9,10},{10,... | collective-permute-start | bytes 589832 | tf_op jit(solution)/shard_map/ppermute | solution.py:155
  10.2 10.2 %collective-permute-start.1 = (bf16[64,1536]{1,0:T(8,128)(2,1)S(1)}, bf16[64,1536]{1,0:T(8,128)(2,1)S(1)}, u32[]{:S(2)}, u32[]{:S(2)}) collective-permute-start(bf16[64,1536]{1,0:T(8,128)(2,1)S(1)} %get-tuple-element.59), channel_id=1, source_target_pairs={{0,2},{1,3},{2,0},{3,1},{4,6},{5,7},{6,4},{7,5},{8,10},{9,11},{10,... | collective-permute-start | bytes 589832 | tf_op jit(solution)/shard_map/ppermute | solution.py:155
  27.4 10.7 %collective-permute-start.5 = (bf16[64,6144]{1,0:T(8,128)(2,1)}, bf16[64,6144]{1,0:T(8,128)(2,1)}, u32[]{:S(2)}, u32[]{:S(2)}) collective-permute-start(bf16[64,6144]{1,0:T(8,128)(2,1)} %collective-permute-done.4.refs_2_.refs_8_), channel_id=1, source_target_pairs={{0,1},{1,0},{2,3},{3,2},{4,5},{5,4},{6,7},{7,6},{8,9},{9,8},{10,11... | collective-permute-start | bytes 2359304 | tf_op jit(solution)/shard_map/ppermute | solution.py:155
  27.4 10.7 %copy-start.3 = (bf16[128,6144]{1,0:T(8,128)(2,1)}, bf16[128,6144]{1,0:T(8,128)(2,1)S(1)}, u32[]{:S(2)}) copy-start(bf16[128,6144]{1,0:T(8,128)(2,1)S(1)} %collective-permute-done.3.refs_1_.refs_10_) | copy-start | bytes 4718596
  27.4 29.6 %collective-permute-start.8 = (bf16[64,6144]{1,0:T(8,128)(2,1)}, bf16[64,6144]{1,0:T(8,128)(2,1)}, u32[]{:S(2)}, u32[]{:S(2)}) collective-permute-start(bf16[64,6144]{1,0:T(8,128)(2,1)} %get-tuple-element.26), channel_id=1, source_target_pairs={{0,2},{1,3},{2,0},{3,1},{4,6},{5,7},{6,4},{7,5},{8,10},{9,11},{10,... | collective-permute-start | bytes 2359304 | tf_op jit(solution)/shard_map/ppermute | solution.py:155
  29.2 27.8 %collective-permute-start.7 = (bf16[256,1536]{1,0:T(8,128)(2,1)}, bf16[256,1536]{1,0:T(8,128)(2,1)S(1)}, u32[]{:S(2)}, u32[]{:S(2)}) collective-permute-start(bf16[256,1536]{1,0:T(8,128)(2,1)} %pad_maximum_fusion.refs_0_), channel_id=1, source_target_pairs={{8,0},{16,8},{24,16},{9,1},{17,9},{25,17},{10,2},{18,10},{26,18},{... | collective-permute-start | bytes 2359304 | tf_op jit(solution)/shard_map/ppermute | solution.py:248
  30.5 26.5 %collective-permute-start.6 = (bf16[256,1536]{1,0:T(8,128)(2,1)}, bf16[256,1536]{1,0:T(8,128)(2,1)}, u32[]{:S(2)}, u32[]{:S(2)}) collective-permute-start(bf16[256,1536]{1,0:T(8,128)(2,1)} %pad_maximum_fusion.refs_0_), channel_id=1, source_target_pairs={{0,8},{8,16},{16,24},{1,9},{9,17},{17,25},{2,10},{10,18},{18,26},{... | collective-permute-start | bytes 2359304 | tf_op jit(solution)/shard_map/ppermute | solution.py:247
  36.0 21.1 %collective-permute-start.10 = (bf16[64,6144]{1,0:T(8,128)(2,1)}, bf16[64,6144]{1,0:T(8,128)(2,1)S(1)}, u32[]{:S(2)}, u32[]{:S(2)}) collective-permute-start(bf16[64,6144]{1,0:T(8,128)(2,1)} %get-tuple-element.39), channel_id=1, source_target_pairs={{0,4},{4,0},{1,5},{5,1},{2,6},{6,2},{3,7},{7,3},{8,12},{12,8},{9,1... | collective-permute-start | bytes 2359304 | tf_op jit(solution)/shard_map/ppermute | solution.py:158
  58.0 11.5 %copy-start.6 = (bf16[64,6144]{1,0:T(8,128)(2,1)}, bf16[64,6144]{1,0:T(8,128)(2,1)S(1)}, u32[]{:S(2)}) copy-start(bf16[64,6144]{1,0:T(8,128)(2,1)S(1)} %collective-permute-done.10.refs_2_.refs_9_) | copy-start | bytes 2359300
  58.0 10.6 %collective-permute-start.9 = (bf16[64,6144]{1,0:T(8,128)(2,1)}, bf16[64,6144]{1,0:T(8,128)(2,1)S(1)}, u32[]{:S(2)}, u32[]{:S(2)}) collective-permute-start(bf16[64,6144]{1,0:T(8,128)(2,1)} %collective-permute-done.8.refs_13_), channel_id=1, source_target_pairs={{0,1},{1,0},{2,3},{3,2},{4,5},{5,4},{6,7},{7,6},{8,9},{9,8},{10,11... | collective-permute-start | bytes 2359304 | tf_op jit(solution)/shard_map/ppermute | solution.py:155
  58.0 3.9 %collective-permute-start.11 = (bf16[64,6144]{1,0:T(8,128)(2,1)S(1)}, bf16[64,6144]{1,0:T(8,128)(2,1)S(1)}, u32[]{:S(2)}, u32[]{:S(2)}) collective-permute-start(bf16[64,6144]{1,0:T(8,128)(2,1)S(1)} %collective-permute-done.10.refs_2_.refs_9_), channel_id=1, source_target_pairs={{0,1},{1,0},{2,3},{3,2},{4,5},{5,4},{6,7},{7,6},{8,9},{9,8},{10,11... | collective-permute-start | bytes 2359304 | tf_op jit(solution)/shard_map/ppermute | solution.py:155
  58.5 29.9 %collective-permute-start.17 = (bf16[64,6144]{1,0:T(8,128)(2,1)}, bf16[64,6144]{1,0:T(8,128)(2,1)}, u32[]{:S(2)}, u32[]{:S(2)}) collective-permute-start(bf16[64,6144]{1,0:T(8,128)(2,1)} %get-tuple-element.39), channel_id=1, source_target_pairs={{0,2},{1,3},{2,0},{3,1},{4,6},{5,7},{6,4},{7,5},{8,10},{9,11},{10,... | collective-permute-start | bytes 2359304 | tf_op jit(solution)/shard_map/ppermute | solution.py:155
  61.9 7.5 %copy-start.7 = (bf16[64,6144]{1,0:T(8,128)(2,1)}, bf16[64,6144]{1,0:T(8,128)(2,1)S(1)}, u32[]{:S(2)}) copy-start(bf16[64,6144]{1,0:T(8,128)(2,1)S(1)} %collective-permute-done.11.refs_3_.refs_12_) | copy-start | bytes 2359300
  61.9 28.0 %collective-permute-start.12 = (bf16[256,1536]{1,0:T(8,128)(2,1)}, bf16[256,1536]{1,0:T(8,128)(2,1)}, u32[]{:S(2)}, u32[]{:S(2)}) collective-permute-start(bf16[256,1536]{1,0:T(8,128)(2,1)} %get-tuple-element.32), channel_id=1, source_target_pairs={{0,8},{8,16},{16,24},{1,9},{9,17},{17,25},{2,10},{10,18},{18,26},{... | collective-permute-start | bytes 2359304 | tf_op jit(solution)/shard_map/ppermute | solution.py:247
  66.6 23.4 %collective-permute-start.13 = (bf16[256,1536]{1,0:T(8,128)(2,1)}, bf16[256,1536]{1,0:T(8,128)(2,1)}, u32[]{:S(2)}, u32[]{:S(2)}) collective-permute-start(bf16[256,1536]{1,0:T(8,128)(2,1)} %get-tuple-element.33), channel_id=1, source_target_pairs={{8,0},{16,8},{24,16},{9,1},{17,9},{25,17},{10,2},{18,10},{26,18},{... | collective-permute-start | bytes 2359304 | tf_op jit(solution)/shard_map/ppermute | solution.py:248
  67.9 36.9 %collective-permute-start.18 = (bf16[64,6144]{1,0:T(8,128)(2,1)}, bf16[64,6144]{1,0:T(8,128)(2,1)}, u32[]{:S(2)}, u32[]{:S(2)}) collective-permute-start(bf16[64,6144]{1,0:T(8,128)(2,1)} %collective-permute-done.8.refs_13_), channel_id=1, source_target_pairs={{0,4},{4,0},{1,5},{5,1},{2,6},{6,2},{3,7},{7,3},{8,12},{12,8},{9,1... | collective-permute-start | bytes 2359304 | tf_op jit(solution)/shard_map/ppermute | solution.py:158
  69.4 20.5 %copy-start = (bf16[2,2,128,1536]{3,2,1,0:T(8,128)(2,1)S(1)}, bf16[2,2,128,1536]{3,2,1,0:T(8,128)(2,1)}, u32[]{:S(2)}) copy-start(bf16[2,2,128,1536]{3,2,1,0:T(8,128)(2,1)} %shard_map.77) | copy-start | bytes 4718596
  88.4 19.0 %collective-permute-start.19 = (bf16[64,6144]{1,0:T(8,128)(2,1)}, bf16[64,6144]{1,0:T(8,128)(2,1)}, u32[]{:S(2)}, u32[]{:S(2)}) collective-permute-start(bf16[64,6144]{1,0:T(8,128)(2,1)} %copy-done.6), channel_id=1, source_target_pairs={{0,2},{1,3},{2,0},{3,1},{4,6},{5,7},{6,4},{7,5},{8,10},{9,11},{10,... | collective-permute-start | bytes 2359304 | tf_op jit(solution)/shard_map/ppermute | solution.py:155
  94.1 21.2 %collective-permute-start.15 = (bf16[256,1536]{1,0:T(8,128)(2,1)}, bf16[256,1536]{1,0:T(8,128)(2,1)}, u32[]{:S(2)}, u32[]{:S(2)}) collective-permute-start(bf16[256,1536]{1,0:T(8,128)(2,1)} %fusion.7), channel_id=1, source_target_pairs={{8,0},{16,8},{24,16},{9,1},{17,9},{25,17},{10,2},{18,10},{26,18},{... | collective-permute-start | bytes 2359304 | tf_op jit(solution)/shard_map/ppermute | solution.py:248
  95.3 10.0 %copy-start.2 = (bf16[2,2,128,1536]{3,2,1,0:T(8,128)(2,1)S(1)}, bf16[2,2,128,1536]{3,2,1,0:T(8,128)(2,1)}, u32[]{:S(2)}) copy-start(bf16[2,2,128,1536]{3,2,1,0:T(8,128)(2,1)} %shard_map.78) | copy-start | bytes 4718596
  98.0 21.0 %collective-permute-start.14 = (bf16[256,1536]{1,0:T(8,128)(2,1)}, bf16[256,1536]{1,0:T(8,128)(2,1)}, u32[]{:S(2)}, u32[]{:S(2)}) collective-permute-start(bf16[256,1536]{1,0:T(8,128)(2,1)} %fusion.6), channel_id=1, source_target_pairs={{0,8},{8,16},{16,24},{1,9},{9,17},{17,25},{2,10},{10,18},{18,26},{... | collective-permute-start | bytes 2359304 | tf_op jit(solution)/shard_map/ppermute | solution.py:247
  104.8 23.8 %collective-permute-start.20 = (bf16[64,6144]{1,0:T(8,128)(2,1)}, bf16[64,6144]{1,0:T(8,128)(2,1)}, u32[]{:S(2)}, u32[]{:S(2)}) collective-permute-start(bf16[64,6144]{1,0:T(8,128)(2,1)} %collective-permute-done.17.refs_14_), channel_id=1, source_target_pairs={{0,1},{1,0},{2,3},{3,2},{4,5},{5,4},{6,7},{7,6},{8,9},{9,8},{10,11... | collective-permute-start | bytes 2359304 | tf_op jit(solution)/shard_map/ppermute | solution.py:155
  104.8 23.8 %collective-permute-start.21 = (bf16[64,6144]{1,0:T(8,128)(2,1)}, bf16[64,6144]{1,0:T(8,128)(2,1)}, u32[]{:S(2)}, u32[]{:S(2)}) collective-permute-start(bf16[64,6144]{1,0:T(8,128)(2,1)} %collective-permute-done.18.refs_15_), channel_id=1, source_target_pairs={{0,1},{1,0},{2,3},{3,2},{4,5},{5,4},{6,7},{7,6},{8,9},{9,8},{10,11... | collective-permute-start | bytes 2359304 | tf_op jit(solution)/shard_map/ppermute | solution.py:155
  107.4 21.2 %collective-permute-start.22 = (bf16[64,6144]{1,0:T(8,128)(2,1)}, bf16[64,6144]{1,0:T(8,128)(2,1)}, u32[]{:S(2)}, u32[]{:S(2)}) collective-permute-start(bf16[64,6144]{1,0:T(8,128)(2,1)} %collective-permute-done.19.refs_16_), channel_id=1, source_target_pairs={{0,1},{1,0},{2,3},{3,2},{4,5},{5,4},{6,7},{7,6},{8,9},{9,8},{10,11... | collective-permute-start | bytes 2359304 | tf_op jit(solution)/shard_map/ppermute | solution.py:155
  120.6 36.2 %collective-permute-start.23 = (bf16[256,1536]{1,0:T(8,128)(2,1)S(1)}, bf16[256,1536]{1,0:T(8,128)(2,1)S(1)}, u32[]{:S(2)}, u32[]{:S(2)}) collective-permute-start(bf16[256,1536]{1,0:T(8,128)(2,1)S(1)} %fusion), channel_id=1, source_target_pairs={{8,0},{16,8},{24,16},{9,1},{17,9},{25,17},{10,2},{18,10},{26,18},{... | collective-permute-start | bytes 2359304 | tf_op jit(solution)/shard_map/ppermute | solution.py:248
  123.2 33.6 %copy-start.4 = (bf16[1,2,128,1536]{3,2,1,0:T(8,128)(2,1)S(1)}, bf16[1,2,128,1536]{3,2,1,0:T(8,128)(2,1)}, u32[]{:S(2)}) copy-start(bf16[1,2,128,1536]{3,2,1,0:T(8,128)(2,1)} %dynamic-slice_select_fusion.4) | copy-start | bytes 2359300
  123.2 33.6 %collective-permute-start.16 = (bf16[256,1536]{1,0:T(8,128)(2,1)S(1)}, bf16[256,1536]{1,0:T(8,128)(2,1)S(1)}, u32[]{:S(2)}, u32[]{:S(2)}) collective-permute-start(bf16[256,1536]{1,0:T(8,128)(2,1)S(1)} %fusion.1), channel_id=1, source_target_pairs={{0,8},{8,16},{16,24},{1,9},{9,17},{17,25},{2,10},{10,18},{18,26},{... | collective-permute-start | bytes 2359304 | tf_op jit(solution)/shard_map/ppermute | solution.py:247
  157.2 1.8 %collective-permute-start.24 = (bf16[2,64,1536]{2,1,0:T(8,128)(2,1)S(1)}, bf16[2,64,1536]{2,1,0:T(8,128)(2,1)S(1)}, u32[]{:S(2)}, u32[]{:S(2)}) collective-permute-start(bf16[2,64,1536]{2,1,0:T(8,128)(2,1)S(1)} %get-tuple-element.54), channel_id=1, source_target_pairs={{0,1},{1,0},{2,3},{3,2},{4,5},{5,4},{6,7},{7,6},{8,9},{9,8},{10,11... | collective-permute-start | bytes 1179656 | tf_op jit(solution)/shard_map/ppermute | solution.py:155
  (8 other events, 17.8 us)

commit v3 on v2

--- a/solution.py
+++ b/solution.py
@@ -228,31 +228,37 @@
         def passes(targets):
             return sorted({slot(t // per_w, t % per_w) for t in targets})
 
-        right, left, sums = [x_own], [x_own], [None, None]
+        even = h % 2 == 0
+        pairs = [
+            [edge for j in range(first, n_h - 1, 2) for edge in ((j, j + 1), (j + 1, j))] for first in range(2)
+        ]
+        planes = [(h, h >= 0, x_own)]
+        came = [x_own, x_own]
 
         def step_planes(m, *late):
             step, apart = m - 1, n_h - m + 1
-            to_right, to_left = (right[-1], left[-1]) if m < n_h else (None, None)
-            if step:
-                choices = passes([j + apart for j in range(step)] + [j - apart for j in range(apart, n_h)])
-                come = tuple(sums)
-                up, down = share_of(h + apart, choices, come), share_of(h - apart, choices, come)
-                if step > 1:
-                    up = (up.astype(jnp.float32) + sums[0].astype(jnp.float32)).astype(jnp.bfloat16)
-                    down = (down.astype(jnp.float32) + sums[1].astype(jnp.float32)).astype(jnp.bfloat16)
-                to_right = up if to_right is None else jnp.where(h >= step, to_right, up)
-                to_left = down if to_left is None else jnp.where(h < apart, to_left, down)
-            if late:
-                to_right, to_left = after(to_right, *late), after(to_left, *late)
-            come_right = lax.ppermute(to_right, "hidden", [(j, j + 1) for j in range(n_h - 1)])
-            come_left = lax.ppermute(to_left, "hidden", [(j, j - 1) for j in range(1, n_h)])
-            if m < n_h:
-                right.append(come_right)
-                left.append(come_left)
-            sums[:] = [come_right, come_left]
+            choices = passes([j + apart for j in range(step)] + [j - apart for j in range(apart, n_h)]) if step else []
+            come, sent = tuple(came), []
+            for kind in range(2):
+                to_right = even if kind == 0 else ~even
+                value = come[1 - kind] if m < n_h else None
+                if step:
+                    total = share_of(jnp.where(to_right, h + apart, h - apart), choices, come)
+                    if step > 1:
+                        total = (total.astype(jnp.float32) + come[1 - kind].astype(jnp.float32)).astype(jnp.bfloat16)
+                    is_input = jnp.where(to_right, h >= step, h < apart)
+                    value = total if value is None else jnp.where(is_input, value, total)
+                sent.append(after(value, *late) if late else value)
+            for kind in range(2):
+                came[kind] = lax.ppermute(sent[kind], "hidden", pairs[kind])
+                from_right = even if kind == 0 else ~even
+                if m < n_h:
+                    plane = jnp.where(from_right, h + m, h - m)
+                    planes.append((plane, (plane >= 0) & (plane < n_h), came[kind]))
 
         send_x(0)
         step_planes(1)
+        came_in = [None, tuple(came)]
         send_y(0, *parts, *whole[1:])
         for dx in range(1, n_w):
             cores[0, dx, 0] = spread(piece[0, dx, 0])
@@ -264,7 +270,7 @@
                     tokens.append((cores[0, dx, q][dc], w * 0) if dx else (whole[dc], slot_of(w, q)))
             due = late + tuple(parts)
             if q:
-                due = late + (right[q], left[q]) + tuple(cores[dy, 0, q - 1][-1] for dy in range(1, n_y))
+                due = late + tuple(came_in[q]) + tuple(cores[dy, 0, q - 1][-1] for dy in range(1, n_y))
             if q + 1 < per_w:
                 send_x(q + 1, *over_x(q), *whole[1:])
             share = input_grad(c, n_c, rows, tokens, weight, n_w, n_y, due)
@@ -275,6 +281,7 @@
                 for dx in range(1, n_w):
                     cores[0, dx, q + 1] = spread(piece[0, dx, q + 1], share)
                 step_planes(q + 2, *(cores[0, dx, q + 1][-1] for dx in range(1, n_w)))
+                came_in.append(tuple(came))
                 send_y(q + 1, share, *over_y(q))
                 send_on(q, *over_x(q + 1))
         for q in range(per_w - 1, per_w):
@@ -285,23 +292,18 @@
                     cores[dy, dx, q] = spread(piece[dy, dx, q])
         for m in range(per_w + 1, n_h):
             step_planes(m)
-        due = tuple(sums)
+        due = tuple(came)
         step_planes(n_h)
 
         places, pieces = [], []
-        for k in range(n_h):
-            if right[k] is left[k]:
-                sides = [(jnp.where(h >= k, h - k, h + k), right[k], (h >= k) | (h + k < n_h))]
-            else:
-                sides = [(h - k, right[k], h >= k), (h + k, left[k], h + k < n_h)]
-            for plane, planes_x, there in sides:
-                owner, group = plane // per_w, plane % per_w
-                dx = (w - owner) % n_w
-                for dy in range(n_y):
-                    sent_order = slot_of(owner, group) if dy else jnp.where(dx == 0, group, slot_of(owner, group))
-                    place = jnp.where(there, dx * per_w + sent_order, -1).astype(jnp.int32)
-                    places += [place] * n_c
-                pieces.append(planes_x)
+        for plane, there, values in planes:
+            owner, group = plane // per_w, plane % per_w
+            dx = (w - owner) % n_w
+            for dy in range(n_y):
+                sent_order = slot_of(owner, group) if dy else jnp.where(dx == 0, group, slot_of(owner, group))
+                place = jnp.where(there, dx * per_w + sent_order, -1).astype(jnp.int32)
+                places += [place] * n_c
+            pieces.append(values)
         s_pieces = []
         for dy in range(n_y):
             for dc in range(n_c):
@@ -312,9 +314,9 @@
                         s_pieces += [cores[dy, dx, q][dc] for q in range(per_w)]
         places = jnp.stack(places)
         grad_weight = weight_grad(places, pieces, s_pieces, n_h, rows, due)
-        from_left, from_right = after(sums[0], grad_weight), sums[1]
+        came[0] = after(came[0], grad_weight)
         total = share_of(h, range(per_w)).astype(jnp.float32)
-        total = total + from_left.astype(jnp.float32) + from_right.astype(jnp.float32)
+        total = total + came[0].astype(jnp.float32) + came[1].astype(jnp.float32)
         total = total.astype(jnp.bfloat16).reshape(n_y, n_c, rows, d_own)
         held = [total[:, 0]] + [over_replica(total[:, dc], 0, n_c - dc) for dc in range(1, n_c)]
         held = jnp.stack(held)

time: 161 us -> 154 us (0.957)
  starting transfers between devices: 38.9 us -> 32.4 us
  waiting for transfers between devices: 30.2 us -> 28.3 us
    ppermute x8, starting transfers between devices: 26.7 us -> 20.3 us  [step_planes(): came[kind] = lax.ppermute(sent[kind], 'hidden', pairs[kind])]
    ppermute x8, waiting for transfers between devices: 11.7 us -> 5.35 us  [step_planes(): came[kind] = lax.ppermute(sent[kind], 'hidden', pairs[kind])]
    ppermute x14, waiting for transfers between devices: 13.4 us -> 17.8 us  [over_replica(): return lax.ppermute(value, 'replica', replica_perm(dy, dc))]
  transfers between devices with their start and end apart: 25 -> 25, of which waited for: 8 -> 7; matrix products, arithmetic and copies ran while one was open for 11% -> 13% of each run, Pallas kernels for 41% -> 43%
where the time goes in v3:
time: 154 us; the launch traced here: 153 us
  Pallas kernels  66 us (43%)
  starting transfers between devices  32.4 us (21%)
  waiting for transfers between devices  28.3 us (18%)
  other arithmetic  17.6 us (11%)
  local copies, waits for them, and re-layouts  7.5 us (5%)
    pallas_call x2, Pallas kernels, input_grad(): pl.pallas_call(input_grad_kernel, grid_spec=pltpu.PrefetchScalarGridSpec(...  37.8 us
    pallas_call x1, Pallas kernels, weight_grad(): pl.pallas_call(body, grid_spec=pltpu.PrefetchScalarGridSpec(num_scalar_pr...  28.1 us
    ppermute x8, starting transfers between devices, step_planes(): came[kind] = lax.ppermute(sent[kind], 'hidden', pairs[kind])  20.3 us
    ppermute x14, waiting for transfers between devices, over_replica(): return lax.ppermute(value, 'replica', replica_perm(dy, dc))  17.8 us
    select_n x3, other arithmetic, step_planes(): value = total if value is None else jnp.where(is_input, value, total)  7.74 us
    ppermute x14, starting transfers between devices, over_replica(): return lax.ppermute(value, 'replica', replica_perm(dy, dc))  7.49 us
    ppermute x8, waiting for transfers between devices, step_planes(): came[kind] = lax.ppermute(sent[kind], 'hidden', pairs[kind])  5.35 us
    ppermute x3, waiting for transfers between devices, over_width(): lax.ppermute(value, 'width', [(w, (w + dx) % n_w) for w in range(n_w)])  5.11 us
  transfers between devices with their start and end apart: 25, of which 7 were waited for; matrix products, arithmetic and copies ran while one was open for 13% of the time, Pallas kernels for 43%

profile of v3, /device:TPU:0, one launch (start us, length us, event | category | flops | bytes accessed | tf_op | source)
XLA Modules:
  0.0 152.8 jit_solution(1431970257123293527)
XLA Ops:
  0.8 2.1 %constant_dynamic-slice_fusion.8 = (bf16[64,1536]{1,0:T(8,128)(2,1)S(1)}, bf16[64,1536]{1,0:T(8,128)(2,1)}, bf16[64,1536]{1,0:T(8,128)(2,1)}, bf16[64,1536]{1,0:T(8,128)(2,1)S(1)}) fusion(bf16[64,6144]{1,0:T(8,128)(2,1)} %param.6, s32[]{:T(128)S(6)} %select_n.483, s32[]{:T(128)S(6)} %select_n.485, s32[]{:T(128)S(6)} %select_n.488, s32[]{:T(128)S(6)} %select_n.487), kind=kLoop, calls=%fused_computation.45 | loop fusion | bytes 1572880 | tf_op jit(solution)/shard_map/dynamic_slice | solution.py:173
  5.1 1.2 constant_dynamic-slice_fusion.2
  6.4 2.6 %collective-permute-start.4 = (bf16[64,6144]{1,0:T(8,128)(2,1)}, bf16[64,6144]{1,0:T(8,128)(2,1)}, u32[]{:S(2)}, u32[]{:S(2)}) collective-permute-start(bf16[64,6144]{1,0:T(8,128)(2,1)} %get-tuple-element.26), channel_id=1, source_target_pairs={{0,4},{4,0},{1,5},{5,1},{2,6},{6,2},{3,7},{7,3},{8,12},{12,8},{9,1... | collective-permute-start | bytes 2359304 | tf_op jit(solution)/shard_map/ppermute | solution.py:158
  9.0 1.2 collective-permute-start.2
  10.7 5.2 %collective-permute-done.2 = bf16[64,1536]{1,0:T(8,128)(2,1)S(1)} collective-permute-done((bf16[64,1536]{1,0:T(8,128)(2,1)S(1)}, bf16[64,1536]{1,0:T(8,128)(2,1)S(1)}, u32[]{:S(2)}, u32[]{:S(2)}) %collective-permute-start.2) | collective-permute-done | bytes 196640 | tf_op jit(solution)/shard_map/ppermute | solution.py:155
  16.0 4.5 %collective-permute-done.1 = bf16[64,1536]{1,0:T(8,128)(2,1)S(1)} collective-permute-done((bf16[64,1536]{1,0:T(8,128)(2,1)S(1)}, bf16[64,1536]{1,0:T(8,128)(2,1)S(1)}, u32[]{:S(2)}, u32[]{:S(2)}) %collective-permute-start.1) | collective-permute-done | bytes 196640 | tf_op jit(solution)/shard_map/ppermute | solution.py:155
  20.4 1.9 %pad_maximum_fusion.refs_0_ = bf16[256,1536]{1,0:T(8,128)(2,1)} fusion(bf16[64,1536]{1,0:T(8,128)(2,1)S(1)} %collective-permute-done.2, bf16[64,1536]{1,0:T(8,128)(2,1)S(1)} %collective-permute-done.1, bf16[64,1536]{1,0:T(8,128)(2,1)} %collective-permute-done, bf16[64,1536]{1,0:T(8,128)(2,1)S(1)} %get-tuple-element.56), kind=kLoop, calls=%fused_computation.18 | loop fusion | flops 3145728 | bytes 1572864 | tf_op jit(solution)/shard_map/concatenate | solution.py:175
  22.3 5.1 %collective-permute-done.4.refs_2_.refs_8_ = bf16[64,6144]{1,0:T(8,128)(2,1)} collective-permute-done((bf16[64,6144]{1,0:T(8,128)(2,1)}, bf16[64,6144]{1,0:T(8,128)(2,1)}, u32[]{:S(2)}, u32[]{:S(2)}) %collective-permute-start.4) | collective-permute-done | bytes 786464 | tf_op jit(solution)/shard_map/ppermute | solution.py:158
  27.4 1.8 %collective-permute-start.8 = (bf16[64,6144]{1,0:T(8,128)(2,1)}, bf16[64,6144]{1,0:T(8,128)(2,1)}, u32[]{:S(2)}, u32[]{:S(2)}) collective-permute-start(bf16[64,6144]{1,0:T(8,128)(2,1)} %get-tuple-element.26), channel_id=1, source_target_pairs={{0,2},{1,3},{2,0},{3,1},{4,6},{5,7},{6,4},{7,5},{8,10},{9,11},{10,... | collective-permute-start | bytes 2359304 | tf_op jit(solution)/shard_map/ppermute | solution.py:155
  29.9 4.4 %collective-permute-start.6 = (bf16[256,1536]{1,0:T(8,128)(2,1)}, bf16[256,1536]{1,0:T(8,128)(2,1)}, u32[]{:S(2)}, u32[]{:S(2)}) collective-permute-start(bf16[256,1536]{1,0:T(8,128)(2,1)} %pad_maximum_fusion.refs_0_), channel_id=1, source_target_pairs={{0,8},{8,0},{16,24},{24,16},{1,9},{9,1},{17,25},{25,17},{2,10},{10... | collective-permute-start | bytes 2359304 | tf_op jit(solution)/shard_map/ppermute | solution.py:253
  34.4 1.5 collective-permute-start.10
  36.5 18.9 %shard_map.77 = bf16[2,2,128,1536]{3,2,1,0:T(8,128)(2,1)} custom-call(s32[5]{0:T(128)} %get-tuple-element.23.first_ref, bf16[128,6144]{1,0:T(8,128)(2,1)} %copy-done.1, bf16[128,6144]{1,0:T(8,128)(2,1)} %copy-done.3, bf16[64,6144]{1,0:T(8,128)(2,1)} %collective-permute-done.4.refs_2_.refs_8_, bf16[64,6144]{1,0:T(8,128)(2,1)} %collective-permute-done.5.refs_3_.refs_11_, ...), custom_call_target="tpu_custom_call" | custom-call | tf_op jit(solution)/shard_map/pallas_call | solution.py:120
  55.4 0.9 copy-done.8
  57.4 1.5 constant_dynamic-slice_fusion
  58.9 2.5 %bitcast_select_fusion = (bf16[256,1536]{1,0:T(8,128)(2,1)}, bf16[256,1536]{1,0:T(8,128)(2,1)}) fusion(bf16[256,1536]{1,0:T(8,128)(2,1)S(1)} %copy-done.9, bf16[1,2,128,1536]{3,2,1,0:T(8,128)(2,1)S(1)} %get-tuple-element.48, pred[]{:T(512)S(6)} %select_n.516, bf16[256,1536]{1,0:T(8,128)(2,1)} %collective-permute-done.6.refs_1_, ...), kind=kLoop, calls=%fused_computation.20 | loop fusion | flops 786432 | bytes 4718594 | tf_op jit(solution)/shard_map/jit(_where)/select_n | solution.py:250
  61.4 1.6 %collective-permute-start.12 = (bf16[256,1536]{1,0:T(8,128)(2,1)}, bf16[256,1536]{1,0:T(8,128)(2,1)}, u32[]{:S(2)}, u32[]{:S(2)}) collective-permute-start(bf16[256,1536]{1,0:T(8,128)(2,1)} %get-tuple-element.32), channel_id=1, source_target_pairs={{8,16},{16,8},{9,17},{17,9},{10,18},{18,10},{11,19},{19,11},{12,20... | collective-permute-start | bytes 2359304 | tf_op jit(solution)/shard_map/ppermute | solution.py:253
  62.9 0.9 collective-permute-start.13
  65.3 19.0 %shard_map.78 = bf16[2,2,128,1536]{3,2,1,0:T(8,128)(2,1)} custom-call(s32[5]{0:T(128)} %get-tuple-element.28.first_ref, bf16[128,6144]{1,0:T(8,128)(2,1)} %copy-done.1, bf16[128,6144]{1,0:T(8,128)(2,1)} %copy-done.3, bf16[64,6144]{1,0:T(8,128)(2,1)} %copy-done.6, bf16[64,6144]{1,0:T(8,128)(2,1)} %copy-done.7, bf16[6144,6144]{1,0:T(8,128)(2,1)} %refs_4_.3), custom_call_target="tpu_custom_call" | custom-call | tf_op jit(solution)/shard_map/pallas_call | solution.py:120
  84.3 1.5 collective-permute-start.19
  85.8 1.5 %dynamic-slice_select_fusion.2 = (bf16[1,2,128,1536]{3,2,1,0:T(8,128)(2,1)S(1)}, bf16[1,2,128,1536]{3,2,1,0:T(8,128)(2,1)S(1)}) fusion(bf16[2,2,128,1536]{3,2,1,0:T(8,128)(2,1)S(1)} %copy-done, s32[]{:T(128)S(6)} %select_n.535, bf16[2,2,128,1536]{3,2,1,0:T(8,128)(2,1)} %shard_map.78, pred[]{:T(512)S(6)} %eq.98, s32[]{:T(128)S(6)} %select_n.524, pred[]{:T(512)S(6)} %eq.97), kind=kLoop, calls=%fused_computation.24 | loop fusion | flops 786432 | bytes 4718602 | tf_op jit(solution)/shard_map/jit(_where)/select_n | solution.py:225
  87.4 2.6 %fusion.6 = bf16[256,1536]{1,0:T(8,128)(2,1)} fusion(bf16[256,1536]{1,0:T(8,128)(2,1)} %collective-permute-done.12.refs_4_, bf16[1,2,128,1536]{3,2,1,0:T(8,128)(2,1)S(1)} %get-tuple-element.47, pred[]{:T(512)S(6)} %select_n.502), kind=kLoop, calls=%fused_computation.12 | loop fusion | flops 1966080 | bytes 2359297 | tf_op jit(solution)/shard_map/jit(_where)/select_n | solution.py:250
  89.9 1.1 collective-permute-start.14
  91.0 2.7 %fusion.7 = bf16[256,1536]{1,0:T(8,128)(2,1)} fusion(bf16[256,1536]{1,0:T(8,128)(2,1)} %collective-permute-done.13.refs_3_, bf16[1,2,128,1536]{3,2,1,0:T(8,128)(2,1)S(1)} %get-tuple-element.46, pred[]{:T(512)S(6)} %select_n.527), kind=kLoop, calls=%fused_computation.13 | loop fusion | flops 1966080 | bytes 2359297 | tf_op jit(solution)/shard_map/jit(_where)/select_n | solution.py:250
  93.7 1.6 %collective-permute-start.15 = (bf16[256,1536]{1,0:T(8,128)(2,1)}, bf16[256,1536]{1,0:T(8,128)(2,1)}, u32[]{:S(2)}, u32[]{:S(2)}) collective-permute-start(bf16[256,1536]{1,0:T(8,128)(2,1)} %fusion.7), channel_id=1, source_target_pairs={{8,16},{16,8},{9,17},{17,9},{10,18},{18,10},{11,19},{19,11},{12,20... | collective-permute-start | bytes 2359304 | tf_op jit(solution)/shard_map/ppermute | solution.py:253
  96.4 1.0 dynamic-slice_select_fusion.4
  97.4 5.5 %collective-permute-done.19.refs_16_ = bf16[64,6144]{1,0:T(8,128)(2,1)} collective-permute-done((bf16[64,6144]{1,0:T(8,128)(2,1)}, bf16[64,6144]{1,0:T(8,128)(2,1)}, u32[]{:S(2)}, u32[]{:S(2)}) %collective-permute-start.19) | collective-permute-done | bytes 786464 | tf_op jit(solution)/shard_map/ppermute | solution.py:155
  103.0 5.3 %collective-permute-done.14.refs_5_ = bf16[256,1536]{1,0:T(8,128)(2,1)} collective-permute-done((bf16[256,1536]{1,0:T(8,128)(2,1)}, bf16[256,1536]{1,0:T(8,128)(2,1)}, u32[]{:S(2)}, u32[]{:S(2)}) %collective-permute-start.14) | collective-permute-done | bytes 786464 | tf_op jit(solution)/shard_map/ppermute | solution.py:253
  108.5 1.3 fusion
  110.7 1.3 fusion.1
  112.0 9.1 %collective-permute-start.16 = (bf16[256,1536]{1,0:T(8,128)(2,1)S(1)}, bf16[256,1536]{1,0:T(8,128)(2,1)S(1)}, u32[]{:S(2)}, u32[]{:S(2)}) collective-permute-start(bf16[256,1536]{1,0:T(8,128)(2,1)S(1)} %fusion.1), channel_id=1, source_target_pairs={{0,8},{8,0},{16,24},{24,16},{1,9},{9,1},{17,25},{25,17},{2,10},{10... | collective-permute-start | bytes 2359304 | tf_op jit(solution)/shard_map/ppermute | solution.py:253
  121.2 28.1 %shard_map.79 = f32[1536,6144]{1,0:T(8,128)} custom-call(s32[28]{0:T(128)} %stack.102.place_ref, bf16[256,1536]{1,0:T(8,128)(2,1)} %pad_maximum_fusion.refs_0_, bf16[256,1536]{1,0:T(8,128)(2,1)} %collective-permute-done.6.refs_1_, bf16[256,1536]{1,0:T(8,128)(2,1)} %copy-done.8, bf16[256,1536]{1,0:T(8,128)(2,1)} %collective-permute-done.13.refs_3_, ...), custom_call_target="tpu_custom_call" | custom-call | flops 19327352832 | bytes 53477376 | tf_op jit(solution)/shard_map/pallas_call | solution.py:78
  149.9 1.7 %collective-permute-done.24 = bf16[2,64,1536]{2,1,0:T(8,128)(2,1)S(1)} collective-permute-done((bf16[2,64,1536]{2,1,0:T(8,128)(2,1)S(1)}, bf16[2,64,1536]{2,1,0:T(8,128)(2,1)S(1)}, u32[]{:S(2)}, u32[]{:S(2)}) %collective-permute-start.24) | collective-permute-done | bytes 393248 | tf_op jit(solution)/shard_map/ppermute | solution.py:155
  (77 shorter events, 10.6 us)
Async XLA Ops:
  2.9 1.9 %collective-permute-start = (bf16[64,1536]{1,0:T(8,128)(2,1)}, bf16[64,1536]{1,0:T(8,128)(2,1)}, u32[]{:S(2)}, u32[]{:S(2)}) collective-permute-start(bf16[64,1536]{1,0:T(8,128)(2,1)} %get-tuple-element.57), channel_id=1, source_target_pairs={{0,1},{1,0},{2,3},{3,2},{4,5},{5,4},{6,7},{7,6},{8,9},{9,8},{10,11... | collective-permute-start | bytes 589832 | tf_op jit(solution)/shard_map/ppermute | solution.py:155
  4.7 22.6 %collective-permute-start.3 = (bf16[128,6144]{1,0:T(8,128)(2,1)S(1)}, bf16[128,6144]{1,0:T(8,128)(2,1)S(1)}, u32[]{:S(2)}, u32[]{:S(2)}) collective-permute-start(bf16[128,6144]{1,0:T(8,128)(2,1)S(1)} %multiply_convert_fusion.refs_0_.refs_7_), channel_id=1, source_target_pairs={{0,1},{1,0},{2,3},{3,2},{4,5},{5,4},{6,7},{7,6},{8,9},{9,8},{10,11... | collective-permute-start | bytes 4718600 | tf_op jit(solution)/shard_map/ppermute | solution.py:155
  5.1 3.9 %copy-start.10 = (bf16[64,1536]{1,0:T(8,128)(2,1)S(1)}, bf16[64,1536]{1,0:T(8,128)(2,1)}, u32[]{:S(2)}) copy-start(bf16[64,1536]{1,0:T(8,128)(2,1)} %get-tuple-element.58) | copy-start | bytes 589828
  6.4 21.0 %collective-permute-start.4 = (bf16[64,6144]{1,0:T(8,128)(2,1)}, bf16[64,6144]{1,0:T(8,128)(2,1)}, u32[]{:S(2)}, u32[]{:S(2)}) collective-permute-start(bf16[64,6144]{1,0:T(8,128)(2,1)} %get-tuple-element.26), channel_id=1, source_target_pairs={{0,4},{4,0},{1,5},{5,1},{2,6},{6,2},{3,7},{7,3},{8,12},{12,8},{9,1... | collective-permute-start | bytes 2359304 | tf_op jit(solution)/shard_map/ppermute | solution.py:158
  9.0 6.9 %collective-permute-start.2 = (bf16[64,1536]{1,0:T(8,128)(2,1)S(1)}, bf16[64,1536]{1,0:T(8,128)(2,1)S(1)}, u32[]{:S(2)}, u32[]{:S(2)}) collective-permute-start(bf16[64,1536]{1,0:T(8,128)(2,1)S(1)} %copy-done.10), channel_id=1, source_target_pairs={{0,3},{1,2},{2,1},{3,0},{4,7},{5,6},{6,5},{7,4},{8,11},{9,10},{10,... | collective-permute-start | bytes 589832 | tf_op jit(solution)/shard_map/ppermute | solution.py:155
  10.2 10.2 %collective-permute-start.1 = (bf16[64,1536]{1,0:T(8,128)(2,1)S(1)}, bf16[64,1536]{1,0:T(8,128)(2,1)S(1)}, u32[]{:S(2)}, u32[]{:S(2)}) collective-permute-start(bf16[64,1536]{1,0:T(8,128)(2,1)S(1)} %get-tuple-element.59), channel_id=1, source_target_pairs={{0,2},{1,3},{2,0},{3,1},{4,6},{5,7},{6,4},{7,5},{8,10},{9,11},{10,... | collective-permute-start | bytes 589832 | tf_op jit(solution)/shard_map/ppermute | solution.py:155
  27.4 9.1 %collective-permute-start.5 = (bf16[64,6144]{1,0:T(8,128)(2,1)}, bf16[64,6144]{1,0:T(8,128)(2,1)}, u32[]{:S(2)}, u32[]{:S(2)}) collective-permute-start(bf16[64,6144]{1,0:T(8,128)(2,1)} %collective-permute-done.4.refs_2_.refs_8_), channel_id=1, source_target_pairs={{0,1},{1,0},{2,3},{3,2},{4,5},{5,4},{6,7},{7,6},{8,9},{9,8},{10,11... | collective-permute-start | bytes 2359304 | tf_op jit(solution)/shard_map/ppermute | solution.py:155
  27.4 9.1 %copy-start.3 = (bf16[128,6144]{1,0:T(8,128)(2,1)}, bf16[128,6144]{1,0:T(8,128)(2,1)S(1)}, u32[]{:S(2)}) copy-start(bf16[128,6144]{1,0:T(8,128)(2,1)S(1)} %collective-permute-done.3.refs_1_.refs_10_) | copy-start | bytes 4718596
  27.4 28.0 %collective-permute-start.8 = (bf16[64,6144]{1,0:T(8,128)(2,1)}, bf16[64,6144]{1,0:T(8,128)(2,1)}, u32[]{:S(2)}, u32[]{:S(2)}) collective-permute-start(bf16[64,6144]{1,0:T(8,128)(2,1)} %get-tuple-element.26), channel_id=1, source_target_pairs={{0,2},{1,3},{2,0},{3,1},{4,6},{5,7},{6,4},{7,5},{8,10},{9,11},{10,... | collective-permute-start | bytes 2359304 | tf_op jit(solution)/shard_map/ppermute | solution.py:155
  29.2 26.2 %collective-permute-start.7 = (bf16[256,1536]{1,0:T(8,128)(2,1)}, bf16[256,1536]{1,0:T(8,128)(2,1)S(1)}, u32[]{:S(2)}, u32[]{:S(2)}) collective-permute-start(bf16[256,1536]{1,0:T(8,128)(2,1)} %pad_maximum_fusion.refs_0_), channel_id=1, source_target_pairs={{8,16},{16,8},{9,17},{17,9},{10,18},{18,10},{11,19},{19,11},{12,20... | collective-permute-start | bytes 2359304 | tf_op jit(solution)/shard_map/ppermute | solution.py:253
  29.9 25.5 %collective-permute-start.6 = (bf16[256,1536]{1,0:T(8,128)(2,1)}, bf16[256,1536]{1,0:T(8,128)(2,1)}, u32[]{:S(2)}, u32[]{:S(2)}) collective-permute-start(bf16[256,1536]{1,0:T(8,128)(2,1)} %pad_maximum_fusion.refs_0_), channel_id=1, source_target_pairs={{0,8},{8,0},{16,24},{24,16},{1,9},{9,1},{17,25},{25,17},{2,10},{10... | collective-permute-start | bytes 2359304 | tf_op jit(solution)/shard_map/ppermute | solution.py:253
  34.4 21.1 %collective-permute-start.10 = (bf16[64,6144]{1,0:T(8,128)(2,1)}, bf16[64,6144]{1,0:T(8,128)(2,1)S(1)}, u32[]{:S(2)}, u32[]{:S(2)}) collective-permute-start(bf16[64,6144]{1,0:T(8,128)(2,1)} %get-tuple-element.39), channel_id=1, source_target_pairs={{0,4},{4,0},{1,5},{5,1},{2,6},{6,2},{3,7},{7,3},{8,12},{12,8},{9,1... | collective-permute-start | bytes 2359304 | tf_op jit(solution)/shard_map/ppermute | solution.py:158
  56.4 8.9 %copy-start.6 = (bf16[64,6144]{1,0:T(8,128)(2,1)}, bf16[64,6144]{1,0:T(8,128)(2,1)S(1)}, u32[]{:S(2)}) copy-start(bf16[64,6144]{1,0:T(8,128)(2,1)S(1)} %collective-permute-done.10.refs_2_.refs_9_) | copy-start | bytes 2359300
  56.4 8.0 %collective-permute-start.9 = (bf16[64,6144]{1,0:T(8,128)(2,1)}, bf16[64,6144]{1,0:T(8,128)(2,1)S(1)}, u32[]{:S(2)}, u32[]{:S(2)}) collective-permute-start(bf16[64,6144]{1,0:T(8,128)(2,1)} %collective-permute-done.8.refs_13_), channel_id=1, source_target_pairs={{0,1},{1,0},{2,3},{3,2},{4,5},{5,4},{6,7},{7,6},{8,9},{9,8},{10,11... | collective-permute-start | bytes 2359304 | tf_op jit(solution)/shard_map/ppermute | solution.py:155
  56.4 5.0 %collective-permute-start.11 = (bf16[64,6144]{1,0:T(8,128)(2,1)S(1)}, bf16[64,6144]{1,0:T(8,128)(2,1)S(1)}, u32[]{:S(2)}, u32[]{:S(2)}) collective-permute-start(bf16[64,6144]{1,0:T(8,128)(2,1)S(1)} %collective-permute-done.10.refs_2_.refs_9_), channel_id=1, source_target_pairs={{0,1},{1,0},{2,3},{3,2},{4,5},{5,4},{6,7},{7,6},{8,9},{9,8},{10,11... | collective-permute-start | bytes 2359304 | tf_op jit(solution)/shard_map/ppermute | solution.py:155
  56.9 27.4 %collective-permute-start.17 = (bf16[64,6144]{1,0:T(8,128)(2,1)}, bf16[64,6144]{1,0:T(8,128)(2,1)}, u32[]{:S(2)}, u32[]{:S(2)}) collective-permute-start(bf16[64,6144]{1,0:T(8,128)(2,1)} %get-tuple-element.39), channel_id=1, source_target_pairs={{0,2},{1,3},{2,0},{3,1},{4,6},{5,7},{6,4},{7,5},{8,10},{9,11},{10,... | collective-permute-start | bytes 2359304 | tf_op jit(solution)/shard_map/ppermute | solution.py:155
  61.4 3.9 %copy-start.7 = (bf16[64,6144]{1,0:T(8,128)(2,1)}, bf16[64,6144]{1,0:T(8,128)(2,1)S(1)}, u32[]{:S(2)}) copy-start(bf16[64,6144]{1,0:T(8,128)(2,1)S(1)} %collective-permute-done.11.refs_3_.refs_12_) | copy-start | bytes 2359300
  61.4 24.4 %collective-permute-start.12 = (bf16[256,1536]{1,0:T(8,128)(2,1)}, bf16[256,1536]{1,0:T(8,128)(2,1)}, u32[]{:S(2)}, u32[]{:S(2)}) collective-permute-start(bf16[256,1536]{1,0:T(8,128)(2,1)} %get-tuple-element.32), channel_id=1, source_target_pairs={{8,16},{16,8},{9,17},{17,9},{10,18},{18,10},{11,19},{19,11},{12,20... | collective-permute-start | bytes 2359304 | tf_op jit(solution)/shard_map/ppermute | solution.py:253
  62.9 22.9 %collective-permute-start.13 = (bf16[256,1536]{1,0:T(8,128)(2,1)}, bf16[256,1536]{1,0:T(8,128)(2,1)}, u32[]{:S(2)}, u32[]{:S(2)}) collective-permute-start(bf16[256,1536]{1,0:T(8,128)(2,1)} %get-tuple-element.33), channel_id=1, source_target_pairs={{0,8},{8,0},{16,24},{24,16},{1,9},{9,1},{17,25},{25,17},{2,10},{10... | collective-permute-start | bytes 2359304 | tf_op jit(solution)/shard_map/ppermute | solution.py:253
  63.9 32.1 %collective-permute-start.18 = (bf16[64,6144]{1,0:T(8,128)(2,1)}, bf16[64,6144]{1,0:T(8,128)(2,1)}, u32[]{:S(2)}, u32[]{:S(2)}) collective-permute-start(bf16[64,6144]{1,0:T(8,128)(2,1)} %collective-permute-done.8.refs_13_), channel_id=1, source_target_pairs={{0,4},{4,0},{1,5},{5,1},{2,6},{6,2},{3,7},{7,3},{8,12},{12,8},{9,1... | collective-permute-start | bytes 2359304 | tf_op jit(solution)/shard_map/ppermute | solution.py:158
  65.3 20.5 %copy-start = (bf16[2,2,128,1536]{3,2,1,0:T(8,128)(2,1)S(1)}, bf16[2,2,128,1536]{3,2,1,0:T(8,128)(2,1)}, u32[]{:S(2)}) copy-start(bf16[2,2,128,1536]{3,2,1,0:T(8,128)(2,1)} %shard_map.77) | copy-start | bytes 4718596
  84.3 18.7 %collective-permute-start.19 = (bf16[64,6144]{1,0:T(8,128)(2,1)}, bf16[64,6144]{1,0:T(8,128)(2,1)}, u32[]{:S(2)}, u32[]{:S(2)}) collective-permute-start(bf16[64,6144]{1,0:T(8,128)(2,1)} %copy-done.6), channel_id=1, source_target_pairs={{0,2},{1,3},{2,0},{3,1},{4,6},{5,7},{6,4},{7,5},{8,10},{9,11},{10,... | collective-permute-start | bytes 2359304 | tf_op jit(solution)/shard_map/ppermute | solution.py:155
  89.9 18.4 %collective-permute-start.14 = (bf16[256,1536]{1,0:T(8,128)(2,1)}, bf16[256,1536]{1,0:T(8,128)(2,1)}, u32[]{:S(2)}, u32[]{:S(2)}) collective-permute-start(bf16[256,1536]{1,0:T(8,128)(2,1)} %fusion.6), channel_id=1, source_target_pairs={{0,8},{8,0},{16,24},{24,16},{1,9},{9,1},{17,25},{25,17},{2,10},{10... | collective-permute-start | bytes 2359304 | tf_op jit(solution)/shard_map/ppermute | solution.py:253
  91.0 5.4 %copy-start.2 = (bf16[2,2,128,1536]{3,2,1,0:T(8,128)(2,1)S(1)}, bf16[2,2,128,1536]{3,2,1,0:T(8,128)(2,1)}, u32[]{:S(2)}) copy-start(bf16[2,2,128,1536]{3,2,1,0:T(8,128)(2,1)} %shard_map.78) | copy-start | bytes 4718596
  93.7 14.6 %collective-permute-start.15 = (bf16[256,1536]{1,0:T(8,128)(2,1)}, bf16[256,1536]{1,0:T(8,128)(2,1)}, u32[]{:S(2)}, u32[]{:S(2)}) collective-permute-start(bf16[256,1536]{1,0:T(8,128)(2,1)} %fusion.7), channel_id=1, source_target_pairs={{8,16},{16,8},{9,17},{17,9},{10,18},{18,10},{11,19},{19,11},{12,20... | collective-permute-start | bytes 2359304 | tf_op jit(solution)/shard_map/ppermute | solution.py:253
  95.9 25.2 %collective-permute-start.20 = (bf16[64,6144]{1,0:T(8,128)(2,1)}, bf16[64,6144]{1,0:T(8,128)(2,1)}, u32[]{:S(2)}, u32[]{:S(2)}) collective-permute-start(bf16[64,6144]{1,0:T(8,128)(2,1)} %collective-permute-done.17.refs_14_), channel_id=1, source_target_pairs={{0,1},{1,0},{2,3},{3,2},{4,5},{5,4},{6,7},{7,6},{8,9},{9,8},{10,11... | collective-permute-start | bytes 2359304 | tf_op jit(solution)/shard_map/ppermute | solution.py:155
  95.9 25.2 %collective-permute-start.21 = (bf16[64,6144]{1,0:T(8,128)(2,1)}, bf16[64,6144]{1,0:T(8,128)(2,1)}, u32[]{:S(2)}, u32[]{:S(2)}) collective-permute-start(bf16[64,6144]{1,0:T(8,128)(2,1)} %collective-permute-done.18.refs_15_), channel_id=1, source_target_pairs={{0,1},{1,0},{2,3},{3,2},{4,5},{5,4},{6,7},{7,6},{8,9},{9,8},{10,11... | collective-permute-start | bytes 2359304 | tf_op jit(solution)/shard_map/ppermute | solution.py:155
  103.0 18.2 %collective-permute-start.22 = (bf16[64,6144]{1,0:T(8,128)(2,1)}, bf16[64,6144]{1,0:T(8,128)(2,1)}, u32[]{:S(2)}, u32[]{:S(2)}) collective-permute-start(bf16[64,6144]{1,0:T(8,128)(2,1)} %collective-permute-done.19.refs_16_), channel_id=1, source_target_pairs={{0,1},{1,0},{2,3},{3,2},{4,5},{5,4},{6,7},{7,6},{8,9},{9,8},{10,11... | collective-permute-start | bytes 2359304 | tf_op jit(solution)/shard_map/ppermute | solution.py:155
  109.8 39.5 %collective-permute-start.23 = (bf16[256,1536]{1,0:T(8,128)(2,1)S(1)}, bf16[256,1536]{1,0:T(8,128)(2,1)S(1)}, u32[]{:S(2)}, u32[]{:S(2)}) collective-permute-start(bf16[256,1536]{1,0:T(8,128)(2,1)S(1)} %fusion), channel_id=1, source_target_pairs={{8,16},{16,8},{9,17},{17,9},{10,18},{18,10},{11,19},{19,11},{12,20... | collective-permute-start | bytes 2359304 | tf_op jit(solution)/shard_map/ppermute | solution.py:253
  112.0 37.3 %copy-start.4 = (bf16[1,2,128,1536]{3,2,1,0:T(8,128)(2,1)S(1)}, bf16[1,2,128,1536]{3,2,1,0:T(8,128)(2,1)}, u32[]{:S(2)}) copy-start(bf16[1,2,128,1536]{3,2,1,0:T(8,128)(2,1)} %dynamic-slice_select_fusion.4) | copy-start | bytes 2359300
  112.0 37.3 %collective-permute-start.16 = (bf16[256,1536]{1,0:T(8,128)(2,1)S(1)}, bf16[256,1536]{1,0:T(8,128)(2,1)S(1)}, u32[]{:S(2)}, u32[]{:S(2)}) collective-permute-start(bf16[256,1536]{1,0:T(8,128)(2,1)S(1)} %fusion.1), channel_id=1, source_target_pairs={{0,8},{8,0},{16,24},{24,16},{1,9},{9,1},{17,25},{25,17},{2,10},{10... | collective-permute-start | bytes 2359304 | tf_op jit(solution)/shard_map/ppermute | solution.py:253
  149.7 1.8 %collective-permute-start.24 = (bf16[2,64,1536]{2,1,0:T(8,128)(2,1)S(1)}, bf16[2,64,1536]{2,1,0:T(8,128)(2,1)S(1)}, u32[]{:S(2)}, u32[]{:S(2)}) collective-permute-start(bf16[2,64,1536]{2,1,0:T(8,128)(2,1)S(1)} %get-tuple-element.54), channel_id=1, source_target_pairs={{0,1},{1,0},{2,3},{3,2},{4,5},{5,4},{6,7},{7,6},{8,9},{9,8},{10,11... | collective-permute-start | bytes 1179656 | tf_op jit(solution)/shard_map/ppermute | solution.py:155
  (8 other events, 17.8 us)

commit v4 on v3

--- a/solution.py
+++ b/solution.py
@@ -135,6 +135,48 @@
     )(after(first, *due) if due else first, *[piece for piece, _ in pieces], weight)
 
 
+def step_kernel(pick_ref, *refs, choices, has_input, has_sum):
+    n = len(choices)
+    come_refs, share_refs, out_refs = refs[:-2 * n - 2], refs[-2 * n - 2:-2], refs[-2:]
+    for kind in range(2):
+        dx, q, is_input = (pick_ref[3 * kind + i] for i in range(3))
+        out_ref = out_refs[kind]
+        if has_input:
+            @pl.when(is_input == 1)
+            def _(kind=kind, out_ref=out_ref):
+                out_ref[...] = come_refs[1 - kind][...]
+
+        for i, choice in enumerate(choices):
+            @pl.when((is_input == 0) & (q == choice))
+            def _(kind=kind, out_ref=out_ref, i=i):
+                share = share_refs[n * kind + i][0, 0]
+                if has_sum:
+                    share = share.astype(jnp.float32) + come_refs[1 - kind][...].astype(jnp.float32)
+                out_ref[...] = share.astype(out_ref.dtype)
+
+
+def step_values(picks, come, shares, choices, has_input, has_sum):
+    _, n_y, rows, columns = shares[0].shape
+    block = next((b for b in (768, 512, 384, 256, 128) if columns % b == 0), columns)
+    flat = pl.BlockSpec((rows, block), lambda y, j, p: (y, j))
+    return pl.pallas_call(
+        functools.partial(step_kernel, choices=choices, has_input=has_input, has_sum=has_sum),
+        grid_spec=pltpu.PrefetchScalarGridSpec(
+            num_scalar_prefetch=1,
+            grid=(n_y, columns // block),
+            in_specs=[flat] * len(come)
+            + [
+                pl.BlockSpec((1, 1, rows, block), lambda y, j, p, kind=kind: (p[3 * kind], y, 0, j))
+                for kind in range(2)
+                for _ in choices
+            ],
+            out_specs=[flat, flat],
+        ),
+        out_shape=[jax.ShapeDtypeStruct((n_y * rows, columns), jnp.bfloat16)] * 2,
+        compiler_params=pltpu.CompilerParams(vmem_limit_bytes=VMEM),
+    )(picks, *come, *(shares[choice] for choice in choices * 2))
+
+
 def make_body(n_h, n_w, n_r):
     n_c = 2 if n_r % 2 == 0 else 1
     n_y = n_r // n_c
@@ -238,17 +280,20 @@
         def step_planes(m, *late):
             step, apart = m - 1, n_h - m + 1
             choices = passes([j + apart for j in range(step)] + [j - apart for j in range(apart, n_h)]) if step else []
-            come, sent = tuple(came), []
+            come, picks = tuple(came), []
             for kind in range(2):
                 to_right = even if kind == 0 else ~even
-                value = come[1 - kind] if m < n_h else None
-                if step:
-                    total = share_of(jnp.where(to_right, h + apart, h - apart), choices, come)
-                    if step > 1:
-                        total = (total.astype(jnp.float32) + come[1 - kind].astype(jnp.float32)).astype(jnp.bfloat16)
-                    is_input = jnp.where(to_right, h >= step, h < apart)
-                    value = total if value is None else jnp.where(is_input, value, total)
-                sent.append(after(value, *late) if late else value)
+                target = jnp.clip(jnp.where(to_right, h + apart, h - apart), 0, n_h - 1)
+                owner, group = target // per_w, target % per_w
+                is_input = jnp.where(to_right, h >= step, h < apart) & (m < n_h)
+                picks += [(w - owner) % n_w, slot_of(owner, group), is_input.astype(jnp.int32)]
+            if step:
+                picks = jnp.stack(picks).astype(jnp.int32)
+                sent = step_values(picks, come, shares, choices, m < n_h, step > 1)
+            else:
+                sent = [come[1], come[0]]
+            if late:
+                sent = [after(value, *late) for value in sent]
             for kind in range(2):
                 came[kind] = lax.ppermute(sent[kind], "hidden", pairs[kind])
                 from_right = even if kind == 0 else ~even

time: 154 us -> 154 us (level)
  Pallas kernels: 66 us -> 80.8 us
  other arithmetic: 17.6 us -> 5.58 us
  starting transfers between devices: 32.4 us -> 27.2 us
  waiting for transfers between devices: 28.3 us -> 32.8 us
    pallas_call x0 -> x3, Pallas kernels: none -> 15 us  [step_values(): pl.pallas_call(functools.partial(step_kernel, choices=choices, has_input=...]
    ppermute x3, waiting for transfers between devices: 5.11 us -> 16.7 us  [over_width(): lax.ppermute(value, 'width', [(w, (w + dx) % n_w) for w in range(n_w)])]
    select_n x3 -> x0, other arithmetic: 7.74 us -> none  [step_planes(): value = total if value is None else jnp.where(is_input, value, total)]
    ppermute x14, waiting for transfers between devices: 17.8 us -> 11.3 us  [over_replica(): return lax.ppermute(value, 'replica', replica_perm(dy, dc))]
    ppermute x8, starting transfers between devices: 20.3 us -> 14.9 us  [step_planes(): came[kind] = lax.ppermute(sent[kind], 'hidden', pairs[kind])]
    convert_element_type x2 -> x0, other arithmetic: 2.65 us -> none  [step_planes(): (total.astype(jnp.float32) + come[1 - kind].astype(jnp.float32)).astype(j...]
    another operation x1 -> x4, local copies, waits for them, and re-layouts: 0.01 us -> 1.95 us  [the longest x3 1.95 us: step_planes(): picks = jnp.stack(picks).astype(jnp.int32)]
    unnamed x30 -> x28, local copies, waits for them, and re-layouts: 1.87 us -> 0.05 us
  transfers between devices with their start and end apart: 25 -> 25, of which waited for: 7 -> 5; matrix products, arithmetic and copies ran while one was open for 13% -> 5% of each run, Pallas kernels for 43% -> 53%
where the time goes in v4:
time: 154 us
  Pallas kernels  80.8 us (52%)
  waiting for transfers between devices  32.8 us (21%)
  starting transfers between devices  27.2 us (18%)
  local copies, waits for them, and re-layouts  6.13 us (4%)
  other arithmetic  5.58 us (4%)
    pallas_call x2, Pallas kernels, input_grad(): pl.pallas_call(input_grad_kernel, grid_spec=pltpu.PrefetchScalarGridSpec(...  37.7 us
    pallas_call x1, Pallas kernels, weight_grad(): pl.pallas_call(body, grid_spec=pltpu.PrefetchScalarGridSpec(num_scalar_pr...  28.1 us
    ppermute x3, waiting for transfers between devices, over_width(): lax.ppermute(value, 'width', [(w, (w + dx) % n_w) for w in range(n_w)])  16.7 us
    pallas_call x3, Pallas kernels, step_values(): pl.pallas_call(functools.partial(step_kernel, choices=choices, has_input=...  15 us
    ppermute x8, starting transfers between devices, step_planes(): came[kind] = lax.ppermute(sent[kind], 'hidden', pairs[kind])  14.9 us
    ppermute x14, waiting for transfers between devices, over_replica(): return lax.ppermute(value, 'replica', replica_perm(dy, dc))  11.3 us
    ppermute x14, starting transfers between devices, over_replica(): return lax.ppermute(value, 'replica', replica_perm(dy, dc))  7.29 us
    ppermute x3, starting transfers between devices, over_width(): lax.ppermute(value, 'width', [(w, (w + dx) % n_w) for w in range(n_w)])  4.98 us
  transfers between devices with their start and end apart: 25, of which 5 were waited for; matrix products, arithmetic and copies ran while one was open for 5% of the time, Pallas kernels for 53%

profile of v4, /device:TPU:0, one launch (start us, length us, event | category | flops | bytes accessed | tf_op | source)
XLA Modules:
  0.0 153.6 jit_solution(7128294816859648969)
XLA Ops:
  0.8 2.2 %constant_dynamic-slice_fusion.6 = (bf16[64,1536]{1,0:T(8,128)(2,1)S(1)}, bf16[64,1536]{1,0:T(8,128)(2,1)}, bf16[64,1536]{1,0:T(8,128)(2,1)}, bf16[64,1536]{1,0:T(8,128)(2,1)}) fusion(bf16[64,6144]{1,0:T(8,128)(2,1)} %param.6, s32[]{:T(128)S(6)} %select_n.417, s32[]{:T(128)S(6)} %select_n.419, s32[]{:T(128)S(6)} %select_n.422, s32[]{:T(128)S(6)} %select_n.421), kind=kLoop, calls=%fused_computation.27 | loop fusion | bytes 1572880 | tf_op jit(solution)/shard_map/dynamic_slice | solution.py:215
  3.9 0.8 collective-permute-done
  5.0 1.2 constant_dynamic-slice_fusion
  6.3 2.6 %collective-permute-start.4 = (bf16[64,6144]{1,0:T(8,128)(2,1)}, bf16[64,6144]{1,0:T(8,128)(2,1)}, u32[]{:S(2)}, u32[]{:S(2)}) collective-permute-start(bf16[64,6144]{1,0:T(8,128)(2,1)} %get-tuple-element.27), channel_id=1, source_target_pairs={{0,4},{4,0},{1,5},{5,1},{2,6},{6,2},{3,7},{7,3},{8,12},{12,8},{9,1... | collective-permute-start | bytes 2359304 | tf_op jit(solution)/shard_map/ppermute | solution.py:200
  8.9 1.2 collective-permute-start.2
  10.6 16.7 %collective-permute-done.4.refs_2_.refs_8_ = bf16[64,6144]{1,0:T(8,128)(2,1)} collective-permute-done((bf16[64,6144]{1,0:T(8,128)(2,1)}, bf16[64,6144]{1,0:T(8,128)(2,1)}, u32[]{:S(2)}, u32[]{:S(2)}) %collective-permute-start.4) | collective-permute-done | bytes 786464 | tf_op jit(solution)/shard_map/ppermute | solution.py:200
  27.3 1.8 %collective-permute-start.10 = (bf16[64,6144]{1,0:T(8,128)(2,1)}, bf16[64,6144]{1,0:T(8,128)(2,1)S(1)}, u32[]{:S(2)}, u32[]{:S(2)}) collective-permute-start(bf16[64,6144]{1,0:T(8,128)(2,1)} %get-tuple-element.40), channel_id=1, source_target_pairs={{0,4},{4,0},{1,5},{5,1},{2,6},{6,2},{3,7},{7,3},{8,12},{12,8},{9,1... | collective-permute-start | bytes 2359304 | tf_op jit(solution)/shard_map/ppermute | solution.py:200
  29.1 1.5 collective-permute-start.8
  31.3 2.0 %pad_maximum_fusion.refs_0_ = bf16[256,1536]{1,0:T(8,128)(2,1)} fusion(bf16[64,1536]{1,0:T(8,128)(2,1)} %collective-permute-done.2, bf16[64,1536]{1,0:T(8,128)(2,1)} %collective-permute-done.1, bf16[64,1536]{1,0:T(8,128)(2,1)S(1)} %collective-permute-done, bf16[64,1536]{1,0:T(8,128)(2,1)S(1)} %get-tuple-element.52), kind=kLoop, calls=%fused_computation.8 | loop fusion | flops 3145728 | bytes 1572864 | tf_op jit(solution)/shard_map/concatenate | solution.py:217
  33.2 1.6 %collective-permute-start.7 = (bf16[256,1536]{1,0:T(8,128)(2,1)}, bf16[256,1536]{1,0:T(8,128)(2,1)}, u32[]{:S(2)}, u32[]{:S(2)}) collective-permute-start(bf16[256,1536]{1,0:T(8,128)(2,1)} %pad_maximum_fusion.refs_0_), channel_id=1, source_target_pairs={{8,16},{16,8},{9,17},{17,9},{10,18},{18,10},{11,19},{19,11},{12,20... | collective-permute-start | bytes 2359304 | tf_op jit(solution)/shard_map/ppermute | solution.py:298
  34.8 3.5 %collective-permute-start.6 = (bf16[256,1536]{1,0:T(8,128)(2,1)}, bf16[256,1536]{1,0:T(8,128)(2,1)}, u32[]{:S(2)}, u32[]{:S(2)}) collective-permute-start(bf16[256,1536]{1,0:T(8,128)(2,1)} %pad_maximum_fusion.refs_0_), channel_id=1, source_target_pairs={{0,8},{8,0},{16,24},{24,16},{1,9},{9,1},{17,25},{25,17},{2,10},{10... | collective-permute-start | bytes 2359304 | tf_op jit(solution)/shard_map/ppermute | solution.py:298
  38.3 18.9 %shard_map.77.refs_2_.refs_3_.refs_4_ = bf16[2,2,128,1536]{3,2,1,0:T(8,128)(2,1)} custom-call(s32[5]{0:T(128)} %get-tuple-element.24.first_ref, bf16[128,6144]{1,0:T(8,128)(2,1)} %copy-done.2, bf16[128,6144]{1,0:T(8,128)(2,1)} %copy-done.3, bf16[64,6144]{1,0:T(8,128)(2,1)} %collective-permute-done.4.refs_2_.refs_8_, ...), custom_call_target="tpu_custom_call" | custom-call | tf_op jit(solution)/shard_map/pallas_call | solution.py:120
  58.3 0.7 stack.179.pick_ref
  59.0 4.7 %shard_map.79 = (bf16[256,1536]{1,0:T(8,128)(2,1)}, bf16[256,1536]{1,0:T(8,128)(2,1)}) custom-call(s32[6]{0:T(128)} %stack.179.pick_ref, bf16[256,1536]{1,0:T(8,128)(2,1)} %collective-permute-done.6.refs_0_.refs_1_, bf16[256,1536]{1,0:T(8,128)(2,1)} %collective-permute-done.7.refs_1_.refs_2_, bf16[2,2,128,1536]{3,2,1,0:T(8,128)(2,1)} %shard_map.77.refs_2_.refs_3_.refs_4_, ...), custom_call_target="tpu_custom_call" | custom-call | tf_op jit(solution)/shard_map/pallas_call | solution.py:162
  63.6 1.6 %collective-permute-start.13 = (bf16[256,1536]{1,0:T(8,128)(2,1)}, bf16[256,1536]{1,0:T(8,128)(2,1)}, u32[]{:S(2)}, u32[]{:S(2)}) collective-permute-start(bf16[256,1536]{1,0:T(8,128)(2,1)} %get-tuple-element.35), channel_id=1, source_target_pairs={{8,16},{16,8},{9,17},{17,9},{10,18},{18,10},{11,19},{19,11},{12,20... | collective-permute-start | bytes 2359304 | tf_op jit(solution)/shard_map/ppermute | solution.py:298
  65.2 1.6 %collective-permute-start.12 = (bf16[256,1536]{1,0:T(8,128)(2,1)}, bf16[256,1536]{1,0:T(8,128)(2,1)}, u32[]{:S(2)}, u32[]{:S(2)}) collective-permute-start(bf16[256,1536]{1,0:T(8,128)(2,1)} %get-tuple-element.33), channel_id=1, source_target_pairs={{0,8},{8,0},{16,24},{24,16},{1,9},{9,1},{17,25},{25,17},{2,10},{10... | collective-permute-start | bytes 2359304 | tf_op jit(solution)/shard_map/ppermute | solution.py:298
  67.4 18.9 %shard_map.78.refs_3_.refs_5_ = bf16[2,2,128,1536]{3,2,1,0:T(8,128)(2,1)} custom-call(s32[5]{0:T(128)} %get-tuple-element.29.first_ref, bf16[128,6144]{1,0:T(8,128)(2,1)} %copy-done.2, bf16[128,6144]{1,0:T(8,128)(2,1)} %copy-done.3, bf16[64,6144]{1,0:T(8,128)(2,1)} %copy-done.6, bf16[64,6144]{1,0:T(8,128)(2,1)} %copy-done.7, bf16[6144,6144]{1,0:T(8,128)(2,1)} %refs_4_.3), custom_call_target="tpu_custom_call" | custom-call | tf_op jit(solution)/shard_map/pallas_call | solution.py:120
  86.3 1.6 %collective-permute-start.19 = (bf16[64,6144]{1,0:T(8,128)(2,1)}, bf16[64,6144]{1,0:T(8,128)(2,1)}, u32[]{:S(2)}, u32[]{:S(2)}) collective-permute-start(bf16[64,6144]{1,0:T(8,128)(2,1)} %copy-done.6), channel_id=1, source_target_pairs={{0,2},{1,3},{2,0},{3,1},{4,6},{5,7},{6,4},{7,5},{8,10},{9,11},{10,... | collective-permute-start | bytes 2359304 | tf_op jit(solution)/shard_map/ppermute | solution.py:197
  87.9 0.6 stack.170.pick_ref
  88.5 5.2 %shard_map.80 = (bf16[256,1536]{1,0:T(8,128)(2,1)}, bf16[256,1536]{1,0:T(8,128)(2,1)}) custom-call(s32[6]{0:T(128)} %stack.170.pick_ref, bf16[256,1536]{1,0:T(8,128)(2,1)} %collective-permute-done.12.refs_0_.refs_3_, bf16[256,1536]{1,0:T(8,128)(2,1)} %collective-permute-done.13.refs_1_.refs_4_, bf16[2,2,128,1536]{3,2,1,0:T(8,128)(2,1)} %shard_map.77.refs_2_.refs_3_.refs_4_, ...), custom_call_target="tpu_custom_call" | custom-call | tf_op jit(solution)/shard_map/pallas_call | solution.py:162
  94.2 1.6 %collective-permute-start.15 = (bf16[256,1536]{1,0:T(8,128)(2,1)}, bf16[256,1536]{1,0:T(8,128)(2,1)}, u32[]{:S(2)}, u32[]{:S(2)}) collective-permute-start(bf16[256,1536]{1,0:T(8,128)(2,1)} %get-tuple-element.37), channel_id=1, source_target_pairs={{8,16},{16,8},{9,17},{17,9},{10,18},{18,10},{11,19},{19,11},{12,20... | collective-permute-start | bytes 2359304 | tf_op jit(solution)/shard_map/ppermute | solution.py:298
  96.2 8.8 %collective-permute-done.19.refs_16_ = bf16[64,6144]{1,0:T(8,128)(2,1)} collective-permute-done((bf16[64,6144]{1,0:T(8,128)(2,1)}, bf16[64,6144]{1,0:T(8,128)(2,1)}, u32[]{:S(2)}, u32[]{:S(2)}) %collective-permute-start.19) | collective-permute-done | bytes 786464 | tf_op jit(solution)/shard_map/ppermute | solution.py:197
  105.1 0.7 stack.161.pick_ref
  105.7 0.6 stack.194.place_ref
  106.4 1.0 dynamic-slice_select_fusion
  107.4 4.8 %collective-permute-done.14.refs_0_.refs_5_ = bf16[256,1536]{1,0:T(8,128)(2,1)} collective-permute-done((bf16[256,1536]{1,0:T(8,128)(2,1)}, bf16[256,1536]{1,0:T(8,128)(2,1)}, u32[]{:S(2)}, u32[]{:S(2)}) %collective-permute-start.14) | collective-permute-done | bytes 786464 | tf_op jit(solution)/shard_map/ppermute | solution.py:298
  112.2 5.1 %shard_map.81 = (bf16[256,1536]{1,0:T(8,128)(2,1)}, bf16[256,1536]{1,0:T(8,128)(2,1)}) custom-call(s32[6]{0:T(128)} %stack.161.pick_ref, bf16[256,1536]{1,0:T(8,128)(2,1)} %collective-permute-done.14.refs_0_.refs_5_, bf16[256,1536]{1,0:T(8,128)(2,1)} %collective-permute-done.15.refs_1_.refs_6_, bf16[2,2,128,1536]{3,2,1,0:T(8,128)(2,1)} %shard_map.77.refs_2_.refs_3_.refs_4_, ...), custom_call_target="tpu_custom_call" | custom-call | tf_op jit(solution)/shard_map/pallas_call | solution.py:162
  117.3 3.6 %collective-permute-start.16 = (bf16[256,1536]{1,0:T(8,128)(2,1)}, bf16[256,1536]{1,0:T(8,128)(2,1)S(1)}, u32[]{:S(2)}, u32[]{:S(2)}) collective-permute-start(bf16[256,1536]{1,0:T(8,128)(2,1)} %get-tuple-element.38), channel_id=1, source_target_pairs={{0,8},{8,0},{16,24},{24,16},{1,9},{9,1},{17,25},{25,17},{2,10},{10... | collective-permute-start | bytes 2359304 | tf_op jit(solution)/shard_map/ppermute | solution.py:298
  120.9 1.0 collective-permute-start.23
  122.0 28.1 %shard_map.82 = f32[1536,6144]{1,0:T(8,128)} custom-call(s32[28]{0:T(128)} %stack.194.place_ref, bf16[256,1536]{1,0:T(8,128)(2,1)} %pad_maximum_fusion.refs_0_, bf16[256,1536]{1,0:T(8,128)(2,1)} %collective-permute-done.6.refs_0_.refs_1_, bf16[256,1536]{1,0:T(8,128)(2,1)} %collective-permute-done.7.refs_1_.refs_2_, ...), custom_call_target="tpu_custom_call" | custom-call | flops 19327352832 | bytes 53477376 | tf_op jit(solution)/shard_map/pallas_call | solution.py:78
  150.7 1.7 %collective-permute-done.24 = bf16[2,64,1536]{2,1,0:T(8,128)(2,1)S(1)} collective-permute-done((bf16[2,64,1536]{2,1,0:T(8,128)(2,1)S(1)}, bf16[2,64,1536]{2,1,0:T(8,128)(2,1)S(1)}, u32[]{:S(2)}, u32[]{:S(2)}) %collective-permute-start.24) | collective-permute-done | bytes 393248 | tf_op jit(solution)/shard_map/ppermute | solution.py:197
  152.7 0.9 pad_maximum_fusion.1
  (72 shorter events, 5.9 us)
Async XLA Ops:
  2.9 1.7 %collective-permute-start = (bf16[64,1536]{1,0:T(8,128)(2,1)}, bf16[64,1536]{1,0:T(8,128)(2,1)S(1)}, u32[]{:S(2)}, u32[]{:S(2)}) collective-permute-start(bf16[64,1536]{1,0:T(8,128)(2,1)} %get-tuple-element.53), channel_id=1, source_target_pairs={{0,1},{1,0},{2,3},{3,2},{4,5},{5,4},{6,7},{7,6},{8,9},{9,8},{10,11... | collective-permute-start | bytes 589832 | tf_op jit(solution)/shard_map/ppermute | solution.py:197
  4.7 22.6 %collective-permute-start.3 = (bf16[128,6144]{1,0:T(8,128)(2,1)S(1)}, bf16[128,6144]{1,0:T(8,128)(2,1)S(1)}, u32[]{:S(2)}, u32[]{:S(2)}) collective-permute-start(bf16[128,6144]{1,0:T(8,128)(2,1)S(1)} %multiply_convert_fusion.refs_0_.refs_7_), channel_id=1, source_target_pairs={{0,1},{1,0},{2,3},{3,2},{4,5},{5,4},{6,7},{7,6},{8,9},{9,8},{10,11... | collective-permute-start | bytes 4718600 | tf_op jit(solution)/shard_map/ppermute | solution.py:197
  5.0 5.1 %copy-start.8 = (bf16[64,1536]{1,0:T(8,128)(2,1)S(1)}, bf16[64,1536]{1,0:T(8,128)(2,1)}, u32[]{:S(2)}) copy-start(bf16[64,1536]{1,0:T(8,128)(2,1)} %get-tuple-element.55) | copy-start | bytes 589828
  6.3 21.0 %collective-permute-start.4 = (bf16[64,6144]{1,0:T(8,128)(2,1)}, bf16[64,6144]{1,0:T(8,128)(2,1)}, u32[]{:S(2)}, u32[]{:S(2)}) collective-permute-start(bf16[64,6144]{1,0:T(8,128)(2,1)} %get-tuple-element.27), channel_id=1, source_target_pairs={{0,4},{4,0},{1,5},{5,1},{2,6},{6,2},{3,7},{7,3},{8,12},{12,8},{9,1... | collective-permute-start | bytes 2359304 | tf_op jit(solution)/shard_map/ppermute | solution.py:200
  8.9 20.2 %collective-permute-start.2 = (bf16[64,1536]{1,0:T(8,128)(2,1)S(1)}, bf16[64,1536]{1,0:T(8,128)(2,1)}, u32[]{:S(2)}, u32[]{:S(2)}) collective-permute-start(bf16[64,1536]{1,0:T(8,128)(2,1)S(1)} %copy-done.9), channel_id=1, source_target_pairs={{0,3},{1,2},{2,1},{3,0},{4,7},{5,6},{6,5},{7,4},{8,11},{9,10},{10,... | collective-permute-start | bytes 589832 | tf_op jit(solution)/shard_map/ppermute | solution.py:197
  10.1 19.0 %collective-permute-start.1 = (bf16[64,1536]{1,0:T(8,128)(2,1)S(1)}, bf16[64,1536]{1,0:T(8,128)(2,1)}, u32[]{:S(2)}, u32[]{:S(2)}) collective-permute-start(bf16[64,1536]{1,0:T(8,128)(2,1)S(1)} %copy-done.8), channel_id=1, source_target_pairs={{0,2},{1,3},{2,0},{3,1},{4,6},{5,7},{6,4},{7,5},{8,10},{9,11},{10,... | collective-permute-start | bytes 589832 | tf_op jit(solution)/shard_map/ppermute | solution.py:197
  27.3 11.1 %collective-permute-start.5 = (bf16[64,6144]{1,0:T(8,128)(2,1)}, bf16[64,6144]{1,0:T(8,128)(2,1)}, u32[]{:S(2)}, u32[]{:S(2)}) collective-permute-start(bf16[64,6144]{1,0:T(8,128)(2,1)} %collective-permute-done.4.refs_2_.refs_8_), channel_id=1, source_target_pairs={{0,1},{1,0},{2,3},{3,2},{4,5},{5,4},{6,7},{7,6},{8,9},{9,8},{10,11... | collective-permute-start | bytes 2359304 | tf_op jit(solution)/shard_map/ppermute | solution.py:197
  27.3 11.0 %copy-start.3 = (bf16[128,6144]{1,0:T(8,128)(2,1)}, bf16[128,6144]{1,0:T(8,128)(2,1)S(1)}, u32[]{:S(2)}) copy-start(bf16[128,6144]{1,0:T(8,128)(2,1)S(1)} %collective-permute-done.3.refs_1_.refs_10_) | copy-start | bytes 4718596
  27.3 29.9 %collective-permute-start.10 = (bf16[64,6144]{1,0:T(8,128)(2,1)}, bf16[64,6144]{1,0:T(8,128)(2,1)S(1)}, u32[]{:S(2)}, u32[]{:S(2)}) collective-permute-start(bf16[64,6144]{1,0:T(8,128)(2,1)} %get-tuple-element.40), channel_id=1, source_target_pairs={{0,4},{4,0},{1,5},{5,1},{2,6},{6,2},{3,7},{7,3},{8,12},{12,8},{9,1... | collective-permute-start | bytes 2359304 | tf_op jit(solution)/shard_map/ppermute | solution.py:200
  29.1 28.2 %collective-permute-start.8 = (bf16[64,6144]{1,0:T(8,128)(2,1)}, bf16[64,6144]{1,0:T(8,128)(2,1)}, u32[]{:S(2)}, u32[]{:S(2)}) collective-permute-start(bf16[64,6144]{1,0:T(8,128)(2,1)} %get-tuple-element.27), channel_id=1, source_target_pairs={{0,2},{1,3},{2,0},{3,1},{4,6},{5,7},{6,4},{7,5},{8,10},{9,11},{10,... | collective-permute-start | bytes 2359304 | tf_op jit(solution)/shard_map/ppermute | solution.py:197
  33.2 25.7 %collective-permute-start.7 = (bf16[256,1536]{1,0:T(8,128)(2,1)}, bf16[256,1536]{1,0:T(8,128)(2,1)}, u32[]{:S(2)}, u32[]{:S(2)}) collective-permute-start(bf16[256,1536]{1,0:T(8,128)(2,1)} %pad_maximum_fusion.refs_0_), channel_id=1, source_target_pairs={{8,16},{16,8},{9,17},{17,9},{10,18},{18,10},{11,19},{19,11},{12,20... | collective-permute-start | bytes 2359304 | tf_op jit(solution)/shard_map/ppermute | solution.py:298
  34.8 24.1 %collective-permute-start.6 = (bf16[256,1536]{1,0:T(8,128)(2,1)}, bf16[256,1536]{1,0:T(8,128)(2,1)}, u32[]{:S(2)}, u32[]{:S(2)}) collective-permute-start(bf16[256,1536]{1,0:T(8,128)(2,1)} %pad_maximum_fusion.refs_0_), channel_id=1, source_target_pairs={{0,8},{8,0},{16,24},{24,16},{1,9},{9,1},{17,25},{25,17},{2,10},{10... | collective-permute-start | bytes 2359304 | tf_op jit(solution)/shard_map/ppermute | solution.py:298
  57.2 10.2 %copy-start.6 = (bf16[64,6144]{1,0:T(8,128)(2,1)}, bf16[64,6144]{1,0:T(8,128)(2,1)S(1)}, u32[]{:S(2)}) copy-start(bf16[64,6144]{1,0:T(8,128)(2,1)S(1)} %collective-permute-done.10.refs_2_.refs_9_) | copy-start | bytes 2359300
  57.2 6.4 %collective-permute-start.11 = (bf16[64,6144]{1,0:T(8,128)(2,1)S(1)}, bf16[64,6144]{1,0:T(8,128)(2,1)S(1)}, u32[]{:S(2)}, u32[]{:S(2)}) collective-permute-start(bf16[64,6144]{1,0:T(8,128)(2,1)S(1)} %collective-permute-done.10.refs_2_.refs_9_), channel_id=1, source_target_pairs={{0,1},{1,0},{2,3},{3,2},{4,5},{5,4},{6,7},{7,6},{8,9},{9,8},{10,11... | collective-permute-start | bytes 2359304 | tf_op jit(solution)/shard_map/ppermute | solution.py:197
  57.3 10.1 %collective-permute-start.9 = (bf16[64,6144]{1,0:T(8,128)(2,1)}, bf16[64,6144]{1,0:T(8,128)(2,1)S(1)}, u32[]{:S(2)}, u32[]{:S(2)}) collective-permute-start(bf16[64,6144]{1,0:T(8,128)(2,1)} %collective-permute-done.8.refs_13_), channel_id=1, source_target_pairs={{0,1},{1,0},{2,3},{3,2},{4,5},{5,4},{6,7},{7,6},{8,9},{9,8},{10,11... | collective-permute-start | bytes 2359304 | tf_op jit(solution)/shard_map/ppermute | solution.py:197
  57.8 28.5 %collective-permute-start.17 = (bf16[64,6144]{1,0:T(8,128)(2,1)}, bf16[64,6144]{1,0:T(8,128)(2,1)}, u32[]{:S(2)}, u32[]{:S(2)}) collective-permute-start(bf16[64,6144]{1,0:T(8,128)(2,1)} %get-tuple-element.40), channel_id=1, source_target_pairs={{0,2},{1,3},{2,0},{3,1},{4,6},{5,7},{6,4},{7,5},{8,10},{9,11},{10,... | collective-permute-start | bytes 2359304 | tf_op jit(solution)/shard_map/ppermute | solution.py:197
  63.6 24.9 %collective-permute-start.13 = (bf16[256,1536]{1,0:T(8,128)(2,1)}, bf16[256,1536]{1,0:T(8,128)(2,1)}, u32[]{:S(2)}, u32[]{:S(2)}) collective-permute-start(bf16[256,1536]{1,0:T(8,128)(2,1)} %get-tuple-element.35), channel_id=1, source_target_pairs={{8,16},{16,8},{9,17},{17,9},{10,18},{18,10},{11,19},{19,11},{12,20... | collective-permute-start | bytes 2359304 | tf_op jit(solution)/shard_map/ppermute | solution.py:298
  65.2 23.3 %collective-permute-start.12 = (bf16[256,1536]{1,0:T(8,128)(2,1)}, bf16[256,1536]{1,0:T(8,128)(2,1)}, u32[]{:S(2)}, u32[]{:S(2)}) collective-permute-start(bf16[256,1536]{1,0:T(8,128)(2,1)} %get-tuple-element.33), channel_id=1, source_target_pairs={{0,8},{8,0},{16,24},{24,16},{1,9},{9,1},{17,25},{25,17},{2,10},{10... | collective-permute-start | bytes 2359304 | tf_op jit(solution)/shard_map/ppermute | solution.py:298
  66.9 28.9 %collective-permute-start.18 = (bf16[64,6144]{1,0:T(8,128)(2,1)}, bf16[64,6144]{1,0:T(8,128)(2,1)}, u32[]{:S(2)}, u32[]{:S(2)}) collective-permute-start(bf16[64,6144]{1,0:T(8,128)(2,1)} %collective-permute-done.8.refs_13_), channel_id=1, source_target_pairs={{0,4},{4,0},{1,5},{5,1},{2,6},{6,2},{3,7},{7,3},{8,12},{12,8},{9,1... | collective-permute-start | bytes 2359304 | tf_op jit(solution)/shard_map/ppermute | solution.py:200
  67.4 18.9 %copy-start.11 = (bf16[64,6144]{1,0:T(8,128)(2,1)}, bf16[64,6144]{1,0:T(8,128)(2,1)S(1)}, u32[]{:S(2)}) copy-start(bf16[64,6144]{1,0:T(8,128)(2,1)S(1)} %collective-permute-done.9.refs_17_) | copy-start | bytes 2359300
  86.3 18.8 %collective-permute-start.19 = (bf16[64,6144]{1,0:T(8,128)(2,1)}, bf16[64,6144]{1,0:T(8,128)(2,1)}, u32[]{:S(2)}, u32[]{:S(2)}) collective-permute-start(bf16[64,6144]{1,0:T(8,128)(2,1)} %copy-done.6), channel_id=1, source_target_pairs={{0,2},{1,3},{2,0},{3,1},{4,6},{5,7},{6,4},{7,5},{8,10},{9,11},{10,... | collective-permute-start | bytes 2359304 | tf_op jit(solution)/shard_map/ppermute | solution.py:197
  88.5 17.9 %copy-start = (bf16[2,2,128,1536]{3,2,1,0:T(8,128)(2,1)S(1)}, bf16[2,2,128,1536]{3,2,1,0:T(8,128)(2,1)}, u32[]{:S(2)}) copy-start(bf16[2,2,128,1536]{3,2,1,0:T(8,128)(2,1)} %shard_map.77.refs_2_.refs_3_.refs_4_) | copy-start | bytes 4718596
  88.5 17.9 %copy-start.1 = (bf16[2,2,128,1536]{3,2,1,0:T(8,128)(2,1)S(1)}, bf16[2,2,128,1536]{3,2,1,0:T(8,128)(2,1)}, u32[]{:S(2)}) copy-start(bf16[2,2,128,1536]{3,2,1,0:T(8,128)(2,1)} %shard_map.78.refs_3_.refs_5_) | copy-start | bytes 4718596
  93.8 18.4 %collective-permute-start.14 = (bf16[256,1536]{1,0:T(8,128)(2,1)}, bf16[256,1536]{1,0:T(8,128)(2,1)}, u32[]{:S(2)}, u32[]{:S(2)}) collective-permute-start(bf16[256,1536]{1,0:T(8,128)(2,1)} %get-tuple-element.36), channel_id=1, source_target_pairs={{0,8},{8,0},{16,24},{24,16},{1,9},{9,1},{17,25},{25,17},{2,10},{10... | collective-permute-start | bytes 2359304 | tf_op jit(solution)/shard_map/ppermute | solution.py:298
  94.2 18.0 %collective-permute-start.15 = (bf16[256,1536]{1,0:T(8,128)(2,1)}, bf16[256,1536]{1,0:T(8,128)(2,1)}, u32[]{:S(2)}, u32[]{:S(2)}) collective-permute-start(bf16[256,1536]{1,0:T(8,128)(2,1)} %get-tuple-element.37), channel_id=1, source_target_pairs={{8,16},{16,8},{9,17},{17,9},{10,18},{18,10},{11,19},{19,11},{12,20... | collective-permute-start | bytes 2359304 | tf_op jit(solution)/shard_map/ppermute | solution.py:298
  95.7 26.2 %collective-permute-start.20 = (bf16[64,6144]{1,0:T(8,128)(2,1)}, bf16[64,6144]{1,0:T(8,128)(2,1)}, u32[]{:S(2)}, u32[]{:S(2)}) collective-permute-start(bf16[64,6144]{1,0:T(8,128)(2,1)} %collective-permute-done.17.refs_14_), channel_id=1, source_target_pairs={{0,1},{1,0},{2,3},{3,2},{4,5},{5,4},{6,7},{7,6},{8,9},{9,8},{10,11... | collective-permute-start | bytes 2359304 | tf_op jit(solution)/shard_map/ppermute | solution.py:197
  95.7 26.2 %collective-permute-start.21 = (bf16[64,6144]{1,0:T(8,128)(2,1)}, bf16[64,6144]{1,0:T(8,128)(2,1)}, u32[]{:S(2)}, u32[]{:S(2)}) collective-permute-start(bf16[64,6144]{1,0:T(8,128)(2,1)} %collective-permute-done.18.refs_15_), channel_id=1, source_target_pairs={{0,1},{1,0},{2,3},{3,2},{4,5},{5,4},{6,7},{7,6},{8,9},{9,8},{10,11... | collective-permute-start | bytes 2359304 | tf_op jit(solution)/shard_map/ppermute | solution.py:197
  105.1 16.9 %collective-permute-start.22 = (bf16[64,6144]{1,0:T(8,128)(2,1)}, bf16[64,6144]{1,0:T(8,128)(2,1)}, u32[]{:S(2)}, u32[]{:S(2)}) collective-permute-start(bf16[64,6144]{1,0:T(8,128)(2,1)} %collective-permute-done.19.refs_16_), channel_id=1, source_target_pairs={{0,1},{1,0},{2,3},{3,2},{4,5},{5,4},{6,7},{7,6},{8,9},{9,8},{10,11... | collective-permute-start | bytes 2359304 | tf_op jit(solution)/shard_map/ppermute | solution.py:197
  117.3 32.8 %collective-permute-start.16 = (bf16[256,1536]{1,0:T(8,128)(2,1)}, bf16[256,1536]{1,0:T(8,128)(2,1)S(1)}, u32[]{:S(2)}, u32[]{:S(2)}) collective-permute-start(bf16[256,1536]{1,0:T(8,128)(2,1)} %get-tuple-element.38), channel_id=1, source_target_pairs={{0,8},{8,0},{16,24},{24,16},{1,9},{9,1},{17,25},{25,17},{2,10},{10... | collective-permute-start | bytes 2359304 | tf_op jit(solution)/shard_map/ppermute | solution.py:298
  120.9 29.2 %copy-start.4 = (bf16[1,2,128,1536]{3,2,1,0:T(8,128)(2,1)S(1)}, bf16[1,2,128,1536]{3,2,1,0:T(8,128)(2,1)}, u32[]{:S(2)}) copy-start(bf16[1,2,128,1536]{3,2,1,0:T(8,128)(2,1)} %dynamic-slice_select_fusion) | copy-start | bytes 2359300
  120.9 29.2 %collective-permute-start.23 = (bf16[256,1536]{1,0:T(8,128)(2,1)}, bf16[256,1536]{1,0:T(8,128)(2,1)S(1)}, u32[]{:S(2)}, u32[]{:S(2)}) collective-permute-start(bf16[256,1536]{1,0:T(8,128)(2,1)} %get-tuple-element.45), channel_id=1, source_target_pairs={{8,16},{16,8},{9,17},{17,9},{10,18},{18,10},{11,19},{19,11},{12,20... | collective-permute-start | bytes 2359304 | tf_op jit(solution)/shard_map/ppermute | solution.py:298
  150.5 1.8 %collective-permute-start.24 = (bf16[2,64,1536]{2,1,0:T(8,128)(2,1)S(1)}, bf16[2,64,1536]{2,1,0:T(8,128)(2,1)S(1)}, u32[]{:S(2)}, u32[]{:S(2)}) collective-permute-start(bf16[2,64,1536]{2,1,0:T(8,128)(2,1)S(1)} %get-tuple-element.50), channel_id=1, source_target_pairs={{0,1},{1,0},{2,3},{3,2},{4,5},{5,4},{6,7},{7,6},{8,9},{9,8},{10,11... | collective-permute-start | bytes 1179656 | tf_op jit(solution)/shard_map/ppermute | solution.py:197
  (7 other events, 21.1 us)

commit v5 on v3

--- a/solution.py
+++ b/solution.py
@@ -184,8 +184,7 @@
             value = after(value, *late) if late else value
             return [value] + [over_replica(value, 0, dc) for dc in range(1, n_c)]
 
-        whole = spread(scaled, *parts[1:n_c])
-        x_own = after(x_own, *whole[1:])
+        whole = spread(scaled)
         piece, cores = {}, {}
 
         def send_x(q, *late):
@@ -260,20 +259,30 @@
         step_planes(1)
         came_in = [None, tuple(came)]
         send_y(0, *parts, *whole[1:])
+        cut = rows // 2 if rows % 32 == 0 else rows
         for dx in range(1, n_w):
-            cores[0, dx, 0] = spread(piece[0, dx, 0])
+            cores[0, dx, 0] = [piece[0, dx, 0]] + [
+                [over_replica(piece[0, dx, 0][i:i + cut], 0, dc) for i in range(0, rows, cut)] for dc in range(1, n_c)
+            ]
         for q in range(per_w):
             late = tuple(shares[-1:])
             tokens = []
             for dx in range(n_w):
                 for dc in range(n_c):
-                    tokens.append((cores[0, dx, q][dc], w * 0) if dx else (whole[dc], slot_of(w, q)))
+                    held = cores[0, dx, q][dc] if dx else None
+                    for i in range(rows // cut):
+                        if not dx:
+                            tokens.append((whole[dc], slot_of(w, q) * (rows // cut) + i))
+                        elif isinstance(held, list):
+                            tokens.append((held[i], w * 0))
+                        else:
+                            tokens.append((held, w * 0 + i))
             due = late + tuple(parts)
             if q:
                 due = late + tuple(came_in[q]) + tuple(cores[dy, 0, q - 1][-1] for dy in range(1, n_y))
             if q + 1 < per_w:
-                send_x(q + 1, *over_x(q), *whole[1:])
-            share = input_grad(c, n_c, rows, tokens, weight, n_w, n_y, due)
+                send_x(q + 1, *whole[1:])
+            share = input_grad(c, n_c, cut, tokens, weight, n_w, n_y, due)
             shares.append(share)
             for dy in range(1, n_y):
                 cores[dy, 0, q] = spread(piece[dy, 0, q], share)
@@ -311,7 +320,9 @@
                     if dy == dx == 0:
                         s_pieces.append(whole[dc])
                     else:
-                        s_pieces += [cores[dy, dx, q][dc] for q in range(per_w)]
+                        for q in range(per_w):
+                            held = cores[dy, dx, q][dc]
+                            s_pieces += held if isinstance(held, list) else [held]
         places = jnp.stack(places)
         grad_weight = weight_grad(places, pieces, s_pieces, n_h, rows, due)
         came[0] = after(came[0], grad_weight)

time: 154 us -> 150 us (0.974)
  waiting for transfers between devices: 28.3 us -> 23.5 us
    ppermute x3, waiting for transfers between devices: 5.11 us -> 0.01 us  [over_width(): lax.ppermute(value, 'width', [(w, (w + dx) % n_w) for w in range(n_w)])]
    ppermute x14 -> x15, waiting for transfers between devices: 17.8 us -> 19.6 us  [over_replica(): return lax.ppermute(value, 'replica', replica_perm(dy, dc))]
    ppermute x14 -> x15, starting transfers between devices: 7.49 us -> 7.99 us  [over_replica(): return lax.ppermute(value, 'replica', replica_perm(dy, dc))]
  transfers between devices with their start and end apart: 25 -> 26, of which waited for: 7 -> 6; matrix products, arithmetic and copies ran while one was open for 13% -> 13% of each run, Pallas kernels for 43% -> 44%
where the time goes in v5:
time: 150 us; the launch traced here: 149 us
  Pallas kernels  65.8 us (44%)
  starting transfers between devices  32.9 us (22%)
  waiting for transfers between devices  23.5 us (16%)
  other arithmetic  17.6 us (12%)
  local copies, waits for them, and re-layouts  8.03 us (5%)
    pallas_call x2, Pallas kernels, input_grad(): pl.pallas_call(input_grad_kernel, grid_spec=pltpu.PrefetchScalarGridSpec(...  37.7 us
    pallas_call x1, Pallas kernels, weight_grad(): pl.pallas_call(body, grid_spec=pltpu.PrefetchScalarGridSpec(num_scalar_pr...  28.2 us
    ppermute x8, starting transfers between devices, step_planes(): came[kind] = lax.ppermute(sent[kind], 'hidden', pairs[kind])  19.9 us
    ppermute x15, waiting for transfers between devices, over_replica(): return lax.ppermute(value, 'replica', replica_perm(dy, dc))  19.6 us
    ppermute x15, starting transfers between devices, over_replica(): return lax.ppermute(value, 'replica', replica_perm(dy, dc))  7.99 us
    select_n x3, other arithmetic, step_planes(): value = total if value is None else jnp.where(is_input, value, total)  6.31 us
    ppermute x3, starting transfers between devices, over_width(): lax.ppermute(value, 'width', [(w, (w + dx) % n_w) for w in range(n_w)])  4.98 us
    ppermute x8, waiting for transfers between devices, step_planes(): came[kind] = lax.ppermute(sent[kind], 'hidden', pairs[kind])  3.96 us
  transfers between devices with their start and end apart: 26, of which 6 were waited for; matrix products, arithmetic and copies ran while one was open for 13% of the time, Pallas kernels for 44%

profile of v5, /device:TPU:0, one launch (start us, length us, event | category | flops | bytes accessed | tf_op | source)
XLA Modules:
  0.0 148.8 jit_solution(8615308765370014013)
XLA Ops:
  2.1 1.8 %multiply_convert_fusion.refs_0_.refs_1_.refs_7_ = bf16[128,6144]{1,0:T(8,128)(2,1)S(1)} fusion(bf16[128,6144]{1,0:T(8,128)(2,1)} %param.7, f32[128]{0:T(128)S(1)} %fusion.11), kind=kLoop, calls=%fused_computation | loop fusion | flops 2359296 | bytes 3146240 | tf_op jit(solution)/shard_map/convert_element_type | solution.py:179
  4.4 1.3 constant_dynamic-slice_fusion.2
  5.7 2.8 %collective-permute-start.4 = (bf16[64,6144]{1,0:T(8,128)(2,1)}, bf16[64,6144]{1,0:T(8,128)(2,1)}, u32[]{:S(2)}, u32[]{:S(2)}) collective-permute-start(bf16[64,6144]{1,0:T(8,128)(2,1)} %get-tuple-element.22), channel_id=1, source_target_pairs={{0,4},{4,0},{1,5},{5,1},{2,6},{6,2},{3,7},{7,3},{8,12},{12,8},{9,1... | collective-permute-start | bytes 2359304 | tf_op jit(solution)/shard_map/ppermute | solution.py:158
  8.5 1.3 constant_dynamic-slice_fusion.8
  9.9 1.6 %collective-permute-start.2 = (bf16[64,1536]{1,0:T(8,128)(2,1)S(1)}, bf16[64,1536]{1,0:T(8,128)(2,1)S(1)}, u32[]{:S(2)}, u32[]{:S(2)}) collective-permute-start(bf16[64,1536]{1,0:T(8,128)(2,1)S(1)} %get-tuple-element.56), channel_id=1, source_target_pairs={{0,3},{1,2},{2,1},{3,0},{4,7},{5,6},{6,5},{7,4},{8,11},{9,10},{10,... | collective-permute-start | bytes 589832 | tf_op jit(solution)/shard_map/ppermute | solution.py:155
  12.0 4.7 %collective-permute-done.2 = bf16[64,1536]{1,0:T(8,128)(2,1)S(1)} collective-permute-done((bf16[64,1536]{1,0:T(8,128)(2,1)S(1)}, bf16[64,1536]{1,0:T(8,128)(2,1)S(1)}, u32[]{:S(2)}, u32[]{:S(2)}) %collective-permute-start.2) | collective-permute-done | bytes 196640 | tf_op jit(solution)/shard_map/ppermute | solution.py:155
  16.7 4.6 %collective-permute-done.1 = bf16[64,1536]{1,0:T(8,128)(2,1)S(1)} collective-permute-done((bf16[64,1536]{1,0:T(8,128)(2,1)S(1)}, bf16[64,1536]{1,0:T(8,128)(2,1)S(1)}, u32[]{:S(2)}, u32[]{:S(2)}) %collective-permute-start.1) | collective-permute-done | bytes 196640 | tf_op jit(solution)/shard_map/ppermute | solution.py:155
  21.3 0.9 pad_maximum_fusion.refs_0_
  22.3 1.6 %collective-permute-start.8 = (bf16[256,1536]{1,0:T(8,128)(2,1)}, bf16[256,1536]{1,0:T(8,128)(2,1)}, u32[]{:S(2)}, u32[]{:S(2)}) collective-permute-start(bf16[256,1536]{1,0:T(8,128)(2,1)} %pad_maximum_fusion.refs_0_), channel_id=1, source_target_pairs={{8,16},{16,8},{9,17},{17,9},{10,18},{18,10},{11,19},{19,11},{12,20... | collective-permute-start | bytes 2359304 | tf_op jit(solution)/shard_map/ppermute | solution.py:252
  23.9 3.5 %collective-permute-start.7 = (bf16[256,1536]{1,0:T(8,128)(2,1)}, bf16[256,1536]{1,0:T(8,128)(2,1)}, u32[]{:S(2)}, u32[]{:S(2)}) collective-permute-start(bf16[256,1536]{1,0:T(8,128)(2,1)} %pad_maximum_fusion.refs_0_), channel_id=1, source_target_pairs={{0,8},{8,0},{16,24},{24,16},{1,9},{9,1},{17,25},{25,17},{2,10},{10... | collective-permute-start | bytes 2359304 | tf_op jit(solution)/shard_map/ppermute | solution.py:252
  27.9 1.2 fusion.13
  30.9 1.5 %collective-permute-start.9 = (bf16[64,6144]{1,0:T(8,128)(2,1)}, bf16[64,6144]{1,0:T(8,128)(2,1)}, u32[]{:S(2)}, u32[]{:S(2)}) collective-permute-start(bf16[64,6144]{1,0:T(8,128)(2,1)} %get-tuple-element.22), channel_id=1, source_target_pairs={{0,2},{1,3},{2,0},{3,1},{4,6},{5,7},{6,4},{7,5},{8,10},{9,11},{10,... | collective-permute-start | bytes 2359304 | tf_op jit(solution)/shard_map/ppermute | solution.py:155
  33.2 18.8 %shard_map.77 = bf16[2,2,128,1536]{3,2,1,0:T(8,128)(2,1)} custom-call(s32[9]{0:T(128)} %stack.97.first_ref, bf16[128,6144]{1,0:T(8,128)(2,1)} %copy-done, bf16[128,6144]{1,0:T(8,128)(2,1)} %copy-done, bf16[128,6144]{1,0:T(8,128)(2,1)} %copy-done.2, bf16[128,6144]{1,0:T(8,128)(2,1)} %copy-done.2, ...), custom_call_target="tpu_custom_call" | custom-call | tf_op jit(solution)/shard_map/pallas_call | solution.py:120
  52.1 1.5 constant_dynamic-slice_fusion
  53.6 2.5 %bitcast_select_fusion = (bf16[256,1536]{1,0:T(8,128)(2,1)}, bf16[256,1536]{1,0:T(8,128)(2,1)}) fusion(bf16[256,1536]{1,0:T(8,128)(2,1)} %collective-permute-done.8.refs_2_, bf16[1,2,128,1536]{3,2,1,0:T(8,128)(2,1)S(1)} %get-tuple-element.44, pred[]{:T(512)S(6)} %select_n.520, bf16[256,1536]{1,0:T(8,128)(2,1)} %collective-permute-done.7.refs_1_, ...), kind=kLoop, calls=%fused_computation.20 | loop fusion | flops 786432 | bytes 4718594 | tf_op jit(solution)/shard_map/jit(_where)/select_n | solution.py:249
  58.1 3.6 %collective-permute-start.14 = (bf16[256,1536]{1,0:T(8,128)(2,1)}, bf16[256,1536]{1,0:T(8,128)(2,1)}, u32[]{:S(2)}, u32[]{:S(2)}) collective-permute-start(bf16[256,1536]{1,0:T(8,128)(2,1)} %get-tuple-element.29), channel_id=1, source_target_pairs={{0,8},{8,0},{16,24},{24,16},{1,9},{9,1},{17,25},{25,17},{2,10},{10... | collective-permute-start | bytes 2359304 | tf_op jit(solution)/shard_map/ppermute | solution.py:252
  62.3 1.6 %collective-permute-start.19 = (bf16[64,6144]{1,0:T(8,128)(2,1)}, bf16[64,6144]{1,0:T(8,128)(2,1)}, u32[]{:S(2)}, u32[]{:S(2)}) collective-permute-start(bf16[64,6144]{1,0:T(8,128)(2,1)} %collective-permute-done.9.refs_14_), channel_id=1, source_target_pairs={{0,4},{4,0},{1,5},{5,1},{2,6},{6,2},{3,7},{7,3},{8,12},{12,8},{9,1... | collective-permute-start | bytes 2359304 | tf_op jit(solution)/shard_map/ppermute | solution.py:158
  63.9 18.9 %shard_map.78 = bf16[2,2,128,1536]{3,2,1,0:T(8,128)(2,1)} custom-call(s32[9]{0:T(128)} %stack.94.first_ref, bf16[128,6144]{1,0:T(8,128)(2,1)} %copy-done, bf16[128,6144]{1,0:T(8,128)(2,1)} %copy-done, bf16[128,6144]{1,0:T(8,128)(2,1)} %copy-done.2, bf16[128,6144]{1,0:T(8,128)(2,1)} %copy-done.2, ...), custom_call_target="tpu_custom_call" | custom-call | tf_op jit(solution)/shard_map/pallas_call | solution.py:120
  82.8 1.3 collective-permute-start.20
  84.1 1.8 %dynamic-slice_select_fusion.2 = (bf16[1,2,128,1536]{3,2,1,0:T(8,128)(2,1)S(1)}, bf16[1,2,128,1536]{3,2,1,0:T(8,128)(2,1)S(1)}) fusion(bf16[2,2,128,1536]{3,2,1,0:T(8,128)(2,1)S(1)} %copy-done.1, s32[]{:T(128)S(6)} %select_n.539, bf16[2,2,128,1536]{3,2,1,0:T(8,128)(2,1)} %shard_map.78, pred[]{:T(512)S(6)} %eq.98, s32[]{:T(128)S(6)} %select_n.528, pred[]{:T(512)S(6)} %eq.97), kind=kLoop, calls=%fused_computation.24 | loop fusion | flops 786432 | bytes 4718602 | tf_op jit(solution)/shard_map/jit(_where)/select_n | solution.py:224
  85.9 1.2 fusion.6
  87.2 2.7 %fusion.7 = bf16[256,1536]{1,0:T(8,128)(2,1)} fusion(bf16[256,1536]{1,0:T(8,128)(2,1)} %collective-permute-done.14.refs_3_, bf16[1,2,128,1536]{3,2,1,0:T(8,128)(2,1)S(1)} %get-tuple-element.42, pred[]{:T(512)S(6)} %select_n.531), kind=kLoop, calls=%fused_computation.13 | loop fusion | flops 1966080 | bytes 2359297 | tf_op jit(solution)/shard_map/jit(_where)/select_n | solution.py:249
  89.9 1.6 %collective-permute-start.16 = (bf16[256,1536]{1,0:T(8,128)(2,1)}, bf16[256,1536]{1,0:T(8,128)(2,1)}, u32[]{:S(2)}, u32[]{:S(2)}) collective-permute-start(bf16[256,1536]{1,0:T(8,128)(2,1)} %fusion.7), channel_id=1, source_target_pairs={{8,16},{16,8},{9,17},{17,9},{10,18},{18,10},{11,19},{19,11},{12,20... | collective-permute-start | bytes 2359304 | tf_op jit(solution)/shard_map/ppermute | solution.py:252
  92.7 1.0 dynamic-slice_select_fusion.4
  93.6 7.9 %collective-permute-done.20.refs_17_ = bf16[64,6144]{1,0:T(8,128)(2,1)} collective-permute-done((bf16[64,6144]{1,0:T(8,128)(2,1)}, bf16[64,6144]{1,0:T(8,128)(2,1)}, u32[]{:S(2)}, u32[]{:S(2)}) %collective-permute-start.20) | collective-permute-done | bytes 786464 | tf_op jit(solution)/shard_map/ppermute | solution.py:155
  101.6 3.9 %collective-permute-done.15.refs_5_ = bf16[256,1536]{1,0:T(8,128)(2,1)} collective-permute-done((bf16[256,1536]{1,0:T(8,128)(2,1)}, bf16[256,1536]{1,0:T(8,128)(2,1)}, u32[]{:S(2)}, u32[]{:S(2)}) %collective-permute-start.15) | collective-permute-done | bytes 786464 | tf_op jit(solution)/shard_map/ppermute | solution.py:252
  105.7 1.3 fusion
  107.9 1.3 fusion.1
  109.2 7.9 %collective-permute-start.17 = (bf16[256,1536]{1,0:T(8,128)(2,1)S(1)}, bf16[256,1536]{1,0:T(8,128)(2,1)S(1)}, u32[]{:S(2)}, u32[]{:S(2)}) collective-permute-start(bf16[256,1536]{1,0:T(8,128)(2,1)S(1)} %fusion.1), channel_id=1, source_target_pairs={{0,8},{8,0},{16,24},{24,16},{1,9},{9,1},{17,25},{25,17},{2,10},{10... | collective-permute-start | bytes 2359304 | tf_op jit(solution)/shard_map/ppermute | solution.py:252
  117.1 28.2 %shard_map.79 = f32[1536,6144]{1,0:T(8,128)} custom-call(s32[28]{0:T(128)} %stack.112.place_ref, bf16[256,1536]{1,0:T(8,128)(2,1)} %pad_maximum_fusion.refs_0_, bf16[256,1536]{1,0:T(8,128)(2,1)} %collective-permute-done.7.refs_1_, bf16[256,1536]{1,0:T(8,128)(2,1)} %collective-permute-done.8.refs_2_, bf16[256,1536]{1,0:T(8,128)(2,1)} %collective-permute-done.14.refs_3_, ...), custom_call_target="tpu_custom_call" | custom-call | flops 19327352832 | bytes 53477376 | tf_op jit(solution)/shard_map/pallas_call | solution.py:78
  145.8 1.7 %collective-permute-done.25 = bf16[2,64,1536]{2,1,0:T(8,128)(2,1)S(1)} collective-permute-done((bf16[2,64,1536]{2,1,0:T(8,128)(2,1)S(1)}, bf16[2,64,1536]{2,1,0:T(8,128)(2,1)S(1)}, u32[]{:S(2)}, u32[]{:S(2)}) %collective-permute-start.25) | collective-permute-done | bytes 393248 | tf_op jit(solution)/shard_map/ppermute | solution.py:155
  147.9 0.9 pad_maximum_fusion.1
  (69 shorter events, 11.5 us)
Async XLA Ops:
  3.9 23.5 %collective-permute-start.3 = (bf16[128,6144]{1,0:T(8,128)(2,1)S(1)}, bf16[128,6144]{1,0:T(8,128)(2,1)S(1)}, u32[]{:S(2)}, u32[]{:S(2)}) collective-permute-start(bf16[128,6144]{1,0:T(8,128)(2,1)S(1)} %multiply_convert_fusion.refs_0_.refs_1_.refs_7_), channel_id=1, source_target_pairs={{0,1},{1,0},{2,3},{3,2},{4,5},{5,4},{6,7},{7,6},{8,9},{9,8},{10,11... | collective-permute-start | bytes 4718600 | tf_op jit(solution)/shard_map/ppermute | solution.py:155
  5.7 22.2 %collective-permute-start.4 = (bf16[64,6144]{1,0:T(8,128)(2,1)}, bf16[64,6144]{1,0:T(8,128)(2,1)}, u32[]{:S(2)}, u32[]{:S(2)}) collective-permute-start(bf16[64,6144]{1,0:T(8,128)(2,1)} %get-tuple-element.22), channel_id=1, source_target_pairs={{0,4},{4,0},{1,5},{5,1},{2,6},{6,2},{3,7},{7,3},{8,12},{12,8},{9,1... | collective-permute-start | bytes 2359304 | tf_op jit(solution)/shard_map/ppermute | solution.py:158
  9.8 2.2 %collective-permute-start = (bf16[64,1536]{1,0:T(8,128)(2,1)S(1)}, bf16[64,1536]{1,0:T(8,128)(2,1)S(1)}, u32[]{:S(2)}, u32[]{:S(2)}) collective-permute-start(bf16[64,1536]{1,0:T(8,128)(2,1)S(1)} %get-tuple-element.55), channel_id=1, source_target_pairs={{0,1},{1,0},{2,3},{3,2},{4,5},{5,4},{6,7},{7,6},{8,9},{9,8},{10,11... | collective-permute-start | bytes 589832 | tf_op jit(solution)/shard_map/ppermute | solution.py:155
  9.9 6.9 %collective-permute-start.2 = (bf16[64,1536]{1,0:T(8,128)(2,1)S(1)}, bf16[64,1536]{1,0:T(8,128)(2,1)S(1)}, u32[]{:S(2)}, u32[]{:S(2)}) collective-permute-start(bf16[64,1536]{1,0:T(8,128)(2,1)S(1)} %get-tuple-element.56), channel_id=1, source_target_pairs={{0,3},{1,2},{2,1},{3,0},{4,7},{5,6},{6,5},{7,4},{8,11},{9,10},{10,... | collective-permute-start | bytes 589832 | tf_op jit(solution)/shard_map/ppermute | solution.py:155
  11.5 9.8 %collective-permute-start.1 = (bf16[64,1536]{1,0:T(8,128)(2,1)S(1)}, bf16[64,1536]{1,0:T(8,128)(2,1)S(1)}, u32[]{:S(2)}, u32[]{:S(2)}) collective-permute-start(bf16[64,1536]{1,0:T(8,128)(2,1)S(1)} %get-tuple-element.57), channel_id=1, source_target_pairs={{0,2},{1,3},{2,0},{3,1},{4,6},{5,7},{6,4},{7,5},{8,10},{9,11},{10,... | collective-permute-start | bytes 589832 | tf_op jit(solution)/shard_map/ppermute | solution.py:155
  22.3 29.8 %collective-permute-start.8 = (bf16[256,1536]{1,0:T(8,128)(2,1)}, bf16[256,1536]{1,0:T(8,128)(2,1)}, u32[]{:S(2)}, u32[]{:S(2)}) collective-permute-start(bf16[256,1536]{1,0:T(8,128)(2,1)} %pad_maximum_fusion.refs_0_), channel_id=1, source_target_pairs={{8,16},{16,8},{9,17},{17,9},{10,18},{18,10},{11,19},{19,11},{12,20... | collective-permute-start | bytes 2359304 | tf_op jit(solution)/shard_map/ppermute | solution.py:252
  23.9 28.2 %collective-permute-start.7 = (bf16[256,1536]{1,0:T(8,128)(2,1)}, bf16[256,1536]{1,0:T(8,128)(2,1)}, u32[]{:S(2)}, u32[]{:S(2)}) collective-permute-start(bf16[256,1536]{1,0:T(8,128)(2,1)} %pad_maximum_fusion.refs_0_), channel_id=1, source_target_pairs={{0,8},{8,0},{16,24},{24,16},{1,9},{9,1},{17,25},{25,17},{2,10},{10... | collective-permute-start | bytes 2359304 | tf_op jit(solution)/shard_map/ppermute | solution.py:252
  27.4 5.0 %copy-start.2 = (bf16[128,6144]{1,0:T(8,128)(2,1)}, bf16[128,6144]{1,0:T(8,128)(2,1)S(1)}, u32[]{:S(2)}) copy-start(bf16[128,6144]{1,0:T(8,128)(2,1)S(1)} %collective-permute-done.3.refs_2_.refs_3_.refs_10_) | copy-start | bytes 4718596
  27.4 24.7 %collective-permute-start.11 = (bf16[64,6144]{1,0:T(8,128)(2,1)}, bf16[64,6144]{1,0:T(8,128)(2,1)}, u32[]{:S(2)}, u32[]{:S(2)}) collective-permute-start(bf16[64,6144]{1,0:T(8,128)(2,1)} %get-tuple-element.35), channel_id=1, source_target_pairs={{0,4},{4,0},{1,5},{5,1},{2,6},{6,2},{3,7},{7,3},{8,12},{12,8},{9,1... | collective-permute-start | bytes 2359304 | tf_op jit(solution)/shard_map/ppermute | solution.py:158
  29.1 1.8 %collective-permute-start.6 = (bf16[32,6144]{1,0:T(8,128)(2,1)S(1)}, bf16[32,6144]{1,0:T(8,128)(2,1)S(1)}, u32[]{:S(2)}, u32[]{:S(2)}) collective-permute-start(bf16[32,6144]{1,0:T(8,128)(2,1)S(1)} %get-tuple-element.52), channel_id=1, source_target_pairs={{0,1},{1,0},{2,3},{3,2},{4,5},{5,4},{6,7},{7,6},{8,9},{9,8},{10,11... | collective-permute-start | bytes 1179656 | tf_op jit(solution)/shard_map/ppermute | solution.py:155
  29.2 3.2 %collective-permute-start.5 = (bf16[32,6144]{1,0:T(8,128)(2,1)S(1)}, bf16[32,6144]{1,0:T(8,128)(2,1)S(1)}, u32[]{:S(2)}, u32[]{:S(2)}) collective-permute-start(bf16[32,6144]{1,0:T(8,128)(2,1)S(1)} %get-tuple-element.53), channel_id=1, source_target_pairs={{0,1},{1,0},{2,3},{3,2},{4,5},{5,4},{6,7},{7,6},{8,9},{9,8},{10,11... | collective-permute-start | bytes 1179656 | tf_op jit(solution)/shard_map/ppermute | solution.py:155
  30.9 25.2 %collective-permute-start.9 = (bf16[64,6144]{1,0:T(8,128)(2,1)}, bf16[64,6144]{1,0:T(8,128)(2,1)}, u32[]{:S(2)}, u32[]{:S(2)}) collective-permute-start(bf16[64,6144]{1,0:T(8,128)(2,1)} %get-tuple-element.22), channel_id=1, source_target_pairs={{0,2},{1,3},{2,0},{3,1},{4,6},{5,7},{6,4},{7,5},{8,10},{9,11},{10,... | collective-permute-start | bytes 2359304 | tf_op jit(solution)/shard_map/ppermute | solution.py:155
  52.1 5.3 %collective-permute-start.12 = (bf16[64,6144]{1,0:T(8,128)(2,1)}, bf16[64,6144]{1,0:T(8,128)(2,1)S(1)}, u32[]{:S(2)}, u32[]{:S(2)}) collective-permute-start(bf16[64,6144]{1,0:T(8,128)(2,1)} %collective-permute-done.11.refs_4_.refs_5_.refs_9_), channel_id=1, source_target_pairs={{0,1},{1,0},{2,3},{3,2},{4,5},{5,4},{6,7},{7,6},{8,9},{9,8},{10,11... | collective-permute-start | bytes 2359304 | tf_op jit(solution)/shard_map/ppermute | solution.py:155
  56.1 7.8 %collective-permute-start.10 = (bf16[64,6144]{1,0:T(8,128)(2,1)}, bf16[64,6144]{1,0:T(8,128)(2,1)}, u32[]{:S(2)}, u32[]{:S(2)}) collective-permute-start(bf16[64,6144]{1,0:T(8,128)(2,1)} %collective-permute-done.9.refs_14_), channel_id=1, source_target_pairs={{0,1},{1,0},{2,3},{3,2},{4,5},{5,4},{6,7},{7,6},{8,9},{9,8},{10,11... | collective-permute-start | bytes 2359304 | tf_op jit(solution)/shard_map/ppermute | solution.py:155
  56.6 26.2 %collective-permute-start.18 = (bf16[64,6144]{1,0:T(8,128)(2,1)}, bf16[64,6144]{1,0:T(8,128)(2,1)}, u32[]{:S(2)}, u32[]{:S(2)}) collective-permute-start(bf16[64,6144]{1,0:T(8,128)(2,1)} %get-tuple-element.35), channel_id=1, source_target_pairs={{0,2},{1,3},{2,0},{3,1},{4,6},{5,7},{6,4},{7,5},{8,10},{9,11},{10,... | collective-permute-start | bytes 2359304 | tf_op jit(solution)/shard_map/ppermute | solution.py:155
  57.3 6.6 %copy-start.4 = (bf16[64,6144]{1,0:T(8,128)(2,1)}, bf16[64,6144]{1,0:T(8,128)(2,1)S(1)}, u32[]{:S(2)}) copy-start(bf16[64,6144]{1,0:T(8,128)(2,1)S(1)} %collective-permute-done.12.refs_6_.refs_7_.refs_13_) | copy-start | bytes 2359300
  57.3 26.7 %collective-permute-start.13 = (bf16[256,1536]{1,0:T(8,128)(2,1)}, bf16[256,1536]{1,0:T(8,128)(2,1)S(1)}, u32[]{:S(2)}, u32[]{:S(2)}) collective-permute-start(bf16[256,1536]{1,0:T(8,128)(2,1)} %get-tuple-element.28), channel_id=1, source_target_pairs={{8,16},{16,8},{9,17},{17,9},{10,18},{18,10},{11,19},{19,11},{12,20... | collective-permute-start | bytes 2359304 | tf_op jit(solution)/shard_map/ppermute | solution.py:252
  58.1 26.0 %collective-permute-start.14 = (bf16[256,1536]{1,0:T(8,128)(2,1)}, bf16[256,1536]{1,0:T(8,128)(2,1)}, u32[]{:S(2)}, u32[]{:S(2)}) collective-permute-start(bf16[256,1536]{1,0:T(8,128)(2,1)} %get-tuple-element.29), channel_id=1, source_target_pairs={{0,8},{8,0},{16,24},{24,16},{1,9},{9,1},{17,25},{25,17},{2,10},{10... | collective-permute-start | bytes 2359304 | tf_op jit(solution)/shard_map/ppermute | solution.py:252
  62.3 21.8 %copy-start.1 = (bf16[2,2,128,1536]{3,2,1,0:T(8,128)(2,1)S(1)}, bf16[2,2,128,1536]{3,2,1,0:T(8,128)(2,1)}, u32[]{:S(2)}) copy-start(bf16[2,2,128,1536]{3,2,1,0:T(8,128)(2,1)} %shard_map.77) | copy-start | bytes 4718596
  62.3 29.9 %collective-permute-start.19 = (bf16[64,6144]{1,0:T(8,128)(2,1)}, bf16[64,6144]{1,0:T(8,128)(2,1)}, u32[]{:S(2)}, u32[]{:S(2)}) collective-permute-start(bf16[64,6144]{1,0:T(8,128)(2,1)} %collective-permute-done.9.refs_14_), channel_id=1, source_target_pairs={{0,4},{4,0},{1,5},{5,1},{2,6},{6,2},{3,7},{7,3},{8,12},{12,8},{9,1... | collective-permute-start | bytes 2359304 | tf_op jit(solution)/shard_map/ppermute | solution.py:158
  82.8 18.8 %collective-permute-start.20 = (bf16[64,6144]{1,0:T(8,128)(2,1)}, bf16[64,6144]{1,0:T(8,128)(2,1)}, u32[]{:S(2)}, u32[]{:S(2)}) collective-permute-start(bf16[64,6144]{1,0:T(8,128)(2,1)} %collective-permute-done.11.refs_4_.refs_5_.refs_9_), channel_id=1, source_target_pairs={{0,2},{1,3},{2,0},{3,1},{4,6},{5,7},{6,4},{7,5},{8,10},{9,11},{10,... | collective-permute-start | bytes 2359304 | tf_op jit(solution)/shard_map/ppermute | solution.py:155
  84.1 1.8 %copy-start.6 = (bf16[256,1536]{1,0:T(8,128)(2,1)}, bf16[256,1536]{1,0:T(8,128)(2,1)S(1)}, u32[]{:S(2)}) copy-start(bf16[256,1536]{1,0:T(8,128)(2,1)S(1)} %collective-permute-done.13.refs_4_) | copy-start | bytes 2359300
  87.1 18.4 %collective-permute-start.15 = (bf16[256,1536]{1,0:T(8,128)(2,1)}, bf16[256,1536]{1,0:T(8,128)(2,1)}, u32[]{:S(2)}, u32[]{:S(2)}) collective-permute-start(bf16[256,1536]{1,0:T(8,128)(2,1)} %fusion.6), channel_id=1, source_target_pairs={{0,8},{8,0},{16,24},{24,16},{1,9},{9,1},{17,25},{25,17},{2,10},{10... | collective-permute-start | bytes 2359304 | tf_op jit(solution)/shard_map/ppermute | solution.py:252
  87.2 5.4 %copy-start.3 = (bf16[2,2,128,1536]{3,2,1,0:T(8,128)(2,1)S(1)}, bf16[2,2,128,1536]{3,2,1,0:T(8,128)(2,1)}, u32[]{:S(2)}) copy-start(bf16[2,2,128,1536]{3,2,1,0:T(8,128)(2,1)} %shard_map.78) | copy-start | bytes 4718596
  89.9 15.6 %collective-permute-start.16 = (bf16[256,1536]{1,0:T(8,128)(2,1)}, bf16[256,1536]{1,0:T(8,128)(2,1)}, u32[]{:S(2)}, u32[]{:S(2)}) collective-permute-start(bf16[256,1536]{1,0:T(8,128)(2,1)} %fusion.7), channel_id=1, source_target_pairs={{8,16},{16,8},{9,17},{17,9},{10,18},{18,10},{11,19},{19,11},{12,20... | collective-permute-start | bytes 2359304 | tf_op jit(solution)/shard_map/ppermute | solution.py:252
  92.1 25.0 %collective-permute-start.21 = (bf16[64,6144]{1,0:T(8,128)(2,1)}, bf16[64,6144]{1,0:T(8,128)(2,1)}, u32[]{:S(2)}, u32[]{:S(2)}) collective-permute-start(bf16[64,6144]{1,0:T(8,128)(2,1)} %collective-permute-done.18.refs_15_), channel_id=1, source_target_pairs={{0,1},{1,0},{2,3},{3,2},{4,5},{5,4},{6,7},{7,6},{8,9},{9,8},{10,11... | collective-permute-start | bytes 2359304 | tf_op jit(solution)/shard_map/ppermute | solution.py:155
  92.2 25.0 %collective-permute-start.22 = (bf16[64,6144]{1,0:T(8,128)(2,1)}, bf16[64,6144]{1,0:T(8,128)(2,1)}, u32[]{:S(2)}, u32[]{:S(2)}) collective-permute-start(bf16[64,6144]{1,0:T(8,128)(2,1)} %collective-permute-done.19.refs_16_), channel_id=1, source_target_pairs={{0,1},{1,0},{2,3},{3,2},{4,5},{5,4},{6,7},{7,6},{8,9},{9,8},{10,11... | collective-permute-start | bytes 2359304 | tf_op jit(solution)/shard_map/ppermute | solution.py:155
  101.6 15.6 %collective-permute-start.23 = (bf16[64,6144]{1,0:T(8,128)(2,1)}, bf16[64,6144]{1,0:T(8,128)(2,1)}, u32[]{:S(2)}, u32[]{:S(2)}) collective-permute-start(bf16[64,6144]{1,0:T(8,128)(2,1)} %collective-permute-done.20.refs_17_), channel_id=1, source_target_pairs={{0,1},{1,0},{2,3},{3,2},{4,5},{5,4},{6,7},{7,6},{8,9},{9,8},{10,11... | collective-permute-start | bytes 2359304 | tf_op jit(solution)/shard_map/ppermute | solution.py:155
  107.0 38.3 %collective-permute-start.24 = (bf16[256,1536]{1,0:T(8,128)(2,1)S(1)}, bf16[256,1536]{1,0:T(8,128)(2,1)S(1)}, u32[]{:S(2)}, u32[]{:S(2)}) collective-permute-start(bf16[256,1536]{1,0:T(8,128)(2,1)S(1)} %fusion), channel_id=1, source_target_pairs={{8,16},{16,8},{9,17},{17,9},{10,18},{18,10},{11,19},{19,11},{12,20... | collective-permute-start | bytes 2359304 | tf_op jit(solution)/shard_map/ppermute | solution.py:252
  109.2 36.1 %copy-start.5 = (bf16[1,2,128,1536]{3,2,1,0:T(8,128)(2,1)S(1)}, bf16[1,2,128,1536]{3,2,1,0:T(8,128)(2,1)}, u32[]{:S(2)}) copy-start(bf16[1,2,128,1536]{3,2,1,0:T(8,128)(2,1)} %dynamic-slice_select_fusion.4) | copy-start | bytes 2359300
  109.2 36.0 %collective-permute-start.17 = (bf16[256,1536]{1,0:T(8,128)(2,1)S(1)}, bf16[256,1536]{1,0:T(8,128)(2,1)S(1)}, u32[]{:S(2)}, u32[]{:S(2)}) collective-permute-start(bf16[256,1536]{1,0:T(8,128)(2,1)S(1)} %fusion.1), channel_id=1, source_target_pairs={{0,8},{8,0},{16,24},{24,16},{1,9},{9,1},{17,25},{25,17},{2,10},{10... | collective-permute-start | bytes 2359304 | tf_op jit(solution)/shard_map/ppermute | solution.py:252
  145.7 1.8 %collective-permute-start.25 = (bf16[2,64,1536]{2,1,0:T(8,128)(2,1)S(1)}, bf16[2,64,1536]{2,1,0:T(8,128)(2,1)S(1)}, u32[]{:S(2)}, u32[]{:S(2)}) collective-permute-start(bf16[2,64,1536]{2,1,0:T(8,128)(2,1)S(1)} %get-tuple-element.50), channel_id=1, source_target_pairs={{0,1},{1,0},{2,3},{3,2},{4,5},{5,4},{6,7},{7,6},{8,9},{9,8},{10,11... | collective-permute-start | bytes 1179656 | tf_op jit(solution)/shard_map/ppermute | solution.py:155
  (3 other events, 4.1 us)

commit v6 on v5

--- a/solution.py
+++ b/solution.py
@@ -113,7 +113,7 @@
     width = d // n_c
     n = rows * len(pieces)
     part = width // parts
-    block = next(b for b in (512, 256, 128, part) if part % b == 0)
+    block = next(b for b in (768, 512, 256, 128, part) if part % b == 0)
     per_part = part // block
     steps = width // block
     first = jnp.stack([core * steps] + [index for _, index in pieces]).astype(jnp.int32)
@@ -244,7 +244,7 @@
                 if step:
                     total = share_of(jnp.where(to_right, h + apart, h - apart), choices, come)
                     if step > 1:
-                        total = (total.astype(jnp.float32) + come[1 - kind].astype(jnp.float32)).astype(jnp.bfloat16)
+                        total = total + come[1 - kind]
                     is_input = jnp.where(to_right, h >= step, h < apart)
                     value = total if value is None else jnp.where(is_input, value, total)
                 sent.append(after(value, *late) if late else value)

time: 150 us -> 148 us (0.987)
    convert_element_type x2 -> x0, other arithmetic: 2.65 us -> none  [step_planes(): (total.astype(jnp.float32) + come[1 - kind].astype(jnp.float32)).astype(j...]
    add x0 -> x2, other arithmetic: none -> 2.43 us  [step_planes(): total = total + come[1 - kind]]
where the time goes in v6:
time: 148 us; the launch traced here: 147 us
  Pallas kernels  64.8 us (44%)
  starting transfers between devices  32.4 us (22%)
  waiting for transfers between devices  24.1 us (16%)
  other arithmetic  16.8 us (11%)
  local copies, waits for them, and re-layouts  8.03 us (5%)
    pallas_call x2, Pallas kernels, input_grad(): pl.pallas_call(input_grad_kernel, grid_spec=pltpu.PrefetchScalarGridSpec(...  36.7 us
    pallas_call x1, Pallas kernels, weight_grad(): pl.pallas_call(body, grid_spec=pltpu.PrefetchScalarGridSpec(num_scalar_pr...  28.2 us
    ppermute x15, waiting for transfers between devices, over_replica(): return lax.ppermute(value, 'replica', replica_perm(dy, dc))  20.4 us
    ppermute x8, starting transfers between devices, step_planes(): came[kind] = lax.ppermute(sent[kind], 'hidden', pairs[kind])  19.5 us
    ppermute x15, starting transfers between devices, over_replica(): return lax.ppermute(value, 'replica', replica_perm(dy, dc))  7.99 us
    select_n x3, other arithmetic, step_planes(): value = total if value is None else jnp.where(is_input, value, total)  5.72 us
    ppermute x3, starting transfers between devices, over_width(): lax.ppermute(value, 'width', [(w, (w + dx) % n_w) for w in range(n_w)])  4.97 us
    ppermute x8, waiting for transfers between devices, step_planes(): came[kind] = lax.ppermute(sent[kind], 'hidden', pairs[kind])  3.7 us
  transfers between devices with their start and end apart: 26, of which 6 were waited for; matrix products, arithmetic and copies ran while one was open for 13% of the time, Pallas kernels for 44%

profile of v6, /device:TPU:0, one launch (start us, length us, event | category | flops | bytes accessed | tf_op | source)
XLA Modules:
  0.0 147.1 jit_solution(13371352759012803538)
XLA Ops:
  2.1 1.8 %multiply_convert_fusion.refs_0_.refs_1_.refs_7_ = bf16[128,6144]{1,0:T(8,128)(2,1)S(1)} fusion(bf16[128,6144]{1,0:T(8,128)(2,1)} %param.7, f32[128]{0:T(128)S(1)} %fusion.5), kind=kLoop, calls=%fused_computation | loop fusion | flops 2359296 | bytes 3146240 | tf_op jit(solution)/shard_map/convert_element_type | solution.py:179
  4.4 1.3 constant_dynamic-slice_fusion.2
  5.7 2.8 %collective-permute-start.4 = (bf16[64,6144]{1,0:T(8,128)(2,1)}, bf16[64,6144]{1,0:T(8,128)(2,1)}, u32[]{:S(2)}, u32[]{:S(2)}) collective-permute-start(bf16[64,6144]{1,0:T(8,128)(2,1)} %get-tuple-element.22), channel_id=1, source_target_pairs={{0,4},{4,0},{1,5},{5,1},{2,6},{6,2},{3,7},{7,3},{8,12},{12,8},{9,1... | collective-permute-start | bytes 2359304 | tf_op jit(solution)/shard_map/ppermute | solution.py:158
  8.5 1.3 constant_dynamic-slice_fusion.8
  9.9 1.6 %collective-permute-start.2 = (bf16[64,1536]{1,0:T(8,128)(2,1)S(1)}, bf16[64,1536]{1,0:T(8,128)(2,1)S(1)}, u32[]{:S(2)}, u32[]{:S(2)}) collective-permute-start(bf16[64,1536]{1,0:T(8,128)(2,1)S(1)} %get-tuple-element.56), channel_id=1, source_target_pairs={{0,3},{1,2},{2,1},{3,0},{4,7},{5,6},{6,5},{7,4},{8,11},{9,10},{10,... | collective-permute-start | bytes 589832 | tf_op jit(solution)/shard_map/ppermute | solution.py:155
  12.0 4.7 %collective-permute-done.2 = bf16[64,1536]{1,0:T(8,128)(2,1)S(1)} collective-permute-done((bf16[64,1536]{1,0:T(8,128)(2,1)S(1)}, bf16[64,1536]{1,0:T(8,128)(2,1)S(1)}, u32[]{:S(2)}, u32[]{:S(2)}) %collective-permute-start.2) | collective-permute-done | bytes 196640 | tf_op jit(solution)/shard_map/ppermute | solution.py:155
  16.7 4.6 %collective-permute-done.1 = bf16[64,1536]{1,0:T(8,128)(2,1)S(1)} collective-permute-done((bf16[64,1536]{1,0:T(8,128)(2,1)S(1)}, bf16[64,1536]{1,0:T(8,128)(2,1)S(1)}, u32[]{:S(2)}, u32[]{:S(2)}) %collective-permute-start.1) | collective-permute-done | bytes 196640 | tf_op jit(solution)/shard_map/ppermute | solution.py:155
  21.3 0.9 pad_maximum_fusion.refs_0_
  22.3 1.6 %collective-permute-start.8 = (bf16[256,1536]{1,0:T(8,128)(2,1)}, bf16[256,1536]{1,0:T(8,128)(2,1)}, u32[]{:S(2)}, u32[]{:S(2)}) collective-permute-start(bf16[256,1536]{1,0:T(8,128)(2,1)} %pad_maximum_fusion.refs_0_), channel_id=1, source_target_pairs={{8,16},{16,8},{9,17},{17,9},{10,18},{18,10},{11,19},{19,11},{12,20... | collective-permute-start | bytes 2359304 | tf_op jit(solution)/shard_map/ppermute | solution.py:252
  23.9 3.5 %collective-permute-start.7 = (bf16[256,1536]{1,0:T(8,128)(2,1)}, bf16[256,1536]{1,0:T(8,128)(2,1)}, u32[]{:S(2)}, u32[]{:S(2)}) collective-permute-start(bf16[256,1536]{1,0:T(8,128)(2,1)} %pad_maximum_fusion.refs_0_), channel_id=1, source_target_pairs={{0,8},{8,0},{16,24},{24,16},{1,9},{9,1},{17,25},{25,17},{2,10},{10... | collective-permute-start | bytes 2359304 | tf_op jit(solution)/shard_map/ppermute | solution.py:252
  27.9 1.2 fusion.7
  30.9 1.5 %collective-permute-start.9 = (bf16[64,6144]{1,0:T(8,128)(2,1)}, bf16[64,6144]{1,0:T(8,128)(2,1)}, u32[]{:S(2)}, u32[]{:S(2)}) collective-permute-start(bf16[64,6144]{1,0:T(8,128)(2,1)} %get-tuple-element.22), channel_id=1, source_target_pairs={{0,2},{1,3},{2,0},{3,1},{4,6},{5,7},{6,4},{7,5},{8,10},{9,11},{10,... | collective-permute-start | bytes 2359304 | tf_op jit(solution)/shard_map/ppermute | solution.py:155
  33.2 18.3 %shard_map.77 = bf16[2,2,128,1536]{3,2,1,0:T(8,128)(2,1)} custom-call(s32[9]{0:T(128)} %stack.97.first_ref, bf16[128,6144]{1,0:T(8,128)(2,1)} %copy-done, bf16[128,6144]{1,0:T(8,128)(2,1)} %copy-done, bf16[128,6144]{1,0:T(8,128)(2,1)} %copy-done.2, bf16[128,6144]{1,0:T(8,128)(2,1)} %copy-done.2, ...), custom_call_target="tpu_custom_call" | custom-call | tf_op jit(solution)/shard_map/pallas_call | solution.py:120
  51.6 1.5 %constant_dynamic-slice_fusion = (bf16[1,2,128,1536]{3,2,1,0:T(8,128)(2,1)S(1)}, bf16[1,2,128,1536]{3,2,1,0:T(8,128)(2,1)S(1)}) fusion(bf16[2,2,128,1536]{3,2,1,0:T(8,128)(2,1)} %shard_map.77, s32[]{:T(128)S(6)} %select_n.533, s32[]{:T(128)S(6)} %select_n.521), kind=kLoop, calls=%fused_computation.31 | loop fusion | bytes 3145736 | tf_op jit(solution)/shard_map/jit(dynamic_index_in_dim)/dynamic_slice | solution.py:223
  53.1 2.5 %bitcast_select_fusion = (bf16[256,1536]{1,0:T(8,128)(2,1)}, bf16[256,1536]{1,0:T(8,128)(2,1)}) fusion(bf16[256,1536]{1,0:T(8,128)(2,1)} %collective-permute-done.8.refs_2_, bf16[1,2,128,1536]{3,2,1,0:T(8,128)(2,1)S(1)} %get-tuple-element.44, pred[]{:T(512)S(6)} %select_n.528, bf16[256,1536]{1,0:T(8,128)(2,1)} %collective-permute-done.7.refs_1_, ...), kind=kLoop, calls=%fused_computation.14 | loop fusion | flops 786432 | bytes 4718594 | tf_op jit(solution)/shard_map/jit(_where)/select_n | solution.py:249
  57.5 3.6 %collective-permute-start.14 = (bf16[256,1536]{1,0:T(8,128)(2,1)}, bf16[256,1536]{1,0:T(8,128)(2,1)}, u32[]{:S(2)}, u32[]{:S(2)}) collective-permute-start(bf16[256,1536]{1,0:T(8,128)(2,1)} %get-tuple-element.29), channel_id=1, source_target_pairs={{0,8},{8,0},{16,24},{24,16},{1,9},{9,1},{17,25},{25,17},{2,10},{10... | collective-permute-start | bytes 2359304 | tf_op jit(solution)/shard_map/ppermute | solution.py:252
  61.8 1.6 %collective-permute-start.19 = (bf16[64,6144]{1,0:T(8,128)(2,1)}, bf16[64,6144]{1,0:T(8,128)(2,1)}, u32[]{:S(2)}, u32[]{:S(2)}) collective-permute-start(bf16[64,6144]{1,0:T(8,128)(2,1)} %collective-permute-done.9.refs_14_), channel_id=1, source_target_pairs={{0,4},{4,0},{1,5},{5,1},{2,6},{6,2},{3,7},{7,3},{8,12},{12,8},{9,1... | collective-permute-start | bytes 2359304 | tf_op jit(solution)/shard_map/ppermute | solution.py:158
  63.4 18.4 %shard_map.78 = bf16[2,2,128,1536]{3,2,1,0:T(8,128)(2,1)} custom-call(s32[9]{0:T(128)} %stack.94.first_ref, bf16[128,6144]{1,0:T(8,128)(2,1)} %copy-done, bf16[128,6144]{1,0:T(8,128)(2,1)} %copy-done, bf16[128,6144]{1,0:T(8,128)(2,1)} %copy-done.2, bf16[128,6144]{1,0:T(8,128)(2,1)} %copy-done.2, ...), custom_call_target="tpu_custom_call" | custom-call | tf_op jit(solution)/shard_map/pallas_call | solution.py:120
  81.8 1.3 collective-permute-start.20
  83.1 1.8 %dynamic-slice_select_fusion.2 = (bf16[1,2,128,1536]{3,2,1,0:T(8,128)(2,1)S(1)}, bf16[1,2,128,1536]{3,2,1,0:T(8,128)(2,1)S(1)}) fusion(bf16[2,2,128,1536]{3,2,1,0:T(8,128)(2,1)S(1)} %copy-done.1, s32[]{:T(128)S(6)} %select_n.548, bf16[2,2,128,1536]{3,2,1,0:T(8,128)(2,1)} %shard_map.78, pred[]{:T(512)S(6)} %eq.98, s32[]{:T(128)S(6)} %select_n.536, pred[]{:T(512)S(6)} %eq.97), kind=kLoop, calls=%fused_computation.18 | loop fusion | flops 786432 | bytes 4718602 | tf_op jit(solution)/shard_map/jit(_where)/select_n | solution.py:224
  84.9 1.0 add_select_fusion.1
  86.1 2.2 %add_select_fusion = bf16[256,1536]{1,0:T(8,128)(2,1)} fusion(bf16[256,1536]{1,0:T(8,128)(2,1)} %collective-permute-done.14.refs_3_, bf16[1,2,128,1536]{3,2,1,0:T(8,128)(2,1)S(1)} %get-tuple-element.42, pred[]{:T(512)S(6)} %select_n.540), kind=kLoop, calls=%fused_computation.4 | loop fusion | flops 786432 | bytes 2359297 | tf_op jit(solution)/shard_map/jit(_where)/select_n | solution.py:249
  88.3 1.6 %collective-permute-start.16 = (bf16[256,1536]{1,0:T(8,128)(2,1)}, bf16[256,1536]{1,0:T(8,128)(2,1)}, u32[]{:S(2)}, u32[]{:S(2)}) collective-permute-start(bf16[256,1536]{1,0:T(8,128)(2,1)} %add_select_fusion), channel_id=1, source_target_pairs={{8,16},{16,8},{9,17},{17,9},{10,18},{18,10},{11,19},{19,11},{12,20... | collective-permute-start | bytes 2359304 | tf_op jit(solution)/shard_map/ppermute | solution.py:252
  91.1 1.0 dynamic-slice_select_fusion.4
  92.0 8.7 %collective-permute-done.20.refs_17_ = bf16[64,6144]{1,0:T(8,128)(2,1)} collective-permute-done((bf16[64,6144]{1,0:T(8,128)(2,1)}, bf16[64,6144]{1,0:T(8,128)(2,1)}, u32[]{:S(2)}, u32[]{:S(2)}) %collective-permute-start.20) | collective-permute-done | bytes 786464 | tf_op jit(solution)/shard_map/ppermute | solution.py:155
  100.8 3.7 %collective-permute-done.15.refs_5_ = bf16[256,1536]{1,0:T(8,128)(2,1)} collective-permute-done((bf16[256,1536]{1,0:T(8,128)(2,1)}, bf16[256,1536]{1,0:T(8,128)(2,1)}, u32[]{:S(2)}, u32[]{:S(2)}) %collective-permute-start.15) | collective-permute-done | bytes 786464 | tf_op jit(solution)/shard_map/ppermute | solution.py:252
  104.6 1.2 bitcast_add_fusion
  106.7 1.2 bitcast_add_fusion.1
  108.0 7.4 %collective-permute-start.17 = (bf16[256,1536]{1,0:T(8,128)(2,1)S(1)}, bf16[256,1536]{1,0:T(8,128)(2,1)S(1)}, u32[]{:S(2)}, u32[]{:S(2)}) collective-permute-start(bf16[256,1536]{1,0:T(8,128)(2,1)S(1)} %bitcast_add_fusion.1), channel_id=1, source_target_pairs={{0,8},{8,0},{16,24},{24,16},{1,9},{9,1},{17,25},{25,17},{2,10},{10... | collective-permute-start | bytes 2359304 | tf_op jit(solution)/shard_map/ppermute | solution.py:252
  115.4 28.2 %shard_map.79 = f32[1536,6144]{1,0:T(8,128)} custom-call(s32[28]{0:T(128)} %stack.112.place_ref, bf16[256,1536]{1,0:T(8,128)(2,1)} %pad_maximum_fusion.refs_0_, bf16[256,1536]{1,0:T(8,128)(2,1)} %collective-permute-done.7.refs_1_, bf16[256,1536]{1,0:T(8,128)(2,1)} %collective-permute-done.8.refs_2_, bf16[256,1536]{1,0:T(8,128)(2,1)} %collective-permute-done.14.refs_3_, ...), custom_call_target="tpu_custom_call" | custom-call | flops 19327352832 | bytes 53477376 | tf_op jit(solution)/shard_map/pallas_call | solution.py:78
  144.1 1.7 %collective-permute-done.25 = bf16[2,64,1536]{2,1,0:T(8,128)(2,1)S(1)} collective-permute-done((bf16[2,64,1536]{2,1,0:T(8,128)(2,1)S(1)}, bf16[2,64,1536]{2,1,0:T(8,128)(2,1)S(1)}, u32[]{:S(2)}, u32[]{:S(2)}) %collective-permute-start.25) | collective-permute-done | bytes 393248 | tf_op jit(solution)/shard_map/ppermute | solution.py:155
  146.2 0.9 pad_maximum_fusion.1
  (69 shorter events, 11.5 us)
Async XLA Ops:
  3.9 23.5 %collective-permute-start.3 = (bf16[128,6144]{1,0:T(8,128)(2,1)S(1)}, bf16[128,6144]{1,0:T(8,128)(2,1)S(1)}, u32[]{:S(2)}, u32[]{:S(2)}) collective-permute-start(bf16[128,6144]{1,0:T(8,128)(2,1)S(1)} %multiply_convert_fusion.refs_0_.refs_1_.refs_7_), channel_id=1, source_target_pairs={{0,1},{1,0},{2,3},{3,2},{4,5},{5,4},{6,7},{7,6},{8,9},{9,8},{10,11... | collective-permute-start | bytes 4718600 | tf_op jit(solution)/shard_map/ppermute | solution.py:155
  5.7 22.2 %collective-permute-start.4 = (bf16[64,6144]{1,0:T(8,128)(2,1)}, bf16[64,6144]{1,0:T(8,128)(2,1)}, u32[]{:S(2)}, u32[]{:S(2)}) collective-permute-start(bf16[64,6144]{1,0:T(8,128)(2,1)} %get-tuple-element.22), channel_id=1, source_target_pairs={{0,4},{4,0},{1,5},{5,1},{2,6},{6,2},{3,7},{7,3},{8,12},{12,8},{9,1... | collective-permute-start | bytes 2359304 | tf_op jit(solution)/shard_map/ppermute | solution.py:158
  9.8 2.2 %collective-permute-start = (bf16[64,1536]{1,0:T(8,128)(2,1)S(1)}, bf16[64,1536]{1,0:T(8,128)(2,1)S(1)}, u32[]{:S(2)}, u32[]{:S(2)}) collective-permute-start(bf16[64,1536]{1,0:T(8,128)(2,1)S(1)} %get-tuple-element.55), channel_id=1, source_target_pairs={{0,1},{1,0},{2,3},{3,2},{4,5},{5,4},{6,7},{7,6},{8,9},{9,8},{10,11... | collective-permute-start | bytes 589832 | tf_op jit(solution)/shard_map/ppermute | solution.py:155
  9.9 6.9 %collective-permute-start.2 = (bf16[64,1536]{1,0:T(8,128)(2,1)S(1)}, bf16[64,1536]{1,0:T(8,128)(2,1)S(1)}, u32[]{:S(2)}, u32[]{:S(2)}) collective-permute-start(bf16[64,1536]{1,0:T(8,128)(2,1)S(1)} %get-tuple-element.56), channel_id=1, source_target_pairs={{0,3},{1,2},{2,1},{3,0},{4,7},{5,6},{6,5},{7,4},{8,11},{9,10},{10,... | collective-permute-start | bytes 589832 | tf_op jit(solution)/shard_map/ppermute | solution.py:155
  11.5 9.8 %collective-permute-start.1 = (bf16[64,1536]{1,0:T(8,128)(2,1)S(1)}, bf16[64,1536]{1,0:T(8,128)(2,1)S(1)}, u32[]{:S(2)}, u32[]{:S(2)}) collective-permute-start(bf16[64,1536]{1,0:T(8,128)(2,1)S(1)} %get-tuple-element.57), channel_id=1, source_target_pairs={{0,2},{1,3},{2,0},{3,1},{4,6},{5,7},{6,4},{7,5},{8,10},{9,11},{10,... | collective-permute-start | bytes 589832 | tf_op jit(solution)/shard_map/ppermute | solution.py:155
  22.3 29.3 %collective-permute-start.8 = (bf16[256,1536]{1,0:T(8,128)(2,1)}, bf16[256,1536]{1,0:T(8,128)(2,1)}, u32[]{:S(2)}, u32[]{:S(2)}) collective-permute-start(bf16[256,1536]{1,0:T(8,128)(2,1)} %pad_maximum_fusion.refs_0_), channel_id=1, source_target_pairs={{8,16},{16,8},{9,17},{17,9},{10,18},{18,10},{11,19},{19,11},{12,20... | collective-permute-start | bytes 2359304 | tf_op jit(solution)/shard_map/ppermute | solution.py:252
  23.9 27.7 %collective-permute-start.7 = (bf16[256,1536]{1,0:T(8,128)(2,1)}, bf16[256,1536]{1,0:T(8,128)(2,1)}, u32[]{:S(2)}, u32[]{:S(2)}) collective-permute-start(bf16[256,1536]{1,0:T(8,128)(2,1)} %pad_maximum_fusion.refs_0_), channel_id=1, source_target_pairs={{0,8},{8,0},{16,24},{24,16},{1,9},{9,1},{17,25},{25,17},{2,10},{10... | collective-permute-start | bytes 2359304 | tf_op jit(solution)/shard_map/ppermute | solution.py:252
  27.4 5.0 %copy-start.2 = (bf16[128,6144]{1,0:T(8,128)(2,1)}, bf16[128,6144]{1,0:T(8,128)(2,1)S(1)}, u32[]{:S(2)}) copy-start(bf16[128,6144]{1,0:T(8,128)(2,1)S(1)} %collective-permute-done.3.refs_2_.refs_3_.refs_10_) | copy-start | bytes 4718596
  27.4 24.1 %collective-permute-start.11 = (bf16[64,6144]{1,0:T(8,128)(2,1)}, bf16[64,6144]{1,0:T(8,128)(2,1)}, u32[]{:S(2)}, u32[]{:S(2)}) collective-permute-start(bf16[64,6144]{1,0:T(8,128)(2,1)} %get-tuple-element.35), channel_id=1, source_target_pairs={{0,4},{4,0},{1,5},{5,1},{2,6},{6,2},{3,7},{7,3},{8,12},{12,8},{9,1... | collective-permute-start | bytes 2359304 | tf_op jit(solution)/shard_map/ppermute | solution.py:158
  29.1 1.8 %collective-permute-start.6 = (bf16[32,6144]{1,0:T(8,128)(2,1)S(1)}, bf16[32,6144]{1,0:T(8,128)(2,1)S(1)}, u32[]{:S(2)}, u32[]{:S(2)}) collective-permute-start(bf16[32,6144]{1,0:T(8,128)(2,1)S(1)} %get-tuple-element.52), channel_id=1, source_target_pairs={{0,1},{1,0},{2,3},{3,2},{4,5},{5,4},{6,7},{7,6},{8,9},{9,8},{10,11... | collective-permute-start | bytes 1179656 | tf_op jit(solution)/shard_map/ppermute | solution.py:155
  29.2 3.2 %collective-permute-start.5 = (bf16[32,6144]{1,0:T(8,128)(2,1)S(1)}, bf16[32,6144]{1,0:T(8,128)(2,1)S(1)}, u32[]{:S(2)}, u32[]{:S(2)}) collective-permute-start(bf16[32,6144]{1,0:T(8,128)(2,1)S(1)} %get-tuple-element.53), channel_id=1, source_target_pairs={{0,1},{1,0},{2,3},{3,2},{4,5},{5,4},{6,7},{7,6},{8,9},{9,8},{10,11... | collective-permute-start | bytes 1179656 | tf_op jit(solution)/shard_map/ppermute | solution.py:155
  30.9 24.7 %collective-permute-start.9 = (bf16[64,6144]{1,0:T(8,128)(2,1)}, bf16[64,6144]{1,0:T(8,128)(2,1)}, u32[]{:S(2)}, u32[]{:S(2)}) collective-permute-start(bf16[64,6144]{1,0:T(8,128)(2,1)} %get-tuple-element.22), channel_id=1, source_target_pairs={{0,2},{1,3},{2,0},{3,1},{4,6},{5,7},{6,4},{7,5},{8,10},{9,11},{10,... | collective-permute-start | bytes 2359304 | tf_op jit(solution)/shard_map/ppermute | solution.py:155
  51.6 5.3 %collective-permute-start.12 = (bf16[64,6144]{1,0:T(8,128)(2,1)}, bf16[64,6144]{1,0:T(8,128)(2,1)S(1)}, u32[]{:S(2)}, u32[]{:S(2)}) collective-permute-start(bf16[64,6144]{1,0:T(8,128)(2,1)} %collective-permute-done.11.refs_4_.refs_5_.refs_9_), channel_id=1, source_target_pairs={{0,1},{1,0},{2,3},{3,2},{4,5},{5,4},{6,7},{7,6},{8,9},{9,8},{10,11... | collective-permute-start | bytes 2359304 | tf_op jit(solution)/shard_map/ppermute | solution.py:155
  55.6 7.8 %collective-permute-start.10 = (bf16[64,6144]{1,0:T(8,128)(2,1)}, bf16[64,6144]{1,0:T(8,128)(2,1)}, u32[]{:S(2)}, u32[]{:S(2)}) collective-permute-start(bf16[64,6144]{1,0:T(8,128)(2,1)} %collective-permute-done.9.refs_14_), channel_id=1, source_target_pairs={{0,1},{1,0},{2,3},{3,2},{4,5},{5,4},{6,7},{7,6},{8,9},{9,8},{10,11... | collective-permute-start | bytes 2359304 | tf_op jit(solution)/shard_map/ppermute | solution.py:155
  56.1 25.7 %collective-permute-start.18 = (bf16[64,6144]{1,0:T(8,128)(2,1)}, bf16[64,6144]{1,0:T(8,128)(2,1)}, u32[]{:S(2)}, u32[]{:S(2)}) collective-permute-start(bf16[64,6144]{1,0:T(8,128)(2,1)} %get-tuple-element.35), channel_id=1, source_target_pairs={{0,2},{1,3},{2,0},{3,1},{4,6},{5,7},{6,4},{7,5},{8,10},{9,11},{10,... | collective-permute-start | bytes 2359304 | tf_op jit(solution)/shard_map/ppermute | solution.py:155
  56.8 6.6 %copy-start.4 = (bf16[64,6144]{1,0:T(8,128)(2,1)}, bf16[64,6144]{1,0:T(8,128)(2,1)S(1)}, u32[]{:S(2)}) copy-start(bf16[64,6144]{1,0:T(8,128)(2,1)S(1)} %collective-permute-done.12.refs_6_.refs_7_.refs_13_) | copy-start | bytes 2359300
  56.8 26.2 %collective-permute-start.13 = (bf16[256,1536]{1,0:T(8,128)(2,1)}, bf16[256,1536]{1,0:T(8,128)(2,1)S(1)}, u32[]{:S(2)}, u32[]{:S(2)}) collective-permute-start(bf16[256,1536]{1,0:T(8,128)(2,1)} %get-tuple-element.28), channel_id=1, source_target_pairs={{8,16},{16,8},{9,17},{17,9},{10,18},{18,10},{11,19},{19,11},{12,20... | collective-permute-start | bytes 2359304 | tf_op jit(solution)/shard_map/ppermute | solution.py:252
  57.5 25.5 %collective-permute-start.14 = (bf16[256,1536]{1,0:T(8,128)(2,1)}, bf16[256,1536]{1,0:T(8,128)(2,1)}, u32[]{:S(2)}, u32[]{:S(2)}) collective-permute-start(bf16[256,1536]{1,0:T(8,128)(2,1)} %get-tuple-element.29), channel_id=1, source_target_pairs={{0,8},{8,0},{16,24},{24,16},{1,9},{9,1},{17,25},{25,17},{2,10},{10... | collective-permute-start | bytes 2359304 | tf_op jit(solution)/shard_map/ppermute | solution.py:252
  61.8 21.3 %copy-start.1 = (bf16[2,2,128,1536]{3,2,1,0:T(8,128)(2,1)S(1)}, bf16[2,2,128,1536]{3,2,1,0:T(8,128)(2,1)}, u32[]{:S(2)}) copy-start(bf16[2,2,128,1536]{3,2,1,0:T(8,128)(2,1)} %shard_map.77) | copy-start | bytes 4718596
  61.8 28.8 %collective-permute-start.19 = (bf16[64,6144]{1,0:T(8,128)(2,1)}, bf16[64,6144]{1,0:T(8,128)(2,1)}, u32[]{:S(2)}, u32[]{:S(2)}) collective-permute-start(bf16[64,6144]{1,0:T(8,128)(2,1)} %collective-permute-done.9.refs_14_), channel_id=1, source_target_pairs={{0,4},{4,0},{1,5},{5,1},{2,6},{6,2},{3,7},{7,3},{8,12},{12,8},{9,1... | collective-permute-start | bytes 2359304 | tf_op jit(solution)/shard_map/ppermute | solution.py:158
  81.8 19.0 %collective-permute-start.20 = (bf16[64,6144]{1,0:T(8,128)(2,1)}, bf16[64,6144]{1,0:T(8,128)(2,1)}, u32[]{:S(2)}, u32[]{:S(2)}) collective-permute-start(bf16[64,6144]{1,0:T(8,128)(2,1)} %collective-permute-done.11.refs_4_.refs_5_.refs_9_), channel_id=1, source_target_pairs={{0,2},{1,3},{2,0},{3,1},{4,6},{5,7},{6,4},{7,5},{8,10},{9,11},{10,... | collective-permute-start | bytes 2359304 | tf_op jit(solution)/shard_map/ppermute | solution.py:155
  83.1 1.8 %copy-start.6 = (bf16[256,1536]{1,0:T(8,128)(2,1)}, bf16[256,1536]{1,0:T(8,128)(2,1)S(1)}, u32[]{:S(2)}) copy-start(bf16[256,1536]{1,0:T(8,128)(2,1)S(1)} %collective-permute-done.13.refs_4_) | copy-start | bytes 2359300
  85.9 18.5 %collective-permute-start.15 = (bf16[256,1536]{1,0:T(8,128)(2,1)}, bf16[256,1536]{1,0:T(8,128)(2,1)}, u32[]{:S(2)}, u32[]{:S(2)}) collective-permute-start(bf16[256,1536]{1,0:T(8,128)(2,1)} %add_select_fusion.1), channel_id=1, source_target_pairs={{0,8},{8,0},{16,24},{24,16},{1,9},{9,1},{17,25},{25,17},{2,10},{10... | collective-permute-start | bytes 2359304 | tf_op jit(solution)/shard_map/ppermute | solution.py:252
  86.1 5.0 %copy-start.3 = (bf16[2,2,128,1536]{3,2,1,0:T(8,128)(2,1)S(1)}, bf16[2,2,128,1536]{3,2,1,0:T(8,128)(2,1)}, u32[]{:S(2)}) copy-start(bf16[2,2,128,1536]{3,2,1,0:T(8,128)(2,1)} %shard_map.78) | copy-start | bytes 4718596
  88.3 16.2 %collective-permute-start.16 = (bf16[256,1536]{1,0:T(8,128)(2,1)}, bf16[256,1536]{1,0:T(8,128)(2,1)}, u32[]{:S(2)}, u32[]{:S(2)}) collective-permute-start(bf16[256,1536]{1,0:T(8,128)(2,1)} %add_select_fusion), channel_id=1, source_target_pairs={{8,16},{16,8},{9,17},{17,9},{10,18},{18,10},{11,19},{19,11},{12,20... | collective-permute-start | bytes 2359304 | tf_op jit(solution)/shard_map/ppermute | solution.py:252
  90.6 24.9 %collective-permute-start.21 = (bf16[64,6144]{1,0:T(8,128)(2,1)}, bf16[64,6144]{1,0:T(8,128)(2,1)}, u32[]{:S(2)}, u32[]{:S(2)}) collective-permute-start(bf16[64,6144]{1,0:T(8,128)(2,1)} %collective-permute-done.18.refs_15_), channel_id=1, source_target_pairs={{0,1},{1,0},{2,3},{3,2},{4,5},{5,4},{6,7},{7,6},{8,9},{9,8},{10,11... | collective-permute-start | bytes 2359304 | tf_op jit(solution)/shard_map/ppermute | solution.py:155
  90.6 24.8 %collective-permute-start.22 = (bf16[64,6144]{1,0:T(8,128)(2,1)}, bf16[64,6144]{1,0:T(8,128)(2,1)}, u32[]{:S(2)}, u32[]{:S(2)}) collective-permute-start(bf16[64,6144]{1,0:T(8,128)(2,1)} %collective-permute-done.19.refs_16_), channel_id=1, source_target_pairs={{0,1},{1,0},{2,3},{3,2},{4,5},{5,4},{6,7},{7,6},{8,9},{9,8},{10,11... | collective-permute-start | bytes 2359304 | tf_op jit(solution)/shard_map/ppermute | solution.py:155
  100.8 14.6 %collective-permute-start.23 = (bf16[64,6144]{1,0:T(8,128)(2,1)}, bf16[64,6144]{1,0:T(8,128)(2,1)}, u32[]{:S(2)}, u32[]{:S(2)}) collective-permute-start(bf16[64,6144]{1,0:T(8,128)(2,1)} %collective-permute-done.20.refs_17_), channel_id=1, source_target_pairs={{0,1},{1,0},{2,3},{3,2},{4,5},{5,4},{6,7},{7,6},{8,9},{9,8},{10,11... | collective-permute-start | bytes 2359304 | tf_op jit(solution)/shard_map/ppermute | solution.py:155
  105.8 37.7 %collective-permute-start.24 = (bf16[256,1536]{1,0:T(8,128)(2,1)S(1)}, bf16[256,1536]{1,0:T(8,128)(2,1)S(1)}, u32[]{:S(2)}, u32[]{:S(2)}) collective-permute-start(bf16[256,1536]{1,0:T(8,128)(2,1)S(1)} %bitcast_add_fusion), channel_id=1, source_target_pairs={{8,16},{16,8},{9,17},{17,9},{10,18},{18,10},{11,19},{19,11},{12,20... | collective-permute-start | bytes 2359304 | tf_op jit(solution)/shard_map/ppermute | solution.py:252
  108.0 35.6 %copy-start.5 = (bf16[1,2,128,1536]{3,2,1,0:T(8,128)(2,1)S(1)}, bf16[1,2,128,1536]{3,2,1,0:T(8,128)(2,1)}, u32[]{:S(2)}) copy-start(bf16[1,2,128,1536]{3,2,1,0:T(8,128)(2,1)} %dynamic-slice_select_fusion.4) | copy-start | bytes 2359300
  108.0 35.6 %collective-permute-start.17 = (bf16[256,1536]{1,0:T(8,128)(2,1)S(1)}, bf16[256,1536]{1,0:T(8,128)(2,1)S(1)}, u32[]{:S(2)}, u32[]{:S(2)}) collective-permute-start(bf16[256,1536]{1,0:T(8,128)(2,1)S(1)} %bitcast_add_fusion.1), channel_id=1, source_target_pairs={{0,8},{8,0},{16,24},{24,16},{1,9},{9,1},{17,25},{25,17},{2,10},{10... | collective-permute-start | bytes 2359304 | tf_op jit(solution)/shard_map/ppermute | solution.py:252
  144.0 1.8 %collective-permute-start.25 = (bf16[2,64,1536]{2,1,0:T(8,128)(2,1)S(1)}, bf16[2,64,1536]{2,1,0:T(8,128)(2,1)S(1)}, u32[]{:S(2)}, u32[]{:S(2)}) collective-permute-start(bf16[2,64,1536]{2,1,0:T(8,128)(2,1)S(1)} %get-tuple-element.50), channel_id=1, source_target_pairs={{0,1},{1,0},{2,3},{3,2},{4,5},{5,4},{6,7},{7,6},{8,9},{9,8},{10,11... | collective-permute-start | bytes 1179656 | tf_op jit(solution)/shard_map/ppermute | solution.py:155
  (3 other events, 4.1 us)

commit v7 on v6

--- a/solution.py
+++ b/solution.py
@@ -10,7 +10,7 @@
 K = 4
 CDW = 2
 CDX = 0
-VMEM = 60 << 20
+VMEM = 63 << 20
 
 
 def pass_weights(samples, correct):

time: 148 us -> 153 us (1.034)
  other arithmetic: 16.8 us -> 21.3 us
    add x2, other arithmetic: 2.43 us -> 4.22 us  [step_planes(): total = total + come[1 - kind]]
  transfers between devices with their start and end apart: 26 -> 26, of which waited for: 6 -> 6; matrix products, arithmetic and copies ran while one was open for 13% -> 15% of each run, Pallas kernels for 44% -> 43%
where the time goes in v7:
time: 153 us; the launch traced here: 152 us
  Pallas kernels  64.8 us (42%)
  starting transfers between devices  32 us (21%)
  waiting for transfers between devices  23.9 us (16%)
  other arithmetic  21.3 us (14%)
  local copies, waits for them, and re-layouts  9.19 us (6%)
    pallas_call x2, Pallas kernels, input_grad(): pl.pallas_call(input_grad_kernel, grid_spec=pltpu.PrefetchScalarGridSpec(...  36.7 us
    pallas_call x1, Pallas kernels, weight_grad(): pl.pallas_call(body, grid_spec=pltpu.PrefetchScalarGridSpec(num_scalar_pr...  28.1 us
    ppermute x8, starting transfers between devices, step_planes(): came[kind] = lax.ppermute(sent[kind], 'hidden', pairs[kind])  19.1 us
    ppermute x15, waiting for transfers between devices, over_replica(): return lax.ppermute(value, 'replica', replica_perm(dy, dc))  19 us
    ppermute x15, starting transfers between devices, over_replica(): return lax.ppermute(value, 'replica', replica_perm(dy, dc))  7.99 us
    select_n x3, other arithmetic, step_planes(): value = total if value is None else jnp.where(is_input, value, total)  6.88 us
    ppermute x8, waiting for transfers between devices, step_planes(): came[kind] = lax.ppermute(sent[kind], 'hidden', pairs[kind])  4.94 us
    ppermute x3, starting transfers between devices, over_width(): lax.ppermute(value, 'width', [(w, (w + dx) % n_w) for w in range(n_w)])  4.9 us
  transfers between devices with their start and end apart: 26, of which 6 were waited for; matrix products, arithmetic and copies ran while one was open for 15% of the time, Pallas kernels for 43%

profile of v7, /device:TPU:0, one launch (start us, length us, event | category | flops | bytes accessed | tf_op | source)
XLA Modules:
  0.0 152.0 jit_solution(12837727084770182196)
XLA Ops:
  2.1 1.8 %multiply_convert_fusion.refs_0_.refs_1_.refs_7_ = bf16[128,6144]{1,0:T(8,128)(2,1)S(1)} fusion(bf16[128,6144]{1,0:T(8,128)(2,1)} %param.7, f32[128]{0:T(128)S(1)} %fusion.5), kind=kLoop, calls=%fused_computation | loop fusion | flops 2359296 | bytes 3146240 | tf_op jit(solution)/shard_map/convert_element_type | solution.py:179
  4.4 1.2 constant_dynamic-slice_fusion.2
  5.6 2.9 %collective-permute-start.4 = (bf16[64,6144]{1,0:T(8,128)(2,1)}, bf16[64,6144]{1,0:T(8,128)(2,1)}, u32[]{:S(2)}, u32[]{:S(2)}) collective-permute-start(bf16[64,6144]{1,0:T(8,128)(2,1)} %get-tuple-element.22), channel_id=1, source_target_pairs={{0,4},{4,0},{1,5},{5,1},{2,6},{6,2},{3,7},{7,3},{8,12},{12,8},{9,1... | collective-permute-start | bytes 2359304 | tf_op jit(solution)/shard_map/ppermute | solution.py:158
  8.5 1.3 constant_dynamic-slice_fusion.8
  9.9 1.6 %collective-permute-start.2 = (bf16[64,1536]{1,0:T(8,128)(2,1)S(1)}, bf16[64,1536]{1,0:T(8,128)(2,1)S(1)}, u32[]{:S(2)}, u32[]{:S(2)}) collective-permute-start(bf16[64,1536]{1,0:T(8,128)(2,1)S(1)} %get-tuple-element.56), channel_id=1, source_target_pairs={{0,3},{1,2},{2,1},{3,0},{4,7},{5,6},{6,5},{7,4},{8,11},{9,10},{10,... | collective-permute-start | bytes 589832 | tf_op jit(solution)/shard_map/ppermute | solution.py:155
  12.0 4.7 %collective-permute-done.2 = bf16[64,1536]{1,0:T(8,128)(2,1)S(1)} collective-permute-done((bf16[64,1536]{1,0:T(8,128)(2,1)S(1)}, bf16[64,1536]{1,0:T(8,128)(2,1)S(1)}, u32[]{:S(2)}, u32[]{:S(2)}) %collective-permute-start.2) | collective-permute-done | bytes 196640 | tf_op jit(solution)/shard_map/ppermute | solution.py:155
  16.7 4.6 %collective-permute-done.1 = bf16[64,1536]{1,0:T(8,128)(2,1)S(1)} collective-permute-done((bf16[64,1536]{1,0:T(8,128)(2,1)S(1)}, bf16[64,1536]{1,0:T(8,128)(2,1)S(1)}, u32[]{:S(2)}, u32[]{:S(2)}) %collective-permute-start.1) | collective-permute-done | bytes 196640 | tf_op jit(solution)/shard_map/ppermute | solution.py:155
  22.3 1.6 %collective-permute-start.8 = (bf16[256,1536]{1,0:T(8,128)(2,1)}, bf16[256,1536]{1,0:T(8,128)(2,1)}, u32[]{:S(2)}, u32[]{:S(2)}) collective-permute-start(bf16[256,1536]{1,0:T(8,128)(2,1)} %pad_maximum_fusion.refs_0_), channel_id=1, source_target_pairs={{8,16},{16,8},{9,17},{17,9},{10,18},{18,10},{11,19},{19,11},{12,20... | collective-permute-start | bytes 2359304 | tf_op jit(solution)/shard_map/ppermute | solution.py:252
  23.8 3.6 %collective-permute-start.7 = (bf16[256,1536]{1,0:T(8,128)(2,1)}, bf16[256,1536]{1,0:T(8,128)(2,1)}, u32[]{:S(2)}, u32[]{:S(2)}) collective-permute-start(bf16[256,1536]{1,0:T(8,128)(2,1)} %pad_maximum_fusion.refs_0_), channel_id=1, source_target_pairs={{0,8},{8,0},{16,24},{24,16},{1,9},{9,1},{17,25},{25,17},{2,10},{10... | collective-permute-start | bytes 2359304 | tf_op jit(solution)/shard_map/ppermute | solution.py:252
  27.4 1.2 copy-done.2
  32.1 1.5 collective-permute-start.9
  34.4 18.3 %shard_map.77 = bf16[2,2,128,1536]{3,2,1,0:T(8,128)(2,1)} custom-call(s32[9]{0:T(128)} %stack.97.first_ref, bf16[128,6144]{1,0:T(8,128)(2,1)} %copy-done, bf16[128,6144]{1,0:T(8,128)(2,1)} %copy-done, bf16[128,6144]{1,0:T(8,128)(2,1)} %copy-done.2, bf16[128,6144]{1,0:T(8,128)(2,1)} %copy-done.2, ...), custom_call_target="tpu_custom_call" | custom-call | tf_op jit(solution)/shard_map/pallas_call | solution.py:120
  52.8 1.5 constant_dynamic-slice_fusion
  54.3 2.5 %bitcast_select_fusion = (bf16[256,1536]{1,0:T(8,128)(2,1)}, bf16[256,1536]{1,0:T(8,128)(2,1)}) fusion(bf16[256,1536]{1,0:T(8,128)(2,1)} %collective-permute-done.8.refs_2_, bf16[1,2,128,1536]{3,2,1,0:T(8,128)(2,1)S(1)} %get-tuple-element.44, pred[]{:T(512)S(6)} %select_n.528, bf16[256,1536]{1,0:T(8,128)(2,1)} %collective-permute-done.7.refs_1_, ...), kind=kLoop, calls=%fused_computation.14 | loop fusion | flops 786432 | bytes 4718594 | tf_op jit(solution)/shard_map/jit(_where)/select_n | solution.py:249
  58.0 1.6 %collective-permute-start.13 = (bf16[256,1536]{1,0:T(8,128)(2,1)}, bf16[256,1536]{1,0:T(8,128)(2,1)}, u32[]{:S(2)}, u32[]{:S(2)}) collective-permute-start(bf16[256,1536]{1,0:T(8,128)(2,1)} %get-tuple-element.28), channel_id=1, source_target_pairs={{8,16},{16,8},{9,17},{17,9},{10,18},{18,10},{11,19},{19,11},{12,20... | collective-permute-start | bytes 2359304 | tf_op jit(solution)/shard_map/ppermute | solution.py:252
  59.6 1.8 %collective-permute-start.14 = (bf16[256,1536]{1,0:T(8,128)(2,1)}, bf16[256,1536]{1,0:T(8,128)(2,1)}, u32[]{:S(2)}, u32[]{:S(2)}) collective-permute-start(bf16[256,1536]{1,0:T(8,128)(2,1)} %get-tuple-element.29), channel_id=1, source_target_pairs={{0,8},{8,0},{16,24},{24,16},{1,9},{9,1},{17,25},{25,17},{2,10},{10... | collective-permute-start | bytes 2359304 | tf_op jit(solution)/shard_map/ppermute | solution.py:252
  62.0 1.5 collective-permute-start.19
  63.5 18.3 %shard_map.78 = bf16[2,2,128,1536]{3,2,1,0:T(8,128)(2,1)} custom-call(s32[9]{0:T(128)} %stack.94.first_ref, bf16[128,6144]{1,0:T(8,128)(2,1)} %copy-done, bf16[128,6144]{1,0:T(8,128)(2,1)} %copy-done, bf16[128,6144]{1,0:T(8,128)(2,1)} %copy-done.2, bf16[128,6144]{1,0:T(8,128)(2,1)} %copy-done.2, ...), custom_call_target="tpu_custom_call" | custom-call | tf_op jit(solution)/shard_map/pallas_call | solution.py:120
  81.9 1.3 collective-permute-start.20
  83.1 2.0 %dynamic-slice_select_fusion.2 = (bf16[1,2,128,1536]{3,2,1,0:T(8,128)(2,1)S(1)}, bf16[1,2,128,1536]{3,2,1,0:T(8,128)(2,1)S(1)}) fusion(bf16[2,2,128,1536]{3,2,1,0:T(8,128)(2,1)} %shard_map.77, s32[]{:T(128)S(6)} %select_n.548, bf16[2,2,128,1536]{3,2,1,0:T(8,128)(2,1)} %shard_map.78, pred[]{:T(512)S(6)} %eq.98, s32[]{:T(128)S(6)} %select_n.536, pred[]{:T(512)S(6)} %eq.97), kind=kLoop, calls=%fused_computation.18 | loop fusion | flops 786432 | bytes 4718602 | tf_op jit(solution)/shard_map/jit(_where)/select_n | solution.py:224
  85.1 2.1 %add_select_fusion.1 = bf16[256,1536]{1,0:T(8,128)(2,1)} fusion(bf16[256,1536]{1,0:T(8,128)(2,1)} %collective-permute-done.13.refs_4_, bf16[1,2,128,1536]{3,2,1,0:T(8,128)(2,1)S(1)} %get-tuple-element.43, pred[]{:T(512)S(6)} %select_n.514), kind=kLoop, calls=%fused_computation.5 | loop fusion | flops 786432 | bytes 2359297 | tf_op jit(solution)/shard_map/jit(_where)/select_n | solution.py:249
  87.5 2.3 %add_select_fusion = bf16[256,1536]{1,0:T(8,128)(2,1)} fusion(bf16[256,1536]{1,0:T(8,128)(2,1)} %collective-permute-done.14.refs_3_, bf16[1,2,128,1536]{3,2,1,0:T(8,128)(2,1)S(1)} %get-tuple-element.42, pred[]{:T(512)S(6)} %select_n.540), kind=kLoop, calls=%fused_computation.4 | loop fusion | flops 786432 | bytes 2359297 | tf_op jit(solution)/shard_map/jit(_where)/select_n | solution.py:249
  89.7 1.6 %collective-permute-start.16 = (bf16[256,1536]{1,0:T(8,128)(2,1)}, bf16[256,1536]{1,0:T(8,128)(2,1)}, u32[]{:S(2)}, u32[]{:S(2)}) collective-permute-start(bf16[256,1536]{1,0:T(8,128)(2,1)} %add_select_fusion), channel_id=1, source_target_pairs={{8,16},{16,8},{9,17},{17,9},{10,18},{18,10},{11,19},{19,11},{12,20... | collective-permute-start | bytes 2359304 | tf_op jit(solution)/shard_map/ppermute | solution.py:252
  93.5 7.4 %collective-permute-done.20.refs_17_ = bf16[64,6144]{1,0:T(8,128)(2,1)} collective-permute-done((bf16[64,6144]{1,0:T(8,128)(2,1)}, bf16[64,6144]{1,0:T(8,128)(2,1)}, u32[]{:S(2)}, u32[]{:S(2)}) %collective-permute-start.20) | collective-permute-done | bytes 786464 | tf_op jit(solution)/shard_map/ppermute | solution.py:155
  100.9 4.9 %collective-permute-done.15.refs_5_ = bf16[256,1536]{1,0:T(8,128)(2,1)} collective-permute-done((bf16[256,1536]{1,0:T(8,128)(2,1)}, bf16[256,1536]{1,0:T(8,128)(2,1)}, u32[]{:S(2)}, u32[]{:S(2)}) %collective-permute-start.15) | collective-permute-done | bytes 786464 | tf_op jit(solution)/shard_map/ppermute | solution.py:252
  106.0 2.1 %bitcast_add_fusion = bf16[256,1536]{1,0:T(8,128)(2,1)} fusion(bf16[256,1536]{1,0:T(8,128)(2,1)} %collective-permute-done.15.refs_5_, bf16[1,2,128,1536]{3,2,1,0:T(8,128)(2,1)S(1)} %get-tuple-element.41), kind=kLoop, calls=%fused_computation.12 | loop fusion | flops 393216 | bytes 2359296 | tf_op jit(solution)/shard_map/add | solution.py:247
  108.1 1.5 %collective-permute-start.24 = (bf16[256,1536]{1,0:T(8,128)(2,1)}, bf16[256,1536]{1,0:T(8,128)(2,1)}, u32[]{:S(2)}, u32[]{:S(2)}) collective-permute-start(bf16[256,1536]{1,0:T(8,128)(2,1)} %bitcast_add_fusion), channel_id=1, source_target_pairs={{8,16},{16,8},{9,17},{17,9},{10,18},{18,10},{11,19},{19,11},{12,20... | collective-permute-start | bytes 2359304 | tf_op jit(solution)/shard_map/ppermute | solution.py:252
  109.6 2.1 %bitcast_add_fusion.1 = bf16[256,1536]{1,0:T(8,128)(2,1)} fusion(bf16[256,1536]{1,0:T(8,128)(2,1)} %collective-permute-done.16.refs_6_, bf16[1,2,128,1536]{3,2,1,0:T(8,128)(2,1)S(1)} %get-tuple-element.40), kind=kLoop, calls=%fused_computation.13 | loop fusion | flops 393216 | bytes 2359296 | tf_op jit(solution)/shard_map/add | solution.py:247
  111.7 7.3 %collective-permute-start.17 = (bf16[256,1536]{1,0:T(8,128)(2,1)}, bf16[256,1536]{1,0:T(8,128)(2,1)}, u32[]{:S(2)}, u32[]{:S(2)}) collective-permute-start(bf16[256,1536]{1,0:T(8,128)(2,1)} %bitcast_add_fusion.1), channel_id=1, source_target_pairs={{0,8},{8,0},{16,24},{24,16},{1,9},{9,1},{17,25},{25,17},{2,10},{10... | collective-permute-start | bytes 2359304 | tf_op jit(solution)/shard_map/ppermute | solution.py:252
  119.0 28.1 %shard_map.79 = f32[1536,6144]{1,0:T(8,128)} custom-call(s32[28]{0:T(128)} %stack.112.place_ref, bf16[256,1536]{1,0:T(8,128)(2,1)} %pad_maximum_fusion.refs_0_, bf16[256,1536]{1,0:T(8,128)(2,1)} %collective-permute-done.7.refs_1_, bf16[256,1536]{1,0:T(8,128)(2,1)} %collective-permute-done.8.refs_2_, bf16[256,1536]{1,0:T(8,128)(2,1)} %collective-permute-done.14.refs_3_, ...), custom_call_target="tpu_custom_call" | custom-call | flops 19327352832 | bytes 53477376 | tf_op jit(solution)/shard_map/pallas_call | solution.py:78
  147.2 1.7 %fusion.1 = bf16[256,1536]{1,0:T(8,128)(2,1)S(1)} fusion(bf16[256,1536]{1,0:T(8,128)(2,1)} %collective-permute-done.24, bf16[256,1536]{1,0:T(8,128)(2,1)} %collective-permute-done.17, bf16[1,2,128,1536]{3,2,1,0:T(8,128)(2,1)S(1)} %copy-done.5), kind=kLoop, calls=%fused_computation.3 | loop fusion | flops 2359296 | bytes 3145728 | tf_op jit(solution)/shard_map/convert_element_type | solution.py:331
  149.1 1.7 %collective-permute-done.25 = bf16[2,64,1536]{2,1,0:T(8,128)(2,1)S(1)} collective-permute-done((bf16[2,64,1536]{2,1,0:T(8,128)(2,1)S(1)}, bf16[2,64,1536]{2,1,0:T(8,128)(2,1)S(1)}, u32[]{:S(2)}, u32[]{:S(2)}) %collective-permute-start.25) | collective-permute-done | bytes 393248 | tf_op jit(solution)/shard_map/ppermute | solution.py:155
  (67 shorter events, 13.7 us)
Async XLA Ops:
  3.9 1.8 %copy-start = (bf16[128,6144]{1,0:T(8,128)(2,1)}, bf16[128,6144]{1,0:T(8,128)(2,1)S(1)}, u32[]{:S(2)}) copy-start(bf16[128,6144]{1,0:T(8,128)(2,1)S(1)} %multiply_convert_fusion.refs_0_.refs_1_.refs_7_) | copy-start | bytes 4718596
  3.9 23.5 %collective-permute-start.3 = (bf16[128,6144]{1,0:T(8,128)(2,1)S(1)}, bf16[128,6144]{1,0:T(8,128)(2,1)S(1)}, u32[]{:S(2)}, u32[]{:S(2)}) collective-permute-start(bf16[128,6144]{1,0:T(8,128)(2,1)S(1)} %multiply_convert_fusion.refs_0_.refs_1_.refs_7_), channel_id=1, source_target_pairs={{0,1},{1,0},{2,3},{3,2},{4,5},{5,4},{6,7},{7,6},{8,9},{9,8},{10,11... | collective-permute-start | bytes 4718600 | tf_op jit(solution)/shard_map/ppermute | solution.py:155
  5.6 23.5 %collective-permute-start.4 = (bf16[64,6144]{1,0:T(8,128)(2,1)}, bf16[64,6144]{1,0:T(8,128)(2,1)}, u32[]{:S(2)}, u32[]{:S(2)}) collective-permute-start(bf16[64,6144]{1,0:T(8,128)(2,1)} %get-tuple-element.22), channel_id=1, source_target_pairs={{0,4},{4,0},{1,5},{5,1},{2,6},{6,2},{3,7},{7,3},{8,12},{12,8},{9,1... | collective-permute-start | bytes 2359304 | tf_op jit(solution)/shard_map/ppermute | solution.py:158
  9.8 2.2 %collective-permute-start = (bf16[64,1536]{1,0:T(8,128)(2,1)S(1)}, bf16[64,1536]{1,0:T(8,128)(2,1)S(1)}, u32[]{:S(2)}, u32[]{:S(2)}) collective-permute-start(bf16[64,1536]{1,0:T(8,128)(2,1)S(1)} %get-tuple-element.55), channel_id=1, source_target_pairs={{0,1},{1,0},{2,3},{3,2},{4,5},{5,4},{6,7},{7,6},{8,9},{9,8},{10,11... | collective-permute-start | bytes 589832 | tf_op jit(solution)/shard_map/ppermute | solution.py:155
  9.9 6.9 %collective-permute-start.2 = (bf16[64,1536]{1,0:T(8,128)(2,1)S(1)}, bf16[64,1536]{1,0:T(8,128)(2,1)S(1)}, u32[]{:S(2)}, u32[]{:S(2)}) collective-permute-start(bf16[64,1536]{1,0:T(8,128)(2,1)S(1)} %get-tuple-element.56), channel_id=1, source_target_pairs={{0,3},{1,2},{2,1},{3,0},{4,7},{5,6},{6,5},{7,4},{8,11},{9,10},{10,... | collective-permute-start | bytes 589832 | tf_op jit(solution)/shard_map/ppermute | solution.py:155
  11.5 9.8 %collective-permute-start.1 = (bf16[64,1536]{1,0:T(8,128)(2,1)S(1)}, bf16[64,1536]{1,0:T(8,128)(2,1)S(1)}, u32[]{:S(2)}, u32[]{:S(2)}) collective-permute-start(bf16[64,1536]{1,0:T(8,128)(2,1)S(1)} %get-tuple-element.57), channel_id=1, source_target_pairs={{0,2},{1,3},{2,0},{3,1},{4,6},{5,7},{6,4},{7,5},{8,10},{9,11},{10,... | collective-permute-start | bytes 589832 | tf_op jit(solution)/shard_map/ppermute | solution.py:155
  22.3 30.4 %collective-permute-start.8 = (bf16[256,1536]{1,0:T(8,128)(2,1)}, bf16[256,1536]{1,0:T(8,128)(2,1)}, u32[]{:S(2)}, u32[]{:S(2)}) collective-permute-start(bf16[256,1536]{1,0:T(8,128)(2,1)} %pad_maximum_fusion.refs_0_), channel_id=1, source_target_pairs={{8,16},{16,8},{9,17},{17,9},{10,18},{18,10},{11,19},{19,11},{12,20... | collective-permute-start | bytes 2359304 | tf_op jit(solution)/shard_map/ppermute | solution.py:252
  23.8 28.8 %collective-permute-start.7 = (bf16[256,1536]{1,0:T(8,128)(2,1)}, bf16[256,1536]{1,0:T(8,128)(2,1)}, u32[]{:S(2)}, u32[]{:S(2)}) collective-permute-start(bf16[256,1536]{1,0:T(8,128)(2,1)} %pad_maximum_fusion.refs_0_), channel_id=1, source_target_pairs={{0,8},{8,0},{16,24},{24,16},{1,9},{9,1},{17,25},{25,17},{2,10},{10... | collective-permute-start | bytes 2359304 | tf_op jit(solution)/shard_map/ppermute | solution.py:252
  28.6 24.1 %collective-permute-start.11 = (bf16[64,6144]{1,0:T(8,128)(2,1)}, bf16[64,6144]{1,0:T(8,128)(2,1)}, u32[]{:S(2)}, u32[]{:S(2)}) collective-permute-start(bf16[64,6144]{1,0:T(8,128)(2,1)} %get-tuple-element.35), channel_id=1, source_target_pairs={{0,4},{4,0},{1,5},{5,1},{2,6},{6,2},{3,7},{7,3},{8,12},{12,8},{9,1... | collective-permute-start | bytes 2359304 | tf_op jit(solution)/shard_map/ppermute | solution.py:158
  30.3 1.8 %collective-permute-start.6 = (bf16[32,6144]{1,0:T(8,128)(2,1)S(1)}, bf16[32,6144]{1,0:T(8,128)(2,1)S(1)}, u32[]{:S(2)}, u32[]{:S(2)}) collective-permute-start(bf16[32,6144]{1,0:T(8,128)(2,1)S(1)} %get-tuple-element.52), channel_id=1, source_target_pairs={{0,1},{1,0},{2,3},{3,2},{4,5},{5,4},{6,7},{7,6},{8,9},{9,8},{10,11... | collective-permute-start | bytes 1179656 | tf_op jit(solution)/shard_map/ppermute | solution.py:155
  30.4 3.2 %collective-permute-start.5 = (bf16[32,6144]{1,0:T(8,128)(2,1)S(1)}, bf16[32,6144]{1,0:T(8,128)(2,1)S(1)}, u32[]{:S(2)}, u32[]{:S(2)}) collective-permute-start(bf16[32,6144]{1,0:T(8,128)(2,1)S(1)} %get-tuple-element.53), channel_id=1, source_target_pairs={{0,1},{1,0},{2,3},{3,2},{4,5},{5,4},{6,7},{7,6},{8,9},{9,8},{10,11... | collective-permute-start | bytes 1179656 | tf_op jit(solution)/shard_map/ppermute | solution.py:155
  32.1 1.5 %copy-start.6 = (bf16[32,6144]{1,0:T(8,128)(2,1)}, bf16[32,6144]{1,0:T(8,128)(2,1)S(1)}, u32[]{:S(2)}) copy-start(bf16[32,6144]{1,0:T(8,128)(2,1)S(1)} %collective-permute-done.6.refs_7_.refs_12_) | copy-start | bytes 1179652
  32.1 24.7 %collective-permute-start.9 = (bf16[64,6144]{1,0:T(8,128)(2,1)}, bf16[64,6144]{1,0:T(8,128)(2,1)}, u32[]{:S(2)}, u32[]{:S(2)}) collective-permute-start(bf16[64,6144]{1,0:T(8,128)(2,1)} %get-tuple-element.22), channel_id=1, source_target_pairs={{0,2},{1,3},{2,0},{3,1},{4,6},{5,7},{6,4},{7,5},{8,10},{9,11},{10,... | collective-permute-start | bytes 2359304 | tf_op jit(solution)/shard_map/ppermute | solution.py:155
  52.7 5.3 %collective-permute-start.12 = (bf16[64,6144]{1,0:T(8,128)(2,1)}, bf16[64,6144]{1,0:T(8,128)(2,1)S(1)}, u32[]{:S(2)}, u32[]{:S(2)}) collective-permute-start(bf16[64,6144]{1,0:T(8,128)(2,1)} %collective-permute-done.11.refs_4_.refs_5_.refs_9_), channel_id=1, source_target_pairs={{0,1},{1,0},{2,3},{3,2},{4,5},{5,4},{6,7},{7,6},{8,9},{9,8},{10,11... | collective-permute-start | bytes 2359304 | tf_op jit(solution)/shard_map/ppermute | solution.py:155
  56.8 6.7 %collective-permute-start.10 = (bf16[64,6144]{1,0:T(8,128)(2,1)}, bf16[64,6144]{1,0:T(8,128)(2,1)}, u32[]{:S(2)}, u32[]{:S(2)}) collective-permute-start(bf16[64,6144]{1,0:T(8,128)(2,1)} %collective-permute-done.9.refs_14_), channel_id=1, source_target_pairs={{0,1},{1,0},{2,3},{3,2},{4,5},{5,4},{6,7},{7,6},{8,9},{9,8},{10,11... | collective-permute-start | bytes 2359304 | tf_op jit(solution)/shard_map/ppermute | solution.py:155
  57.3 24.6 %collective-permute-start.18 = (bf16[64,6144]{1,0:T(8,128)(2,1)}, bf16[64,6144]{1,0:T(8,128)(2,1)}, u32[]{:S(2)}, u32[]{:S(2)}) collective-permute-start(bf16[64,6144]{1,0:T(8,128)(2,1)} %get-tuple-element.35), channel_id=1, source_target_pairs={{0,2},{1,3},{2,0},{3,1},{4,6},{5,7},{6,4},{7,5},{8,10},{9,11},{10,... | collective-permute-start | bytes 2359304 | tf_op jit(solution)/shard_map/ppermute | solution.py:155
  58.0 5.5 %copy-start.4 = (bf16[64,6144]{1,0:T(8,128)(2,1)}, bf16[64,6144]{1,0:T(8,128)(2,1)S(1)}, u32[]{:S(2)}) copy-start(bf16[64,6144]{1,0:T(8,128)(2,1)S(1)} %collective-permute-done.12.refs_6_.refs_7_.refs_13_) | copy-start | bytes 2359300
  58.0 25.1 %collective-permute-start.13 = (bf16[256,1536]{1,0:T(8,128)(2,1)}, bf16[256,1536]{1,0:T(8,128)(2,1)}, u32[]{:S(2)}, u32[]{:S(2)}) collective-permute-start(bf16[256,1536]{1,0:T(8,128)(2,1)} %get-tuple-element.28), channel_id=1, source_target_pairs={{8,16},{16,8},{9,17},{17,9},{10,18},{18,10},{11,19},{19,11},{12,20... | collective-permute-start | bytes 2359304 | tf_op jit(solution)/shard_map/ppermute | solution.py:252
  59.6 23.6 %collective-permute-start.14 = (bf16[256,1536]{1,0:T(8,128)(2,1)}, bf16[256,1536]{1,0:T(8,128)(2,1)}, u32[]{:S(2)}, u32[]{:S(2)}) collective-permute-start(bf16[256,1536]{1,0:T(8,128)(2,1)} %get-tuple-element.29), channel_id=1, source_target_pairs={{0,8},{8,0},{16,24},{24,16},{1,9},{9,1},{17,25},{25,17},{2,10},{10... | collective-permute-start | bytes 2359304 | tf_op jit(solution)/shard_map/ppermute | solution.py:252
  62.0 30.0 %collective-permute-start.19 = (bf16[64,6144]{1,0:T(8,128)(2,1)}, bf16[64,6144]{1,0:T(8,128)(2,1)}, u32[]{:S(2)}, u32[]{:S(2)}) collective-permute-start(bf16[64,6144]{1,0:T(8,128)(2,1)} %collective-permute-done.9.refs_14_), channel_id=1, source_target_pairs={{0,4},{4,0},{1,5},{5,1},{2,6},{6,2},{3,7},{7,3},{8,12},{12,8},{9,1... | collective-permute-start | bytes 2359304 | tf_op jit(solution)/shard_map/ppermute | solution.py:158
  81.9 19.0 %collective-permute-start.20 = (bf16[64,6144]{1,0:T(8,128)(2,1)}, bf16[64,6144]{1,0:T(8,128)(2,1)}, u32[]{:S(2)}, u32[]{:S(2)}) collective-permute-start(bf16[64,6144]{1,0:T(8,128)(2,1)} %collective-permute-done.11.refs_4_.refs_5_.refs_9_), channel_id=1, source_target_pairs={{0,2},{1,3},{2,0},{3,1},{4,6},{5,7},{6,4},{7,5},{8,10},{9,11},{10,... | collective-permute-start | bytes 2359304 | tf_op jit(solution)/shard_map/ppermute | solution.py:155
  87.3 18.6 %collective-permute-start.15 = (bf16[256,1536]{1,0:T(8,128)(2,1)}, bf16[256,1536]{1,0:T(8,128)(2,1)}, u32[]{:S(2)}, u32[]{:S(2)}) collective-permute-start(bf16[256,1536]{1,0:T(8,128)(2,1)} %add_select_fusion.1), channel_id=1, source_target_pairs={{0,8},{8,0},{16,24},{24,16},{1,9},{9,1},{17,25},{25,17},{2,10},{10... | collective-permute-start | bytes 2359304 | tf_op jit(solution)/shard_map/ppermute | solution.py:252
  87.5 5.0 %copy-start.1 = (bf16[2,2,128,1536]{3,2,1,0:T(8,128)(2,1)S(1)}, bf16[2,2,128,1536]{3,2,1,0:T(8,128)(2,1)}, u32[]{:S(2)}) copy-start(bf16[2,2,128,1536]{3,2,1,0:T(8,128)(2,1)} %shard_map.77) | copy-start | bytes 4718596
  87.5 5.0 %copy-start.3 = (bf16[2,2,128,1536]{3,2,1,0:T(8,128)(2,1)S(1)}, bf16[2,2,128,1536]{3,2,1,0:T(8,128)(2,1)}, u32[]{:S(2)}) copy-start(bf16[2,2,128,1536]{3,2,1,0:T(8,128)(2,1)} %shard_map.78) | copy-start | bytes 4718596
  89.7 16.1 %collective-permute-start.16 = (bf16[256,1536]{1,0:T(8,128)(2,1)}, bf16[256,1536]{1,0:T(8,128)(2,1)}, u32[]{:S(2)}, u32[]{:S(2)}) collective-permute-start(bf16[256,1536]{1,0:T(8,128)(2,1)} %add_select_fusion), channel_id=1, source_target_pairs={{8,16},{16,8},{9,17},{17,9},{10,18},{18,10},{11,19},{19,11},{12,20... | collective-permute-start | bytes 2359304 | tf_op jit(solution)/shard_map/ppermute | solution.py:252
  92.0 27.0 %collective-permute-start.21 = (bf16[64,6144]{1,0:T(8,128)(2,1)}, bf16[64,6144]{1,0:T(8,128)(2,1)}, u32[]{:S(2)}, u32[]{:S(2)}) collective-permute-start(bf16[64,6144]{1,0:T(8,128)(2,1)} %collective-permute-done.18.refs_15_), channel_id=1, source_target_pairs={{0,1},{1,0},{2,3},{3,2},{4,5},{5,4},{6,7},{7,6},{8,9},{9,8},{10,11... | collective-permute-start | bytes 2359304 | tf_op jit(solution)/shard_map/ppermute | solution.py:155
  92.0 27.0 %collective-permute-start.22 = (bf16[64,6144]{1,0:T(8,128)(2,1)}, bf16[64,6144]{1,0:T(8,128)(2,1)}, u32[]{:S(2)}, u32[]{:S(2)}) collective-permute-start(bf16[64,6144]{1,0:T(8,128)(2,1)} %collective-permute-done.19.refs_16_), channel_id=1, source_target_pairs={{0,1},{1,0},{2,3},{3,2},{4,5},{5,4},{6,7},{7,6},{8,9},{9,8},{10,11... | collective-permute-start | bytes 2359304 | tf_op jit(solution)/shard_map/ppermute | solution.py:155
  100.9 18.2 %collective-permute-start.23 = (bf16[64,6144]{1,0:T(8,128)(2,1)}, bf16[64,6144]{1,0:T(8,128)(2,1)}, u32[]{:S(2)}, u32[]{:S(2)}) collective-permute-start(bf16[64,6144]{1,0:T(8,128)(2,1)} %collective-permute-done.20.refs_17_), channel_id=1, source_target_pairs={{0,1},{1,0},{2,3},{3,2},{4,5},{5,4},{6,7},{7,6},{8,9},{9,8},{10,11... | collective-permute-start | bytes 2359304 | tf_op jit(solution)/shard_map/ppermute | solution.py:155
  108.1 39.1 %collective-permute-start.24 = (bf16[256,1536]{1,0:T(8,128)(2,1)}, bf16[256,1536]{1,0:T(8,128)(2,1)}, u32[]{:S(2)}, u32[]{:S(2)}) collective-permute-start(bf16[256,1536]{1,0:T(8,128)(2,1)} %bitcast_add_fusion), channel_id=1, source_target_pairs={{8,16},{16,8},{9,17},{17,9},{10,18},{18,10},{11,19},{19,11},{12,20... | collective-permute-start | bytes 2359304 | tf_op jit(solution)/shard_map/ppermute | solution.py:252
  111.7 35.5 %copy-start.5 = (bf16[1,2,128,1536]{3,2,1,0:T(8,128)(2,1)S(1)}, bf16[1,2,128,1536]{3,2,1,0:T(8,128)(2,1)}, u32[]{:S(2)}) copy-start(bf16[1,2,128,1536]{3,2,1,0:T(8,128)(2,1)} %dynamic-slice_select_fusion.4) | copy-start | bytes 2359300
  111.7 35.5 %collective-permute-start.17 = (bf16[256,1536]{1,0:T(8,128)(2,1)}, bf16[256,1536]{1,0:T(8,128)(2,1)}, u32[]{:S(2)}, u32[]{:S(2)}) collective-permute-start(bf16[256,1536]{1,0:T(8,128)(2,1)} %bitcast_add_fusion.1), channel_id=1, source_target_pairs={{0,8},{8,0},{16,24},{24,16},{1,9},{9,1},{17,25},{25,17},{2,10},{10... | collective-permute-start | bytes 2359304 | tf_op jit(solution)/shard_map/ppermute | solution.py:252
  149.0 1.8 %collective-permute-start.25 = (bf16[2,64,1536]{2,1,0:T(8,128)(2,1)S(1)}, bf16[2,64,1536]{2,1,0:T(8,128)(2,1)S(1)}, u32[]{:S(2)}, u32[]{:S(2)}) collective-permute-start(bf16[2,64,1536]{2,1,0:T(8,128)(2,1)S(1)} %get-tuple-element.50), channel_id=1, source_target_pairs={{0,1},{1,0},{2,3},{3,2},{4,5},{5,4},{6,7},{7,6},{8,9},{9,8},{10,11... | collective-permute-start | bytes 1179656 | tf_op jit(solution)/shard_map/ppermute | solution.py:155
  (2 other events, 1.9 us)
